TPU v7x, 32 devices: a whole 2x2x4 slice. The times are simulated.
32 devices in a mesh: dp: 4 (over x, core), ctx: 8 (over z, y).
Axes of the slice: x: 2, y: 2, z: 4, core: 2. Of those that a mesh axis runs over, the one named last changes fastest.
Arguments:
- queries: bfloat16 [4, 1024, 2048], P('dp', 'ctx'), may hold values from -6 to 6
- keys: bfloat16 [4, 1024, 2048], P('dp', 'ctx'), may hold values from -6 to 6
- values: bfloat16 [4, 1024, 2048], P('dp', 'ctx'), may hold values from -6 to 6
- out_grad: bfloat16 [4, 1024, 2048], P('dp', 'ctx'), may hold values from -6 to 6
- out_proj: bfloat16 [2048, 2048], P('dp'), may hold values from -0.125 to 0.125
- attn_out: bfloat16 [4, 1024, 2048], P('dp', 'ctx'), may hold values from -3 to 3
- log_sum: float32 [4, 16, 1024], P('dp', None, 'ctx'), may hold values from 3 to 5
- group_order: int32 [4, 32], P('dp'), may hold values from 0 to 31, each once within a row
Outputs:
- query_grad: bfloat16 [4, 1024, 2048], P('dp', 'ctx')
- key_grad: bfloat16 [4, 1024, 2048], P('dp', 'ctx')
- value_grad: bfloat16 [4, 1024, 2048], P('dp', 'ctx')
Inputs may be any that keep to these rules, and one draw needn't show every extreme that they name: `group_order`: each row holds every number once.
All inputs are finite; a program needn't handle non-finite values.
Results may differ from a plain program's by a relative error of at most 0.0075.
Values may be sent and summed in bfloat16 or wider, within the bound.
No kernel may reach another device: no remote copies, remote signals or barrier semaphores. Data moves between devices by JAX's collectives and lax.ppermute only.
A program may use at most 64 MiB of HBM per device.

v0:
```python
import jax
import jax.numpy as jnp
from jax import lax
from jax.sharding import PartitionSpec as P

GROUP = 32


def shifted(array, axis, by):
    size = lax.axis_size(axis)
    return lax.ppermute(array, axis, [(i, (i + by) % size) for i in range(size)])


def pair_grads(query_blk, grad_blk, lse_blk, delta_blk, query_pos, key_blk, value_blk, key_pos):
    factor = query_blk.shape[2] ** (-0.5)
    scores = (
        jnp.einsum("qhd,khd->hqk", query_blk, key_blk, preferred_element_type=jnp.float32) * factor
    )
    visible = key_pos[None, None, :] <= query_pos[None, :, None]
    probs = jnp.where(visible, jnp.exp(scores - lse_blk[:, :, None]), 0.0)
    probs_low = probs.astype(jnp.bfloat16)
    value_part = jnp.einsum("hqk,qhd->khd", probs_low, grad_blk, preferred_element_type=jnp.float32)
    dprobs = jnp.einsum("qhd,khd->hqk", grad_blk, value_blk, preferred_element_type=jnp.float32)
    dscores = (probs * (dprobs - delta_blk[:, :, None])).astype(jnp.bfloat16)
    query_part = (
        jnp.einsum("hqk,khd->qhd", dscores, key_blk, preferred_element_type=jnp.float32) * factor
    )
    key_part = (
        jnp.einsum("hqk,qhd->khd", dscores, query_blk, preferred_element_type=jnp.float32) * factor
    )
    rows = query_blk.shape[0]
    width = query_blk.shape[1] * query_blk.shape[2]
    return (
        query_part.reshape(rows, width),
        key_part.reshape(key_blk.shape[0], width),
        value_part.reshape(key_blk.shape[0], width),
    )


def on_device(queries, keys, values, out_grad, out_proj, attn_out, log_sum, group_order):
    tokens = queries.shape[1]
    width = queries.shape[2]
    heads = log_sum.shape[1]
    head_size = width // heads
    upstream = out_grad[0]
    attn_full = jnp.dot(
        upstream,
        lax.all_gather(out_proj, "dp", axis=0, tiled=True),
        preferred_element_type=jnp.float32,
    )
    attn_grad = attn_full.astype(jnp.bfloat16)
    grad_blk = attn_grad.reshape(tokens, heads, head_size)
    out_blk = attn_out[0].reshape(tokens, heads, head_size)
    delta = jnp.sum(grad_blk.astype(jnp.float32) * out_blk.astype(jnp.float32), axis=2).T
    lse_own = log_sum[0]
    order = group_order[0]
    per_block = tokens // GROUP
    cycle_size = lax.axis_size("ctx")
    here = lax.axis_index("ctx")

    def positions(device):
        group_ids = lax.dynamic_slice_in_dim(order, device * per_block, per_block)
        offsets = jnp.arange(GROUP, dtype=jnp.int32)
        return (group_ids[:, None] * GROUP + offsets[None, :]).reshape(tokens)

    own_pos = positions(here)
    query_blk = queries[0].reshape(tokens, heads, head_size)
    key_flat = keys[0]
    value_flat = values[0]
    key_blk = key_flat.reshape(tokens, heads, head_size)
    value_blk = value_flat.reshape(tokens, heads, head_size)
    own = pair_grads(query_blk, grad_blk, lse_own, delta, own_pos, key_blk, value_blk, own_pos)
    query_next, grad_next = shifted((queries[0], attn_grad), "ctx", -1)
    lse_next, delta_next = shifted((lse_own, delta), "ctx", -1)
    next_pos = positions((here + 1) % cycle_size)
    cross = pair_grads(
        query_next.reshape(tokens, heads, head_size),
        grad_next.reshape(tokens, heads, head_size),
        lse_next,
        delta_next,
        next_pos,
        key_blk,
        value_blk,
        own_pos,
    )
    query_back = shifted(cross[0], "ctx", 1)
    query_total = own[0] + query_back
    key_total = own[1] + cross[1]
    value_total = own[2] + cross[2]
    return (
        query_total.astype(jnp.bfloat16).reshape(1, tokens, width),
        key_total.astype(jnp.bfloat16).reshape(1, tokens, width),
        value_total.astype(jnp.bfloat16).reshape(1, tokens, width),
    )


def solution(mesh):
    return jax.shard_map(
        on_device,
        mesh=mesh,
        in_specs=(
            P("dp", "ctx", None),
            P("dp", "ctx", None),
            P("dp", "ctx", None),
            P("dp", "ctx", None),
            P("dp", None),
            P("dp", "ctx", None),
            P("dp", None, "ctx"),
            P("dp", None),
        ),
        out_specs=(P("dp", "ctx", None), P("dp", "ctx", None), P("dp", "ctx", None)),
        check_vma=False,
    )
```

profile of v0, /device:TPU:0, one launch (start us, length us, event | category | flops | bytes accessed | tf_op | source)
XLA Modules:
  0.0 138.3 jit_solution(10649926830788000702)
XLA Ops:
  7.9 6.1 %collective-permute-start.1 = (f32[16,128]{1,0:T(8,128)}, f32[16,128]{1,0:T(8,128)S(1)}, u32[]{:S(2)}, u32[]{:S(2)}) collective-permute-start(f32[16,128]{1,0:T(8,128)} %bitcast.75), channel_id=1, source_target_pairs={{0,7},{1,0},{2,1},{3,2},{4,3},{5,4},{6,5},{7,6},{8,15},{9,8},{10,9... | collective-permute-start | bytes 24584 | tf_op jit(solution)/shard_map/ppermute | solution.py:11
  14.0 2.0 %copy.84 = bf16[1,128,2048]{1,2,0:T(8,128)(2,1)} copy(bf16[1,128,2048]{2,1,0:T(8,128)(2,1)} %param.8) | data formatting | bytes 1048576 | tf_op jit(solution)/shard_map/reshape;squeeze | solution.py:67
  18.9 2.8 %fusion.10 = f32[16,128,128]{2,1,0:T(8,128)} fusion(bf16[128,16,128]{0,2,1:T(8,128)(2,1)} %bitcast.17, f32[16,128]{1,0:T(8,128)} %bitcast.76, pred[128,128]{1,0:T(8,128)(4,1)S(1)} %get-tuple-element.12, bf16[128,16,128]{2,1,0:T(8,128)(2,1)S(1)} %bitcast.65), kind=kOutput, calls=%fused_computation.19 | convolution fusion | flops 67895296 | bytes 2121728 | tf_op jit(solution)/shard_map/qhd,khd->hqk/dot_general | solution.py:17
  23.3 1.4 copy.88
  25.9 3.8 %collective-permute-done = bf16[128,2048]{0,1:T(8,128)(2,1)} collective-permute-done((bf16[128,2048]{0,1:T(8,128)(2,1)}, bf16[128,2048]{0,1:T(8,128)(2,1)}, u32[]{:S(2)}, u32[]{:S(2)}) %collective-permute-start) | collective-permute-done | bytes 524320 | tf_op jit(solution)/shard_map/ppermute | solution.py:11
  29.7 2.6 %fusion.5 = f32[16,128,128]{2,1,0:T(8,128)} fusion(bf16[128,16,128]{0,2,1:T(8,128)(2,1)} %bitcast.8, f32[16,128]{1,0:T(8,128)S(1)} %collective-permute-done.1, pred[128,128]{1,0:T(8,128)(4,1)S(1)} %get-tuple-element.13, bf16[128,16,128]{2,1,0:T(8,128)(2,1)S(1)} %bitcast.67), kind=kOutput, calls=%fused_computation.11 | convolution fusion | flops 67895296 | bytes 2121728 | tf_op jit(solution)/shard_map/qhd,khd->hqk/dot_general | solution.py:17
  32.3 38.3 %all-gather.2.cloned.1.call-done = bf16[2048,2048]{1,0:T(8,128)(2,1)} async-done(((bf16[512,2048]{1,0:T(8,128)(2,1)}), bf16[2048,2048]{1,0:T(8,128)(2,1)}) %all-gather.2.cloned.1.call-update) | async-done | bytes 8388624 | tf_op jit(solution)/shard_map/all_gather | solution.py:48
  70.6 4.6 %convolution_convert_fusion = bf16[128,2048]{1,0:T(8,128)(2,1)S(1)} fusion(bf16[2048,2048]{1,0:T(8,128)(2,1)} %all-gather.2.cloned.1.call-done, bf16[1,128,2048]{2,1,0:T(8,128)(2,1)S(1)} %copy-done), kind=kOutput, calls=%fused_computation | convolution fusion | flops 1074003968 | bytes 9437184 | tf_op jit(solution)/shard_map/dot_general | solution.py:46
  75.2 4.3 %collective-permute-start.2 = (bf16[128,2048]{1,0:T(8,128)(2,1)S(1)}, bf16[128,2048]{1,0:T(8,128)(2,1)}, u32[]{:S(2)}, u32[]{:S(2)}) collective-permute-start(bf16[128,2048]{1,0:T(8,128)(2,1)S(1)} %convolution_convert_fusion), channel_id=1, source_target_pairs={{0,7},{1,0},{2,1},{3,2},{4,3},{5,4},{6,5},{7,6},{8,15},{9,8},{10,9... | collective-permute-start | bytes 1572872 | tf_op jit(solution)/shard_map/ppermute | solution.py:11
  80.1 1.6 %multiply_reduce_fusion = f32[128,16]{1,0:T(8,128)S(1)} fusion(f32[128,16,128]{2,1,0:T(8,128)} %bitcast.62, bf16[128,16,128]{2,1,0:T(8,128)(2,1)S(1)} %bitcast.59), kind=kLoop, calls=%fused_computation.28 | loop fusion | flops 784384 | bytes 1581056 | tf_op jit(solution)/shard_map/reduce_sum | solution.py:54
  82.3 1.8 %fusion.11 = bf16[16,128,128]{2,1,0:T(8,128)(2,1)S(1)} fusion(f32[16,128,128]{2,1,0:T(8,128)} %fusion.10, bf16[128,16,128]{0,2,1:T(8,128)(2,1)S(1)} %copy.74, f32[16,128]{1,0:T(8,128)S(1)} %copy.57, bf16[128,16,128]{2,1,0:T(8,128)(2,1)S(1)} %bitcast.56), kind=kOutput, calls=%fused_computation.20 | convolution fusion | flops 67895296 | bytes 2629632 | tf_op jit(solution)/shard_map/qhd,khd->hqk/dot_general | solution.py:23
  84.1 1.5 %fusion.6 = f32[128,16,128]{2,0,1:T(8,128)} fusion(bf16[16,128,128]{2,1,0:T(8,128)(2,1)S(1)} %fusion.11, bf16[128,16,128]{0,2,1:T(8,128)(2,1)S(1)} %copy.58), kind=kOutput, calls=%fused_computation.13 | convolution fusion | flops 67371008 | bytes 2097152 | tf_op jit(solution)/shard_map/hqk,khd->qhd/dot_general | solution.py:26
  85.6 2.5 %copy.60 = f32[128,16,128]{0,2,1:T(8,128)} copy(f32[128,16,128]{2,0,1:T(8,128)} %fusion.6) | data formatting | bytes 2097152 | tf_op jit(solution)/shard_map/mul | solution.py:26
  88.2 4.4 %collective-permute-done.3 = f32[16,128]{0,1:T(8,128)S(1)} collective-permute-done((f32[16,128]{0,1:T(8,128)S(1)}, f32[16,128]{0,1:T(8,128)S(1)}, u32[]{:S(2)}, u32[]{:S(2)}) %collective-permute-start.3) | collective-permute-done | bytes 8224 | tf_op jit(solution)/shard_map/ppermute | solution.py:11
  92.6 1.3 copy.85
  93.9 1.8 %fusion.12 = bf16[16,128,128]{2,1,0:T(8,128)(2,1)S(1)} fusion(f32[16,128,128]{2,1,0:T(8,128)} %fusion.5, bf16[128,16,128]{0,2,1:T(8,128)(2,1)S(1)} %bitcast.60, f32[16,128]{1,0:T(8,128)S(1)} %copy.66, bf16[128,16,128]{2,1,0:T(8,128)(2,1)S(1)} %bitcast.57), kind=kOutput, calls=%fused_computation.21 | convolution fusion | flops 67895296 | bytes 2629632 | tf_op jit(solution)/shard_map/qhd,khd->hqk/dot_general | solution.py:23
  95.7 2.5 %fusion.1 = f32[128,16,128]{2,0,1:T(8,128)} fusion(bf16[16,128,128]{2,1,0:T(8,128)(2,1)S(1)} %fusion.12, bf16[128,16,128]{0,2,1:T(8,128)(2,1)} %copy-done.1), kind=kOutput, calls=%fused_computation.5 | convolution fusion | flops 67371008 | bytes 2097152 | tf_op jit(solution)/shard_map/hqk,khd->qhd/dot_general | solution.py:26
  98.3 2.6 %copy.69 = f32[128,16,128]{0,2,1:T(8,128)} copy(f32[128,16,128]{2,0,1:T(8,128)} %fusion.1) | data formatting | bytes 2097152 | tf_op jit(solution)/shard_map/mul | solution.py:26
  101.4 2.6 %fusion.25 = f32[16,128,128]{2,1,0:T(8,128)} fusion(bf16[16,128,128]{2,1,0:T(8,128)(2,1)S(1)} %fusion.11, bf16[128,16,128]{0,2,1:T(8,128)(2,1)} %bitcast.17), kind=kOutput, calls=%fused_computation.43 | convolution fusion | flops 67108864 | bytes 2097152 | tf_op jit(solution)/shard_map/hqk,qhd->khd/dot_general | solution.py:29
  104.0 1.5 %fusion.19 = f32[16,128,128]{2,1,0:T(8,128)S(1)} fusion(bf16[128,16,128]{0,2,1:T(8,128)(2,1)S(1)} %copy.74, f32[16,128,128]{2,1,0:T(8,128)} %fusion.10), kind=kOutput, calls=%fused_computation.31 | convolution fusion | flops 67371008 | bytes 2621440 | tf_op jit(solution)/shard_map/hqk,qhd->khd/dot_general | solution.py:22
  105.5 1.6 %fusion.14 = bf16[16,128,128]{2,1,0:T(8,128)(2,1)S(1)} fusion(f32[16,128,128]{2,1,0:T(8,128)S(1)} %fusion.19, bf16[128,16,128]{0,2,1:T(8,128)(2,1)S(1)} %bitcast.61, f32[16,128,128]{2,1,0:T(8,128)} %fusion.5), kind=kOutput, calls=%fused_computation.23 | convolution fusion | flops 67895296 | bytes 3145728 | tf_op jit(solution)/shard_map/hqk,qhd->khd/dot_general | solution.py:22
  108.2 1.9 %fusion.15 = bf16[128,16,128]{2,0,1:T(8,128)(2,1)S(1)} fusion(f32[16,128,128]{2,1,0:T(8,128)} %fusion.25, bf16[16,128,128]{2,1,0:T(8,128)(2,1)S(1)} %fusion.12, bf16[128,16,128]{0,2,1:T(8,128)(2,1)} %bitcast.8), kind=kOutput, calls=%fused_computation.24 | convolution fusion | flops 67895296 | bytes 2621440 | tf_op jit(solution)/shard_map/hqk,qhd->khd/dot_general | solution.py:29
  111.4 17.8 %collective-permute-done.4 = f32[128,2048]{0,1:T(8,128)} collective-permute-done((f32[128,2048]{0,1:T(8,128)}, f32[128,2048]{0,1:T(8,128)}, u32[]{:S(2)}, u32[]{:S(2)}) %collective-permute-start.4) | collective-permute-done | bytes 1048608 | tf_op jit(solution)/shard_map/ppermute | solution.py:11
  129.1 1.3 fusion.16
  (30 shorter events, 11.6 us)
Async XLA Ops:
  7.2 63.4 %copy-start = (bf16[1,128,2048]{2,1,0:T(8,128)(2,1)S(1)}, bf16[1,128,2048]{2,1,0:T(8,128)(2,1)}, u32[]{:S(2)}) copy-start(bf16[1,128,2048]{2,1,0:T(8,128)(2,1)} %param.11) | copy-start | bytes 1572868
  7.2 63.4 %all-gather.2.cloned.1.call-start = ((), (), s32[]{:S(2)}) async-start(), calls=%async_computation | async-start | bytes 10485760 | tf_op jit(solution)/shard_map/all_gather | solution.py:48
  7.9 18.0 %collective-permute-start.1 = (f32[16,128]{1,0:T(8,128)}, f32[16,128]{1,0:T(8,128)S(1)}, u32[]{:S(2)}, u32[]{:S(2)}) collective-permute-start(f32[16,128]{1,0:T(8,128)} %bitcast.75), channel_id=1, source_target_pairs={{0,7},{1,0},{2,1},{3,2},{4,3},{5,4},{6,5},{7,6},{8,15},{9,8},{10,9... | collective-permute-start | bytes 24584 | tf_op jit(solution)/shard_map/ppermute | solution.py:11
  16.0 13.7 %collective-permute-start = (bf16[128,2048]{0,1:T(8,128)(2,1)}, bf16[128,2048]{0,1:T(8,128)(2,1)}, u32[]{:S(2)}, u32[]{:S(2)}) collective-permute-start(bf16[128,2048]{0,1:T(8,128)(2,1)} %bitcast.7), channel_id=1, source_target_pairs={{0,7},{1,0},{2,1},{3,2},{4,3},{5,4},{6,5},{7,6},{8,15},{9,8},{10,9... | collective-permute-start | bytes 1572872 | tf_op jit(solution)/shard_map/ppermute | solution.py:11
  23.3 60.8 %copy-start.1 = (bf16[128,16,128]{0,2,1:T(8,128)(2,1)}, bf16[128,16,128]{0,2,1:T(8,128)(2,1)S(1)}, u32[]{:S(2)}) copy-start(bf16[128,16,128]{0,2,1:T(8,128)(2,1)S(1)} %copy.58) | copy-start | bytes 1572868
  75.2 17.4 %collective-permute-start.2 = (bf16[128,2048]{1,0:T(8,128)(2,1)S(1)}, bf16[128,2048]{1,0:T(8,128)(2,1)}, u32[]{:S(2)}, u32[]{:S(2)}) collective-permute-start(bf16[128,2048]{1,0:T(8,128)(2,1)S(1)} %convolution_convert_fusion), channel_id=1, source_target_pairs={{0,7},{1,0},{2,1},{3,2},{4,3},{5,4},{6,5},{7,6},{8,15},{9,8},{10,9... | collective-permute-start | bytes 1572872 | tf_op jit(solution)/shard_map/ppermute | solution.py:11
  81.8 10.8 %collective-permute-start.3 = (f32[16,128]{0,1:T(8,128)S(1)}, f32[16,128]{0,1:T(8,128)S(1)}, u32[]{:S(2)}, u32[]{:S(2)}) collective-permute-start(f32[16,128]{0,1:T(8,128)S(1)} %bitcast.74), channel_id=1, source_target_pairs={{0,7},{1,0},{2,1},{3,2},{4,3},{5,4},{6,5},{7,6},{8,15},{9,8},{10,9... | collective-permute-start | bytes 24584 | tf_op jit(solution)/shard_map/ppermute | solution.py:11
  100.8 28.3 %collective-permute-start.4 = (f32[128,2048]{0,1:T(8,128)}, f32[128,2048]{0,1:T(8,128)}, u32[]{:S(2)}, u32[]{:S(2)}) collective-permute-start(f32[128,2048]{0,1:T(8,128)} %bitcast.70), channel_id=1, source_target_pairs={{0,1},{1,2},{2,3},{3,4},{4,5},{5,6},{6,7},{7,0},{8,9},{9,10},{10,1... | collective-permute-start | bytes 3145736 | tf_op jit(solution)/shard_map/ppermute | solution.py:11
  105.5 23.6 %copy-start.2 = (f32[128,16,128]{0,2,1:T(8,128)S(1)}, f32[128,16,128]{0,2,1:T(8,128)}, u32[]{:S(2)}) copy-start(f32[128,16,128]{0,2,1:T(8,128)} %copy.60) | copy-start | bytes 3145732
Sparse Core Ops, SparseCore 0:
  9.6 60.9 all-gather.1
where the time goes:
time: 139 us; the launch traced here: 138 us
  waiting for transfers between devices  64.9 us (47%)
  matrix products  25.2 us (18%)
  local copies, waits for them, and re-layouts  16.9 us (12%)
  between operations  14.2 us (10%)
  starting transfers between devices  12.1 us (9%)
  other arithmetic  5.06 us (4%)
    all_gather x1, waiting for transfers between devices, on_device(): lax.all_gather(out_proj, 'dp', axis=0, tiled=True)  38.3 us
    ppermute x5, waiting for transfers between devices, shifted(): lax.ppermute(array, axis, [(i, (i + by) % size) for i in range(size)])  26 us
    ppermute x5, starting transfers between devices, shifted(): lax.ppermute(array, axis, [(i, (i + by) % size) for i in range(size)])  12.1 us
    unnamed x13, local copies, waits for them, and re-layouts  6.91 us
    dot_general x2, matrix products, pair_grads(): jnp.einsum('qhd,khd->hqk', query_blk, key_blk, preferred_element_type=jnp...  5.34 us
    mul x2, local copies, waits for them, and re-layouts, pair_grads(): jnp.einsum('hqk,khd->qhd', dscores, key_blk, preferred_element_type=jnp.f...  5.09 us
    dot_general x1, matrix products, on_device(): jnp.dot(upstream, lax.all_gather(out_proj, 'dp', axis=0, tiled=True), pre...  4.64 us
    dot_general x2, matrix products, pair_grads(): jnp.einsum('hqk,qhd->khd', dscores, query_blk, preferred_element_type=jnp...  4.46 us
  transfers between devices with their start and end apart: 6, of which 4 were waited for; matrix products, arithmetic and copies ran while one was open for 23% of the time, Pallas kernels for 0%

commit v1 on v0

v1 whole, which is shorter than its diff:
```python
import functools

import jax
import jax.numpy as jnp
from jax import lax
from jax.experimental import pallas as pl
from jax.experimental.pallas import tpu as pltpu
from jax.sharding import PartitionSpec as P

GROUP = 32
CHUNKS = 2
LANES = 512
EXTRA = 16
F32 = jnp.float32
BF16 = jnp.bfloat16


def dot(a, b, ca, cb):
    return lax.dot_general(a, b, (((ca,), (cb,)), ((), ())), preferred_element_type=F32)


def vmem(shape=None, index=None):
    if shape is None:
        return pl.BlockSpec(memory_space=pltpu.VMEM)
    return pl.BlockSpec(shape, index)


def params():
    return pltpu.CompilerParams(vmem_limit_bytes=24 * 1024 * 1024)


def cost(flops, nbytes, exps=0):
    return pl.CostEstimate(flops=int(flops), bytes_accessed=int(nbytes), transcendentals=int(exps))


def project_kernel(chips, pair, *refs):
    lhs, weights = refs[:chips], refs[chips : chips + pair]
    local, remote = refs[chips + pair], refs[chips + pair + 1 :]
    rows = weights[0].shape[0]
    tokens = lhs[0].shape[0]
    stacked = jnp.concatenate([ref[...] for ref in lhs], axis=0)
    total = dot(stacked[:, :rows], weights[0][...], 1, 0)
    for i in range(1, pair):
        total += dot(stacked[:, i * rows : (i + 1) * rows], weights[i][...], 1, 0)
    local[...] = total[:tokens]
    for j, ref in enumerate(remote):
        ref[...] = total[(j + 1) * tokens : (j + 2) * tokens].astype(BF16)


def project(lhs, weights, first, width):
    chips, pair = len(lhs), len(weights)
    tokens, depth = lhs[0].shape
    rows = weights[0].shape[0]
    tile = min(LANES, width)
    base = first // tile
    return pl.pallas_call(
        functools.partial(project_kernel, chips, pair),
        grid=(width // tile,),
        in_specs=[vmem((tokens, depth), lambda i: (0, 0))] * chips
        + [vmem((rows, tile), lambda i: (0, base + i))] * pair,
        out_specs=[vmem((tokens, tile), lambda i: (0, i))] * chips,
        out_shape=[jax.ShapeDtypeStruct((tokens, width), F32)]
        + [jax.ShapeDtypeStruct((tokens, width), BF16)] * (chips - 1),
        compiler_params=params(),
        cost_estimate=cost(2 * chips * tokens * depth * width, 2 * depth * width),
        name="project",
    )(*lhs, *weights)


def grad_kernel(heads, local, *refs):
    parts, out_ref, msg = refs[:-2], refs[-2], refs[-1]
    tokens = local.shape[0]
    size = local.shape[1] // heads
    total = local[...]
    for ref in parts:
        total += ref[...].astype(F32)
    grad = total.astype(BF16)
    msg[:tokens, :] = grad
    product = grad.astype(F32) * out_ref[...].astype(F32)
    high = product.astype(BF16)
    low = (product - high.astype(F32)).astype(BF16)
    ones = jnp.ones((8, size), BF16)
    rows = []
    for h in range(heads):
        cols = slice(h * size, (h + 1) * size)
        rows.append(dot(ones, high[:, cols], 1, 1) + dot(ones, low[:, cols], 1, 1))
    delta = jnp.concatenate(rows, axis=1)
    top = delta.astype(BF16).astype(F32)
    pick = lax.broadcasted_iota(jnp.int32, delta.shape, 0)
    both = jnp.where(pick == 0, top, delta - top)
    msg[tokens:, :] = jnp.concatenate([both, both], axis=0).astype(BF16)


def combine(local, parts, attn_out, first, heads):
    tokens, width = local.shape
    return pl.pallas_call(
        functools.partial(grad_kernel, heads),
        grid=(1,),
        in_specs=[vmem((tokens, width), lambda i: (0, 0))] * (1 + len(parts))
        + [vmem((tokens, width), lambda i: (0, first // width))],
        out_specs=vmem((tokens + EXTRA, width), lambda i: (0, 0)),
        out_shape=jax.ShapeDtypeStruct((tokens + EXTRA, width), BF16),
        compiler_params=params(),
        cost_estimate=cost(tokens * width * 64, tokens * width * 10),
        name="combine",
    )(local, *parts, attn_out)


def delta_row(msg, tokens, cols):
    tail = msg[tokens:, cols].astype(F32)
    return tail[0:1] + tail[1:2]


def own_kernel(heads, head0, query, key, value, msg, lse, bias, dq, dk, dv):
    tokens = query.shape[0]
    size = query.shape[1] // heads
    factor = size ** -0.5
    mask = bias[...]
    for h in range(heads):
        cols = slice(h * size, (h + 1) * size)
        q, k, v, g = query[:, cols], key[:, cols], value[:, cols], msg[:tokens, cols]
        scores = dot(k, q, 1, 1) * factor
        probs = jnp.exp(scores - lse[head0 + h : head0 + h + 1, :] + mask)
        dv[:, cols] = dot(probs.astype(BF16), g, 1, 0)
        dprobs = dot(v, g, 1, 1)
        dscores = (probs * (dprobs - delta_row(msg, tokens, cols))).astype(BF16)
        dk[:, cols] = dot(dscores, q, 1, 0)
        dq[:, cols] = dot(dscores, k, 0, 0) * factor


def own_pair(query, key, value, msg, lse, bias, first, heads):
    tokens = query.shape[0]
    width = msg.shape[1]
    head0 = first // (width // heads)
    part = vmem((tokens, width), lambda i: (0, first // width))
    whole = vmem((tokens, width), lambda i: (0, 0))
    return pl.pallas_call(
        functools.partial(own_kernel, heads, head0),
        grid=(1,),
        in_specs=[part, part, part, vmem(msg.shape, lambda i: (0, 0)), vmem(lse.shape, lambda i: (0, 0)), vmem(bias.shape, lambda i: (0, 0))],
        out_specs=[whole] * 3,
        out_shape=[jax.ShapeDtypeStruct((tokens, width), F32)] * 3,
        compiler_params=params(),
        cost_estimate=cost(10 * tokens * tokens * width, tokens * width * 20, heads * tokens * tokens),
        name="own_pair",
    )(query, key, value, msg, lse, bias)


def cross_kernel(heads, head0, query, key, value, msg, lse, bias, dq, probs_out, dscores_out):
    tokens = query.shape[0]
    size = query.shape[1] // heads
    factor = size ** -0.5
    mask = bias[...]
    for h in range(heads):
        cols = slice(h * size, (h + 1) * size)
        q, k, v, g = query[:, cols], key[:, cols], value[:, cols], msg[:tokens, cols]
        scores = dot(k, q, 1, 1) * factor
        probs = jnp.exp(scores - lse[head0 + h : head0 + h + 1, :] + mask)
        probs_out[:, cols] = probs.astype(BF16)
        dprobs = dot(v, g, 1, 1)
        dscores = (probs * (dprobs - delta_row(msg, tokens, cols))).astype(BF16)
        dscores_out[:, cols] = dscores
        dq[:, cols] = (dot(dscores, k, 0, 0) * factor).astype(BF16)


def cross_pair(query, key, value, msg, lse, bias, first, heads):
    tokens = query.shape[0]
    width = msg.shape[1]
    head0 = first // (width // heads)
    part = vmem((tokens, width), lambda i: (0, first // width))
    whole = vmem((tokens, width), lambda i: (0, 0))
    return pl.pallas_call(
        functools.partial(cross_kernel, heads, head0),
        grid=(1,),
        in_specs=[part, part, part, vmem(msg.shape, lambda i: (0, 0)), vmem(lse.shape, lambda i: (0, 0)), vmem(bias.shape, lambda i: (0, 0))],
        out_specs=[whole] * 3,
        out_shape=[jax.ShapeDtypeStruct((tokens, width), BF16)] * 3,
        compiler_params=params(),
        cost_estimate=cost(6 * tokens * tokens * width, tokens * width * 14, heads * tokens * tokens),
        name="cross_pair",
    )(query, key, value, msg, lse, bias)


def key_kernel(chunks, heads, query, *refs):
    ins, (dk_out, dv_out) = refs[:-2], refs[-2:]
    tokens = query.shape[0]
    size = query.shape[1] // (heads * chunks)
    factor = size ** -0.5
    for c in range(chunks):
        msg, probs, dscores, dk, dv = ins[c * 5 : c * 5 + 5]
        for h in range(heads):
            cols = slice(h * size, (h + 1) * size)
            place = slice((c * heads + h) * size, (c * heads + h + 1) * size)
            dk_out[:, place] = ((dk[:, cols] + dot(dscores[:, cols], query[:, place], 1, 0)) * factor).astype(BF16)
            dv_out[:, place] = (dv[:, cols] + dot(probs[:, cols], msg[:tokens, cols], 1, 0)).astype(BF16)


def key_grads(query, groups, heads):
    tokens, width = query.shape
    return pl.pallas_call(
        functools.partial(key_kernel, len(groups), heads),
        in_specs=[vmem()] * (1 + 5 * len(groups)),
        out_specs=[vmem()] * 2,
        out_shape=[jax.ShapeDtypeStruct((tokens, width), BF16)] * 2,
        compiler_params=params(),
        cost_estimate=cost(4 * tokens * tokens * width, tokens * width * 20),
        name="key_grads",
    )(query, *[a for group in groups for a in group])


def add_kernel(chunks, *refs):
    out = refs[-1]
    width = out.shape[1] // chunks
    for c in range(chunks):
        out[:, c * width : (c + 1) * width] = (refs[2 * c][...] + refs[2 * c + 1][...].astype(F32)).astype(BF16)


def add_all(pairs):
    tokens, width = pairs[0][0].shape
    return pl.pallas_call(
        functools.partial(add_kernel, len(pairs)),
        in_specs=[vmem()] * (2 * len(pairs)),
        out_specs=vmem(),
        out_shape=jax.ShapeDtypeStruct((tokens, width * len(pairs)), BF16),
        compiler_params=params(),
        cost_estimate=cost(2 * tokens * width * len(pairs), 8 * tokens * width * len(pairs)),
        name="query_sum",
    )(*[a for pair in pairs for a in pair])


def on_device(queries, keys, values, out_grad, out_proj, attn_out, log_sum, group_order):
    tokens, width = queries.shape[1:]
    heads = log_sum.shape[1]
    rows = out_proj.shape[0]
    query, key, value, upstream, output = queries[0], keys[0], values[0], out_grad[0], attn_out[0]
    lse = log_sum[0]
    order = group_order[0]
    dp, ctx = lax.axis_size("dp"), lax.axis_size("ctx")
    me, here = lax.axis_index("dp"), lax.axis_index("ctx")
    pair = 2 if dp % 2 == 0 else 1
    chips = dp // pair
    core, chip = me % pair, me // pair

    def along_dp(array, by):
        return lax.ppermute(array, "dp", [(i, (i + by) % dp) for i in range(dp)])

    def along_ctx(array, by):
        return lax.ppermute(array, "ctx", [(i, (i + by) % ctx) for i in range(ctx)])

    def columns_for(there):
        parts = [
            lax.dynamic_slice_in_dim(upstream, (there * pair + (core + i) % pair) * rows, rows, axis=1)
            for i in range(pair)
        ]
        return jnp.concatenate(parts, axis=1)

    arrived = [along_dp(columns_for((chip + j) % chips), pair * j) for j in range(1, chips)]
    weights = [out_proj]
    if pair == 2:
        weights.append(lax.ppermute(out_proj, "dp", [(i, i ^ 1) for i in range(dp)]))
    query_next = along_ctx(query, -1)
    lse_next = along_ctx(lse, -1)
    lhs = [columns_for(chip)] + arrived

    per_block = tokens // GROUP

    def positions(device):
        ids = lax.dynamic_slice_in_dim(order, device * per_block, per_block)
        return (ids[:, None] * GROUP + jnp.arange(GROUP, dtype=jnp.int32)[None, :]).reshape(tokens)

    own_pos = positions(here)
    next_pos = positions((here + 1) % ctx)
    bias_own = jnp.where(own_pos[:, None] <= own_pos[None, :], 0.0, -jnp.inf).astype(F32)
    bias_next = jnp.where(own_pos[:, None] <= next_pos[None, :], 0.0, -jnp.inf).astype(F32)

    chunks = CHUNKS if heads % CHUNKS == 0 else 1
    part = width // chunks
    per = heads // chunks
    groups, sums = [], []
    for c in range(chunks):
        first = c * part
        local, *remote = project(lhs, weights, first, part)
        back = [along_dp(remote[j - 1], -pair * j) for j in range(1, chips)]
        msg = combine(local, back, output, first, per)
        msg_next = along_ctx(msg, -1)
        dq_own, dk_own, dv_own = own_pair(query, key, value, msg, lse, bias_own, first, per)
        dq_cross, probs, dscores = cross_pair(query_next, key, value, msg_next, lse_next, bias_next, first, per)
        groups.append((msg_next, probs, dscores, dk_own, dv_own))
        sums.append((dq_own, along_ctx(dq_cross, 1)))
    key_grad, value_grad = key_grads(query_next, groups, per)
    query_grad = add_all(sums)
    shape = (1, tokens, width)
    return query_grad.reshape(shape), key_grad.reshape(shape), value_grad.reshape(shape)


def solution(mesh):
    return jax.shard_map(
        on_device,
        mesh=mesh,
        in_specs=(
            P("dp", "ctx", None),
            P("dp", "ctx", None),
            P("dp", "ctx", None),
            P("dp", "ctx", None),
            P("dp", None),
            P("dp", "ctx", None),
            P("dp", None, "ctx"),
            P("dp", None),
        ),
        out_specs=(P("dp", "ctx", None), P("dp", "ctx", None), P("dp", "ctx", None)),
        check_vma=False,
    )
```

time: 139 us -> 62.9 us (0.45)
  waiting for transfers between devices: 64.9 us -> 19.8 us
  matrix products: 25.2 us -> 0 us
  Pallas kernels: 0 us -> 19.2 us
  between operations: 14.2 us -> 0.73 us
  local copies, waits for them, and re-layouts: 16.9 us -> 6.75 us
  other arithmetic: 5.06 us -> 0.27 us
  starting transfers between devices: 12.1 us -> 15.8 us
    all_gather x1 -> x0, waiting for transfers between devices: 38.3 us -> none  [on_device(): lax.all_gather(out_proj, 'dp', axis=0, tiled=True)]
    dot_general x11 -> x0, matrix products: 25.2 us -> none  [the longest x2 5.34 us: pair_grads(): jnp.einsum('qhd,khd->hqk', query_blk, key_blk, preferred_element_type=jnp...]
    pallas_call x0 -> x10, Pallas kernels: none -> 19.2 us  [the longest x2 5.31 us: project(): pl.pallas_call(functools.partial(project_kernel, chips, pair), grid=(widt...]
    ppermute x5 -> x10, waiting for transfers between devices: 26 us -> 19.8 us  [the longest x6 13 us: along_ctx(): return lax.ppermute(array, 'ctx', [(i, (i + by) % ctx) for i in range(ctx)])]
    mul x2 -> x0, local copies, waits for them, and re-layouts: 5.09 us -> none  [pair_grads(): jnp.einsum('hqk,khd->qhd', dscores, key_blk, preferred_element_type=jnp.f...]
    ppermute x5 -> x10, starting transfers between devices: 12.1 us -> 15.8 us  [the longest x6 10.5 us: along_ctx(): return lax.ppermute(array, 'ctx', [(i, (i + by) % ctx) for i in range(ctx)])]
    another operation x2 -> x0, local copies, waits for them, and re-layouts: 2.51 us -> none  [the longest x1 2.04 us: on_device(): query_blk = queries[0].reshape(tokens, heads, head_size)]
    reshape x2 -> x0, local copies, waits for them, and re-layouts: 1.8 us -> none  [the longest x1 1.33 us: on_device(): grad_next.reshape(tokens, heads, head_size)]
  transfers between devices with their start and end apart: 6 -> 10, of which waited for: 4 -> 5; matrix products, arithmetic and copies ran while one was open for 23% -> 3% of each run, Pallas kernels for 0% -> 25%
where the time goes in v1:
time: 62.9 us; the launch traced here: 62.5 us
  waiting for transfers between devices  19.8 us (31%)
  Pallas kernels  19.2 us (31%)
  starting transfers between devices  15.8 us (25%)
  local copies, waits for them, and re-layouts  6.75 us (11%)
  between operations  0.73 us (1%)
    ppermute x6, waiting for transfers between devices, along_ctx(): return lax.ppermute(array, 'ctx', [(i, (i + by) % ctx) for i in range(ctx)])  13 us
    ppermute x6, starting transfers between devices, along_ctx(): return lax.ppermute(array, 'ctx', [(i, (i + by) % ctx) for i in range(ctx)])  10.5 us
    ppermute x3, waiting for transfers between devices, along_dp(): return lax.ppermute(array, 'dp', [(i, (i + by) % dp) for i in range(dp)])  6.74 us
    unnamed x26, local copies, waits for them, and re-layouts  5.35 us
    pallas_call x2, Pallas kernels, project(): pl.pallas_call(functools.partial(project_kernel, chips, pair), grid=(widt...  5.31 us
    pallas_call x2, Pallas kernels, own_pair(): pl.pallas_call(functools.partial(own_kernel, heads, head0), grid=(1,), in...  5.25 us
    ppermute x3, starting transfers between devices, along_dp(): return lax.ppermute(array, 'dp', [(i, (i + by) % dp) for i in range(dp)])  4.76 us
    pallas_call x2, Pallas kernels, cross_pair(): pl.pallas_call(functools.partial(cross_kernel, heads, head0), grid=(1,),...  3.74 us
  transfers between devices with their start and end apart: 10, of which 5 were waited for; matrix products, arithmetic and copies ran while one was open for 3% of the time, Pallas kernels for 25%

profile of v1, /device:TPU:0, one launch (start us, length us, event | category | flops | bytes accessed | tf_op | source)
XLA Modules:
  0.0 62.5 jit_solution(3721558632320621346)
XLA Ops:
  1.2 1.2 %dynamic-slice_bitcast_fusion.1 = (bf16[128,512]{1,0:T(8,128)(2,1)S(1)}, bf16[128,512]{1,0:T(8,128)(2,1)S(1)}, bf16[128,512]{1,0:T(8,128)(2,1)S(1)}, bf16[128,512]{1,0:T(8,128)(2,1)S(1)}) fusion(bf16[1,128,2048]{2,1,0:T(8,128)(2,1)} %param.11, s32[]{:T(128)S(6)} %select_n.63, s32[]{:T(128)S(6)} %select_n.61, s32[]{:T(128)S(6)} %select_n.59, s32[]{:T(128)S(6)} %select_n.64), kind=kLoop, calls=%fused_computation.3 | loop fusion | bytes 1048592 | tf_op jit(solution)/shard_map/dynamic_slice | solution.py:252
  2.4 2.7 %collective-permute-start = (bf16[128,1024]{1,0:T(8,128)(2,1)S(1)}, bf16[128,1024]{1,0:T(8,128)(2,1)S(1)}, u32[]{:S(2)}, u32[]{:S(2)}) collective-permute-start(bf16[128,1024]{1,0:T(8,128)(2,1)S(1)} %pad_maximum_fusion.1), channel_id=1, source_target_pairs={{0,16},{8,24},{16,0},{24,8},{1,17},{9,25},{17,1},{25,9},{2,18},{10... | collective-permute-start | bytes 786440 | tf_op jit(solution)/shard_map/ppermute | solution.py:245
  5.1 6.7 %collective-permute-done.refs_1_ = bf16[128,1024]{1,0:T(8,128)(2,1)S(1)} collective-permute-done((bf16[128,1024]{1,0:T(8,128)(2,1)S(1)}, bf16[128,1024]{1,0:T(8,128)(2,1)S(1)}, u32[]{:S(2)}, u32[]{:S(2)}) %collective-permute-start) | collective-permute-done | bytes 262176 | tf_op jit(solution)/shard_map/ppermute | solution.py:245
  11.9 2.6 %project.2 = (f32[128,1024]{1,0:T(8,128)S(1)}, bf16[128,1024]{1,0:T(8,128)(2,1)}) custom-call(bf16[128,1024]{1,0:T(8,128)(2,1)S(1)} %pad_maximum_fusion.refs_0_, bf16[128,1024]{1,0:T(8,128)(2,1)S(1)} %collective-permute-done.refs_1_, bf16[512,2048]{1,0:T(8,128)(2,1)S(1)} %copy-done, bf16[512,2048]{1,0:T(8,128)(2,1)} %collective-permute-done.1.refs_3_), custom_call_target="tpu_custom_call" | custom-call | flops 536870912 | bytes 2097152 | tf_op jit(solution)/shard_map/project/pallas_call | solution.py:56
  14.5 0.8 %copy-done.7 = f32[128,1024]{1,0:T(8,128)} copy-done((f32[128,1024]{1,0:T(8,128)}, f32[128,1024]{1,0:T(8,128)S(1)}, u32[]{:S(2)}) %copy-start.7) | copy-done | bytes 524312
  15.3 1.8 %collective-permute-start.2 = (bf16[128,1024]{1,0:T(8,128)(2,1)}, bf16[128,1024]{1,0:T(8,128)(2,1)S(1)}, u32[]{:S(2)}, u32[]{:S(2)}) collective-permute-start(bf16[128,1024]{1,0:T(8,128)(2,1)} %get-tuple-element.22), channel_id=1, source_target_pairs={{0,16},{8,24},{16,0},{24,8},{1,17},{9,25},{17,1},{25,9},{2,18},{10... | collective-permute-start | bytes 786440 | tf_op jit(solution)/shard_map/ppermute | solution.py:245
  17.1 2.7 %project.3 = (f32[128,1024]{1,0:T(8,128)S(1)}, bf16[128,1024]{1,0:T(8,128)(2,1)}) custom-call(bf16[128,1024]{1,0:T(8,128)(2,1)S(1)} %pad_maximum_fusion.refs_0_, bf16[128,1024]{1,0:T(8,128)(2,1)S(1)} %collective-permute-done.refs_1_, bf16[512,2048]{1,0:T(8,128)(2,1)S(1)} %copy-done, bf16[512,2048]{1,0:T(8,128)(2,1)} %collective-permute-done.1.refs_3_), custom_call_target="tpu_custom_call" | custom-call | flops 536870912 | bytes 2097152 | tf_op jit(solution)/shard_map/project/pallas_call | solution.py:56
  20.9 4.8 %collective-permute-start.3 = (bf16[128,2048]{1,0:T(8,128)(2,1)S(1)}, bf16[128,2048]{1,0:T(8,128)(2,1)S(1)}, u32[]{:S(2)}, u32[]{:S(2)}) collective-permute-start(bf16[128,2048]{1,0:T(8,128)(2,1)S(1)} %bitcast.30), channel_id=1, source_target_pairs={{0,7},{1,0},{2,1},{3,2},{4,3},{5,4},{6,5},{7,6},{8,15},{9,8},{10,9... | collective-permute-start | bytes 1572872 | tf_op jit(solution)/shard_map/ppermute | solution.py:248
  27.0 1.0 %copy-done.8 = f32[128,1024]{1,0:T(8,128)S(1)} copy-done((f32[128,1024]{1,0:T(8,128)S(1)}, f32[128,1024]{1,0:T(8,128)}, u32[]{:S(2)}) %copy-start.8) | copy-done | bytes 524312
  28.0 0.9 %copy-done.10 = bf16[128,1024]{1,0:T(8,128)(2,1)S(1)} copy-done((bf16[128,1024]{1,0:T(8,128)(2,1)S(1)}, bf16[128,1024]{1,0:T(8,128)(2,1)}, u32[]{:S(2)}) %copy-start.10) | copy-done | bytes 262168
  29.4 2.7 %collective-permute-start.4 = (bf16[144,1024]{1,0:T(8,128)(2,1)S(1)}, bf16[144,1024]{1,0:T(8,128)(2,1)S(1)}, u32[]{:S(2)}, u32[]{:S(2)}) collective-permute-start(bf16[144,1024]{1,0:T(8,128)(2,1)S(1)} %combine.2.msg), channel_id=1, source_target_pairs={{0,7},{1,0},{2,1},{3,2},{4,3},{5,4},{6,5},{7,6},{8,15},{9,8},{10,9... | collective-permute-start | bytes 884744 | tf_op jit(solution)/shard_map/ppermute | solution.py:248
  32.1 1.0 %copy-done.6 = f32[128,1024]{1,0:T(8,128)S(1)} copy-done((f32[128,1024]{1,0:T(8,128)S(1)}, f32[128,1024]{1,0:T(8,128)}, u32[]{:S(2)}) %copy-start.6) | copy-done | bytes 524312
  33.1 2.1 %combine.3.msg = bf16[144,1024]{1,0:T(8,128)(2,1)} custom-call(f32[128,1024]{1,0:T(8,128)S(1)} %copy-done.6, bf16[128,1024]{1,0:T(8,128)(2,1)} %collective-permute-done.7.refs_0_, bf16[128,2048]{1,0:T(8,128)(2,1)S(1)} %bitcast.29), custom_call_target="tpu_custom_call" | custom-call | flops 8388608 | bytes 1310720 | tf_op jit(solution)/shard_map/combine/pallas_call | solution.py:96
  35.2 1.7 %collective-permute-start.8 = (bf16[144,1024]{1,0:T(8,128)(2,1)}, bf16[144,1024]{1,0:T(8,128)(2,1)S(1)}, u32[]{:S(2)}, u32[]{:S(2)}) collective-permute-start(bf16[144,1024]{1,0:T(8,128)(2,1)} %combine.3.msg), channel_id=1, source_target_pairs={{0,7},{1,0},{2,1},{3,2},{4,3},{5,4},{6,5},{7,6},{8,15},{9,8},{10,9... | collective-permute-start | bytes 884744 | tf_op jit(solution)/shard_map/ppermute | solution.py:248
  37.3 1.0 %collective-permute-done.5.lse = f32[16,128]{1,0:T(8,128)S(1)} collective-permute-done((f32[16,128]{1,0:T(8,128)S(1)}, f32[16,128]{1,0:T(8,128)S(1)}, u32[]{:S(2)}, u32[]{:S(2)}) %collective-permute-start.5) | collective-permute-done | bytes 8224 | tf_op jit(solution)/shard_map/ppermute | solution.py:248
  38.2 6.3 %collective-permute-done.4.msg.refs_0_ = bf16[144,1024]{1,0:T(8,128)(2,1)S(1)} collective-permute-done((bf16[144,1024]{1,0:T(8,128)(2,1)S(1)}, bf16[144,1024]{1,0:T(8,128)(2,1)S(1)}, u32[]{:S(2)}, u32[]{:S(2)}) %collective-permute-start.4) | collective-permute-done | bytes 294944 | tf_op jit(solution)/shard_map/ppermute | solution.py:248
  44.6 1.9 %cross_pair.2 = (bf16[128,1024]{1,0:T(8,128)(2,1)S(1)}, bf16[128,1024]{1,0:T(8,128)(2,1)S(1)}, bf16[128,1024]{1,0:T(8,128)(2,1)S(1)}) custom-call(bf16[128,2048]{1,0:T(8,128)(2,1)S(1)} %collective-permute-done.3.query, bf16[128,2048]{1,0:T(8,128)(2,1)S(1)} %bitcast.20, bf16[128,2048]{1,0:T(8,128)(2,1)S(1)} %bitcast.24, ...), custom_call_target="tpu_custom_call" | custom-call | flops 100663296 | bytes 1835008 | tf_op jit(solution)/shard_map/cross_pair/pallas_call | solution.py:172
  46.8 2.0 %collective-permute-done.8.msg.refs_5_ = bf16[144,1024]{1,0:T(8,128)(2,1)S(1)} collective-permute-done((bf16[144,1024]{1,0:T(8,128)(2,1)}, bf16[144,1024]{1,0:T(8,128)(2,1)S(1)}, u32[]{:S(2)}, u32[]{:S(2)}) %collective-permute-start.8) | collective-permute-done | bytes 294944 | tf_op jit(solution)/shard_map/ppermute | solution.py:248
  48.9 1.9 %cross_pair.3 = (bf16[128,1024]{1,0:T(8,128)(2,1)S(1)}, bf16[128,1024]{1,0:T(8,128)(2,1)S(1)}, bf16[128,1024]{1,0:T(8,128)(2,1)S(1)}) custom-call(bf16[128,2048]{1,0:T(8,128)(2,1)S(1)} %collective-permute-done.3.query, bf16[128,2048]{1,0:T(8,128)(2,1)S(1)} %bitcast.21, bf16[128,2048]{1,0:T(8,128)(2,1)S(1)} %bitcast.25, ...), custom_call_target="tpu_custom_call" | custom-call | flops 100663296 | bytes 1835008 | tf_op jit(solution)/shard_map/cross_pair/pallas_call | solution.py:172
  51.1 2.1 %own_pair.2 = (f32[128,1024]{1,0:T(8,128)S(1)}, f32[128,1024]{1,0:T(8,128)S(1)}, f32[128,1024]{1,0:T(8,128)S(1)}) custom-call(bf16[128,2048]{1,0:T(8,128)(2,1)S(1)} %bitcast.31, bf16[128,2048]{1,0:T(8,128)(2,1)S(1)} %bitcast.22, bf16[128,2048]{1,0:T(8,128)(2,1)S(1)} %bitcast.26, bf16[144,1024]{1,0:T(8,128)(2,1)S(1)} %combine.2.msg, f32[16,128]{1,0:T(8,128)S(1)} %bitcast.34, ...), custom_call_target="tpu_custom_call" | custom-call | flops 167772160 | bytes 2621440 | tf_op jit(solution)/shard_map/own_pair/pallas_call | solution.py:137
  53.3 3.1 %own_pair.3 = (f32[128,1024]{1,0:T(8,128)S(1)}, f32[128,1024]{1,0:T(8,128)S(1)}, f32[128,1024]{1,0:T(8,128)S(1)}) custom-call(bf16[128,2048]{1,0:T(8,128)(2,1)S(1)} %bitcast.32, bf16[128,2048]{1,0:T(8,128)(2,1)S(1)} %bitcast.23, bf16[128,2048]{1,0:T(8,128)(2,1)S(1)} %bitcast.27, bf16[144,1024]{1,0:T(8,128)(2,1)} %combine.3.msg, f32[16,128]{1,0:T(8,128)S(1)} %bitcast.35, ...), custom_call_target="tpu_custom_call" | custom-call | flops 167772160 | bytes 2621440 | tf_op jit(solution)/shard_map/own_pair/pallas_call | solution.py:137
  56.4 1.5 %key_grads.1 = (bf16[128,2048]{1,0:T(8,128)(2,1)}, bf16[128,2048]{1,0:T(8,128)(2,1)}) custom-call(bf16[128,2048]{1,0:T(8,128)(2,1)S(1)} %collective-permute-done.3.query, bf16[144,1024]{1,0:T(8,128)(2,1)S(1)} %collective-permute-done.4.msg.refs_0_, bf16[128,1024]{1,0:T(8,128)(2,1)S(1)} %get-tuple-element.29.refs_1_, ...), custom_call_target="tpu_custom_call" | custom-call | flops 134217728 | bytes 5242880 | tf_op jit(solution)/shard_map/key_grads/pallas_call | solution.py:200
  57.9 3.7 %collective-permute-done.9.refs_3_ = bf16[128,1024]{1,0:T(8,128)(2,1)S(1)} collective-permute-done((bf16[128,1024]{1,0:T(8,128)(2,1)S(1)}, bf16[128,1024]{1,0:T(8,128)(2,1)S(1)}, u32[]{:S(2)}, u32[]{:S(2)}) %collective-permute-start.9) | collective-permute-done | bytes 262176 | tf_op jit(solution)/shard_map/ppermute | solution.py:248
  61.6 0.9 %query_sum.1 = bf16[128,2048]{1,0:T(8,128)(2,1)} custom-call(f32[128,1024]{1,0:T(8,128)S(1)} %get-tuple-element.23.refs_0_, bf16[128,1024]{1,0:T(8,128)(2,1)S(1)} %collective-permute-done.6.refs_1_, f32[128,1024]{1,0:T(8,128)S(1)} %get-tuple-element.27.refs_2_, bf16[128,1024]{1,0:T(8,128)(2,1)S(1)} %collective-permute-done.9.refs_3_), custom_call_target="tpu_custom_call" | custom-call | flops 524288 | bytes 2097152 | tf_op jit(solution)/shard_map/query_sum/pallas_call | solution.py:220
  (40 shorter events, 4.5 us)
Async XLA Ops:
  0.6 11.2 %copy-start = (bf16[512,2048]{1,0:T(8,128)(2,1)S(1)}, bf16[512,2048]{1,0:T(8,128)(2,1)}, u32[]{:S(2)}) copy-start(bf16[512,2048]{1,0:T(8,128)(2,1)} %refs_2_.3) | copy-start | bytes 6291460
  0.6 11.2 %collective-permute-start.1 = (bf16[512,2048]{1,0:T(8,128)(2,1)}, bf16[512,2048]{1,0:T(8,128)(2,1)}, u32[]{:S(2)}, u32[]{:S(2)}) collective-permute-start(bf16[512,2048]{1,0:T(8,128)(2,1)} %refs_2_.3), channel_id=1, source_target_pairs={{0,8},{8,0},{16,24},{24,16},{1,9},{9,1},{17,25},{25,17},{2,10},{10... | collective-permute-start | bytes 6291464 | tf_op jit(solution)/shard_map/ppermute | solution.py:260
  2.4 9.4 %collective-permute-start = (bf16[128,1024]{1,0:T(8,128)(2,1)S(1)}, bf16[128,1024]{1,0:T(8,128)(2,1)S(1)}, u32[]{:S(2)}, u32[]{:S(2)}) collective-permute-start(bf16[128,1024]{1,0:T(8,128)(2,1)S(1)} %pad_maximum_fusion.1), channel_id=1, source_target_pairs={{0,16},{8,24},{16,0},{24,8},{1,17},{9,25},{17,1},{25,9},{2,18},{10... | collective-permute-start | bytes 786440 | tf_op jit(solution)/shard_map/ppermute | solution.py:245
  14.5 0.8 %copy-start.7 = (f32[128,1024]{1,0:T(8,128)}, f32[128,1024]{1,0:T(8,128)S(1)}, u32[]{:S(2)}) copy-start(f32[128,1024]{1,0:T(8,128)S(1)} %get-tuple-element.21.local) | copy-start | bytes 1572868
  15.3 5.6 %copy-start.4 = (bf16[1,128,2048]{2,1,0:T(8,128)(2,1)S(1)}, bf16[1,128,2048]{2,1,0:T(8,128)(2,1)}, u32[]{:S(2)}) copy-start(bf16[1,128,2048]{2,1,0:T(8,128)(2,1)} %param.8) | copy-start | bytes 1572868
  15.3 10.4 %copy-start.11 = (f32[1,16,128]{2,1,0:T(8,128)S(1)}, f32[1,16,128]{2,1,0:T(8,128)}, u32[]{:S(2)}) copy-start(f32[1,16,128]{2,1,0:T(8,128)} %param.14) | copy-start | bytes 24580
  15.3 10.9 %copy-start.12 = (s32[1,32]{1,0:T(1,128)S(1)}, s32[1,32]{1,0:T(1,128)}, u32[]{:S(2)}) copy-start(s32[1,32]{1,0:T(1,128)} %param.15) | copy-start | bytes 388
  15.3 11.7 %copy-start.3 = (bf16[1,128,2048]{2,1,0:T(8,128)(2,1)S(1)}, bf16[1,128,2048]{2,1,0:T(8,128)(2,1)}, u32[]{:S(2)}) copy-start(bf16[1,128,2048]{2,1,0:T(8,128)(2,1)} %param.13) | copy-start | bytes 1572868
  15.3 11.0 %collective-permute-start.2 = (bf16[128,1024]{1,0:T(8,128)(2,1)}, bf16[128,1024]{1,0:T(8,128)(2,1)S(1)}, u32[]{:S(2)}, u32[]{:S(2)}) collective-permute-start(bf16[128,1024]{1,0:T(8,128)(2,1)} %get-tuple-element.22), channel_id=1, source_target_pairs={{0,16},{8,24},{16,0},{24,8},{1,17},{9,25},{17,1},{25,9},{2,18},{10... | collective-permute-start | bytes 786440 | tf_op jit(solution)/shard_map/ppermute | solution.py:245
  19.8 0.8 %copy-start.5 = (f32[128,1024]{1,0:T(8,128)}, f32[128,1024]{1,0:T(8,128)S(1)}, u32[]{:S(2)}) copy-start(f32[128,1024]{1,0:T(8,128)S(1)} %get-tuple-element.25.local) | copy-start | bytes 1572868
  20.6 24.0 %copy-start.1 = (bf16[1,128,2048]{2,1,0:T(8,128)(2,1)S(1)}, bf16[1,128,2048]{2,1,0:T(8,128)(2,1)}, u32[]{:S(2)}) copy-start(bf16[1,128,2048]{2,1,0:T(8,128)(2,1)} %param.9) | copy-start | bytes 1572868
  20.6 24.0 %copy-start.2 = (bf16[1,128,2048]{2,1,0:T(8,128)(2,1)S(1)}, bf16[1,128,2048]{2,1,0:T(8,128)(2,1)}, u32[]{:S(2)}) copy-start(bf16[1,128,2048]{2,1,0:T(8,128)(2,1)} %param.10) | copy-start | bytes 1572868
  20.6 11.5 %collective-permute-start.7 = (bf16[128,1024]{1,0:T(8,128)(2,1)}, bf16[128,1024]{1,0:T(8,128)(2,1)}, u32[]{:S(2)}, u32[]{:S(2)}) collective-permute-start(bf16[128,1024]{1,0:T(8,128)(2,1)} %get-tuple-element.26), channel_id=1, source_target_pairs={{0,16},{8,24},{16,0},{24,8},{1,17},{9,25},{17,1},{25,9},{2,18},{10... | collective-permute-start | bytes 786440 | tf_op jit(solution)/shard_map/ppermute | solution.py:245
  20.9 17.4 %collective-permute-start.3 = (bf16[128,2048]{1,0:T(8,128)(2,1)S(1)}, bf16[128,2048]{1,0:T(8,128)(2,1)S(1)}, u32[]{:S(2)}, u32[]{:S(2)}) collective-permute-start(bf16[128,2048]{1,0:T(8,128)(2,1)S(1)} %bitcast.30), channel_id=1, source_target_pairs={{0,7},{1,0},{2,1},{3,2},{4,3},{5,4},{6,5},{7,6},{8,15},{9,8},{10,9... | collective-permute-start | bytes 1572872 | tf_op jit(solution)/shard_map/ppermute | solution.py:248
  25.7 12.6 %collective-permute-start.5 = (f32[16,128]{1,0:T(8,128)S(1)}, f32[16,128]{1,0:T(8,128)S(1)}, u32[]{:S(2)}, u32[]{:S(2)}) collective-permute-start(f32[16,128]{1,0:T(8,128)S(1)} %bitcast.33), channel_id=1, source_target_pairs={{0,7},{1,0},{2,1},{3,2},{4,3},{5,4},{6,5},{7,6},{8,15},{9,8},{10,9... | collective-permute-start | bytes 24584 | tf_op jit(solution)/shard_map/ppermute | solution.py:248
  26.3 0.7 %copy-start.9 = (bf16[128,1024]{1,0:T(8,128)(2,1)}, bf16[128,1024]{1,0:T(8,128)(2,1)S(1)}, u32[]{:S(2)}) copy-start(bf16[128,1024]{1,0:T(8,128)(2,1)S(1)} %collective-permute-done.2.refs_0_) | copy-start | bytes 786436
  27.0 1.0 %copy-start.8 = (f32[128,1024]{1,0:T(8,128)S(1)}, f32[128,1024]{1,0:T(8,128)}, u32[]{:S(2)}) copy-start(f32[128,1024]{1,0:T(8,128)} %copy-done.7) | copy-start | bytes 1572868
  28.0 0.9 %copy-start.10 = (bf16[128,1024]{1,0:T(8,128)(2,1)S(1)}, bf16[128,1024]{1,0:T(8,128)(2,1)}, u32[]{:S(2)}) copy-start(bf16[128,1024]{1,0:T(8,128)(2,1)} %copy-done.9) | copy-start | bytes 786436
  29.4 15.2 %collective-permute-start.4 = (bf16[144,1024]{1,0:T(8,128)(2,1)S(1)}, bf16[144,1024]{1,0:T(8,128)(2,1)S(1)}, u32[]{:S(2)}, u32[]{:S(2)}) collective-permute-start(bf16[144,1024]{1,0:T(8,128)(2,1)S(1)} %combine.2.msg), channel_id=1, source_target_pairs={{0,7},{1,0},{2,1},{3,2},{4,3},{5,4},{6,5},{7,6},{8,15},{9,8},{10,9... | collective-permute-start | bytes 884744 | tf_op jit(solution)/shard_map/ppermute | solution.py:248
  32.1 1.0 %copy-start.6 = (f32[128,1024]{1,0:T(8,128)S(1)}, f32[128,1024]{1,0:T(8,128)}, u32[]{:S(2)}) copy-start(f32[128,1024]{1,0:T(8,128)} %copy-done.5) | copy-start | bytes 1572868
  35.2 13.7 %collective-permute-start.8 = (bf16[144,1024]{1,0:T(8,128)(2,1)}, bf16[144,1024]{1,0:T(8,128)(2,1)S(1)}, u32[]{:S(2)}, u32[]{:S(2)}) collective-permute-start(bf16[144,1024]{1,0:T(8,128)(2,1)} %combine.3.msg), channel_id=1, source_target_pairs={{0,7},{1,0},{2,1},{3,2},{4,3},{5,4},{6,5},{7,6},{8,15},{9,8},{10,9... | collective-permute-start | bytes 884744 | tf_op jit(solution)/shard_map/ppermute | solution.py:248
  46.4 11.5 %collective-permute-start.6 = (bf16[128,1024]{1,0:T(8,128)(2,1)S(1)}, bf16[128,1024]{1,0:T(8,128)(2,1)S(1)}, u32[]{:S(2)}, u32[]{:S(2)}) collective-permute-start(bf16[128,1024]{1,0:T(8,128)(2,1)S(1)} %get-tuple-element.24), channel_id=1, source_target_pairs={{0,1},{1,2},{2,3},{3,4},{4,5},{5,6},{6,7},{7,0},{8,9},{9,10},{10,1... | collective-permute-start | bytes 786440 | tf_op jit(solution)/shard_map/ppermute | solution.py:248
  50.7 10.9 %collective-permute-start.9 = (bf16[128,1024]{1,0:T(8,128)(2,1)S(1)}, bf16[128,1024]{1,0:T(8,128)(2,1)S(1)}, u32[]{:S(2)}, u32[]{:S(2)}) collective-permute-start(bf16[128,1024]{1,0:T(8,128)(2,1)S(1)} %get-tuple-element.28), channel_id=1, source_target_pairs={{0,1},{1,2},{2,3},{3,4},{4,5},{5,6},{6,7},{7,0},{8,9},{9,10},{10,1... | collective-permute-start | bytes 786440 | tf_op jit(solution)/shard_map/ppermute | solution.py:248

commit v2 on v0

v2 whole, which is shorter than its diff:
```python
import functools

import jax
import jax.numpy as jnp
from jax import lax
from jax.experimental import pallas as pl
from jax.experimental.pallas import tpu as pltpu
from jax.sharding import PartitionSpec as P

GROUP = 32
CHUNKS = (8, 8)
REPEAT = False
LANES = 256
EXTRA = 16
VMEM_MIB = 20
F32 = jnp.float32
BF16 = jnp.bfloat16


def dot(a, b, ca, cb):
    return lax.dot_general(a, b, (((ca,), (cb,)), ((), ())), preferred_element_type=F32)


def here_in(space):
    return pl.BlockSpec(memory_space=space)


def pin(array):
    return pltpu.with_memory_space_constraint(array, pltpu.VMEM)


def call(body, name, ins, outs, after=(), scalars=(), free=()):
    n_in, n_after = len(scalars) + len(ins), len(after)

    def kernel(*refs):
        body(refs[:n_in], refs[n_in + n_after :])

    moved = sum(a.size * a.dtype.itemsize for a in ins) + sum(jnp.dtype(t).itemsize * r * c for r, c, t, _ in outs)
    return pl.pallas_call(
        kernel,
        in_specs=[here_in(pltpu.SMEM)] * len(scalars) + [here_in(pltpu.VMEM)] * len(ins) + [here_in(pl.ANY)] * n_after,
        out_specs=[here_in(pltpu.VMEM)] * len(outs),
        out_shape=[pltpu.VMEM((r, c), t) if kept else jax.ShapeDtypeStruct((r, c), t) for r, c, t, kept in outs],
        compiler_params=pltpu.CompilerParams(vmem_limit_bytes=VMEM_MIB * 1024 * 1024),
        cost_estimate=pl.CostEstimate(flops=int(1e9), bytes_accessed=int(1 * moved), transcendentals=0),
        name=name,
    )(*scalars, *[a if i in free else pin(a) for i, a in enumerate(ins)], *after)


def stage(parts, first, width, after=()):
    rows, n, n_after = parts[0].shape[0], len(parts), len(after)

    def kernel(*refs):
        out = refs[n + n_after]

        def copy(semaphores):
            moves = []
            for i in range(n):
                source = refs[i].at[:, pl.ds(first, width)]
                moves.append(pltpu.make_async_copy(source, out.at[:, pl.ds(i * width, width)], semaphores.at[i]))
                moves[i].start()
            for move in moves:
                move.wait()

        pl.run_scoped(copy, pltpu.SemaphoreType.DMA((n,)))

    return pl.pallas_call(
        kernel,
        in_specs=[here_in(pl.ANY)] * (n + n_after),
        out_specs=here_in(pltpu.VMEM),
        out_shape=pltpu.VMEM((rows, n * width), parts[0].dtype),
        compiler_params=pltpu.CompilerParams(vmem_limit_bytes=VMEM_MIB * 1024 * 1024),
        cost_estimate=pl.CostEstimate(flops=int(1e9), bytes_accessed=4 * rows * n * width, transcendentals=0),
        name="stage",
    )(*[pltpu.with_memory_space_constraint(a, pltpu.HBM) for a in parts], *after)


def project(place, sources, weights, first, width, kind, after=()):
    pair = len(weights)
    tokens = sources[0].shape[0]
    rows = weights[0].shape[0]

    def body(ins, outs):
        place, sources, weights = ins[0], ins[1 : 1 + len(sources_in)], ins[1 + len(sources_in) :]
        lhs = []
        for i in range(pair):
            start = (place[0] * pair + (place[1] + i) % pair) * rows
            part = pl.ds(pl.multiple_of(start, rows), rows)
            blocks = [ref[:, part] for ref in sources]
            lhs.append(blocks[0] if len(blocks) == 1 else jnp.concatenate(blocks, axis=0))
        for at in range(0, width, LANES):
            cols = slice(at, at + LANES)
            from_cols = slice(first + at, first + at + LANES)
            total = dot(lhs[0], weights[0][:, from_cols], 1, 0)
            for i in range(1, pair):
                total += dot(lhs[i], weights[i][:, from_cols], 1, 0)
            for j, ref in enumerate(outs):
                ref[:, cols] = total[j * tokens : (j + 1) * tokens].astype(kind)

    sources_in = list(sources)
    return call(
        body, "project", [*sources, *weights], [(tokens, width, kind, True)] * len(sources), after, (place,), (len(sources), len(sources) + 1),
    )


def combine(local, parts, attn_out, lse, first, heads, after=()):
    tokens, width = local.shape
    size = width // heads
    head0 = first // size

    def body(ins, outs):
        local, parts, attn_out, lse = ins[0], ins[1:-2], ins[-2], ins[-1]
        (msg,) = outs
        total = local[...]
        for ref in parts:
            total += ref[...].astype(F32)
        grad = total.astype(BF16)
        msg[:tokens, :] = grad
        product = grad.astype(F32) * attn_out[:, first : first + width].astype(F32)
        high = product.astype(BF16)
        low = (product - high.astype(F32)).astype(BF16)
        ones = jnp.ones((8, size), BF16)
        rows, lses = [], []
        for h in range(heads):
            cols = slice(h * size, (h + 1) * size)
            rows.append(dot(ones, high[:, cols], 1, 1) + dot(ones, low[:, cols], 1, 1))
            lses.append(jnp.broadcast_to(lse[head0 + h : head0 + h + 1, :], (8, tokens)))
        pick = lax.broadcasted_iota(jnp.int32, (8, width), 0)
        both = jnp.where(pick < 3, jnp.concatenate(rows, axis=1), jnp.concatenate(lses, axis=1))
        first_part = both.astype(BF16).astype(F32)
        rest = both - first_part
        second = rest.astype(BF16).astype(F32)
        third = rest - second
        turn = jnp.where(pick < 3, pick, pick - 3)
        kept = jnp.where(turn == 0, first_part, jnp.where(turn == 1, second, third))
        msg[tokens:, :] = jnp.concatenate([kept, kept], axis=0).astype(BF16)

    (msg,) = call(
        body, "combine", [local, *parts, attn_out, lse], [(tokens + EXTRA, width, BF16, True)], after,
    )
    return msg


def rows_of(msg, tokens, cols):
    tail = msg[tokens:, cols].astype(F32)
    return tail[0:1] + tail[1:2] + tail[2:3], tail[3:4] + tail[4:5] + tail[5:6]


def weights_of(q, k, v, g, rows, bias):
    delta, lse = rows
    probs = jnp.exp(dot(k, q, 1, 1) * (q.shape[1] ** -0.5) - lse + bias)
    return probs.astype(BF16), (probs * (dot(v, g, 1, 1) - delta)).astype(BF16)


def places(first, heads, size):
    return [(slice(h * size, (h + 1) * size), slice(first + h * size, first + (h + 1) * size)) for h in range(heads)]


def own_pair(query, key, value, msg, bias, first, heads, before=(), after=()):
    tokens, width = query.shape[0], msg.shape[1]
    size = width // heads
    factor = size ** -0.5

    def body(ins, outs):
        query, key, value, msg, bias = ins[:5]
        dq, dk, dv = outs
        for cols, place in places(first, heads, size):
            q, k, v, g = query[:, place], key[:, place], value[:, place], msg[:tokens, cols]
            rows = rows_of(msg, tokens, cols)
            probs, dscores = weights_of(q, k, v, g, rows, bias[...])
            dv[:, cols] = dot(probs, g, 1, 0)
            dk[:, cols] = dot(dscores, q, 1, 0)
            total = dot(dscores, k, 0, 0)
            if before:
                pairs, bias_before = ins[5:]
                k_old, v_old = pairs[:, cols], pairs[:, slice(width + cols.start, width + cols.stop)]
                _, dscores = weights_of(q, k_old, v_old, g, rows, bias_before[...])
                total += dot(dscores, k_old, 0, 0)
            dq[:, cols] = (total * factor).astype(dq.dtype)

    kind = BF16 if before else F32
    return call(
        body, "own_pair", [query, key, value, msg, bias, *before],
        [(tokens, width, kind, True), (tokens, width, F32, True), (tokens, width, F32, True)], after,
    )


def cross_pair(query, key, value, msg, bias, first, heads, after=()):
    tokens, width = query.shape[0], msg.shape[1]
    size = width // heads
    factor = size ** -0.5

    def body(ins, outs):
        query, key, value, msg, bias = ins
        dq, probs_out, dscores_out = outs
        for cols, place in places(first, heads, size):
            q, k, v, g = query[:, place], key[:, place], value[:, place], msg[:tokens, cols]
            probs, dscores = weights_of(q, k, v, g, rows_of(msg, tokens, cols), bias[...])
            probs_out[:, cols] = probs
            dscores_out[:, cols] = dscores
            dq[:, cols] = (dot(dscores, k, 0, 0) * factor).astype(BF16)

    return call(
        body, "cross_pair", [query, key, value, msg, bias], [(tokens, width, BF16, True)] * 3, after,
    )


def key_grads(query, key, value, bias, groups, plan, after=()):
    tokens, width = query.shape

    def body(ins, outs):
        query, key, value, bias = ins[:4]
        dk_out, dv_out = outs
        at = 4
        for (first, part, heads), group in zip(plan, groups):
            size = part // heads
            factor = size ** -0.5
            refs = ins[at : at + len(group)]
            at += len(group)
            msg, dk, dv = refs[:3]
            for cols, place in places(first, heads, size):
                q, g = query[:, place], msg[:tokens, cols]
                if len(refs) > 3:
                    probs, dscores = refs[3][:, cols], refs[4][:, cols]
                else:
                    rows = rows_of(msg, tokens, cols)
                    probs, dscores = weights_of(q, key[:, place], value[:, place], g, rows, bias[...])
                dk_out[:, place] = ((dk[:, cols] + dot(dscores, q, 1, 0)) * factor).astype(BF16)
                dv_out[:, place] = (dv[:, cols] + dot(probs, g, 1, 0)).astype(BF16)

    return call(
        body, "key_grads", [query, key, value, bias] + [a for group in groups for a in group],
        [(tokens, width, BF16, False)] * 2, after,
    )


def query_grads(groups, plan, after=()):
    tokens, width = groups[0][0].shape[0], sum(part for _, part, _ in plan)

    def body(ins, outs):
        (out,) = outs
        at = 0
        for (first, part, _), group in zip(plan, groups):
            total = ins[at][...]
            if len(group) > 1:
                total = (total + ins[at + 1][...].astype(F32)).astype(BF16)
            out[:, first : first + part] = total
            at += len(group)

    (out,) = call(body, "query_grads", [a for group in groups for a in group], [(tokens, width, BF16, False)], after)
    return out


def on_device(queries, keys, values, out_grad, out_proj, attn_out, log_sum, group_order):
    tokens, width = queries.shape[1:]
    heads = log_sum.shape[1]
    size = width // heads
    rows = out_proj.shape[0]
    query, key, value, upstream, output = queries[0], keys[0], values[0], out_grad[0], attn_out[0]
    lse = log_sum[0]
    order = group_order[0]
    dp, ctx = lax.axis_size("dp"), lax.axis_size("ctx")
    me, here = lax.axis_index("dp"), lax.axis_index("ctx")
    pair = 2 if dp % 2 == 0 else 1
    chips = dp // pair
    core, chip = me % pair, me // pair

    def along_dp(array, by):
        return lax.ppermute(array, "dp", [(i, (i + by) % dp) for i in range(dp)])

    def along_ctx(array, by):
        return lax.ppermute(array, "ctx", [(i, (i + by) % ctx) for i in range(ctx)])

    def columns_for(there):
        return lax.dynamic_slice_in_dim(upstream, there * (pair * rows), pair * rows, axis=1)

    pieces = [columns_for((chip + j) % chips) for j in range(1, chips)]
    arrived = [along_dp(piece, pair * (j + 1)) for j, piece in enumerate(pieces)]
    at_own = jnp.stack([chip, core]).astype(jnp.int32)
    at_cut = jnp.stack([jnp.zeros_like(core), core]).astype(jnp.int32)
    weights = [stage([out_proj], 0, width, pieces)]
    if pair == 2:
        weights.append(lax.ppermute(out_proj, "dp", [(i, i ^ 1) for i in range(dp)]))
    query_sent, _ = lax.optimization_barrier((query, pieces))
    query_next = along_ctx(query_sent, -1)

    per_block = tokens // GROUP

    def positions(device):
        ids = lax.dynamic_slice_in_dim(order, device * per_block, per_block)
        return (ids[:, None] * GROUP + jnp.arange(GROUP, dtype=jnp.int32)[None, :]).reshape(tokens)

    def bias_of(key_block, query_block):
        visible = positions(key_block)[:, None] <= positions(query_block)[None, :]
        return jnp.where(visible, 0.0, -jnp.inf).astype(F32)

    bias_own = bias_of(here, here)
    bias_next = bias_of(here, (here + 1) % ctx)
    bias_before = bias_of((here + ctx - 1) % ctx, here)

    shares = CHUNKS if heads % sum(CHUNKS) == 0 else (1, 0)
    counts = [share * heads // sum(shares) for share in shares]
    plan, done = [], 0
    for count in counts:
        if count:
            plan.append((done * size, count * size, count))
            done += count

    backs, held = [], []
    for first, part, _ in plan:
        remote = project(at_cut, arrived, weights, first, part, BF16, after=held) if arrived else []
        held = list(remote[:1])
        backs.append([along_dp(remote[j - 1], -pair * j) for j in range(1, chips)])

    before = []
    if REPEAT and len(plan) > 1:
        first, part, _ = plan[1]
        before = [along_ctx(stage([key, value], first, part, held), 1)]

    msgs, nexts = [], []
    for c, (first, part, count) in enumerate(plan):
        waits = [query_next] if c == 0 else before + msgs
        (local,) = project(at_own, [upstream], weights, first, part, F32, after=waits + held)
        msgs.append(combine(local, backs[c], output, lse, first, count))
        nexts.append(along_ctx(msgs[c], -1))

    crosses = []
    for c, (first, part, count) in enumerate(plan):
        if not (c and before):
            crosses.append(cross_pair(query_next, key, value, nexts[c], bias_next, first, count))
    sent = [cross[0] for cross in crosses]
    backs = [along_ctx(dq, 1) for dq in sent]
    key_parts, query_parts = [], []
    for c, (first, part, count) in enumerate(plan):
        if c and before:
            extra = (before[0], bias_before)
            own = own_pair(query, key, value, msgs[c], bias_own, first, count, before=extra, after=sent)
            key_parts.append((nexts[c], own[1], own[2]))
            query_parts.append((own[0],))
        else:
            own = own_pair(query, key, value, msgs[c], bias_own, first, count, after=sent)
            key_parts.append((nexts[c], own[1], own[2], crosses[c][1], crosses[c][2]))
            query_parts.append((own[0], backs[c]))
    key_grad, value_grad = key_grads(query_next, key, value, bias_next, key_parts, plan)
    query_grad = query_grads(query_parts, plan)
    shape = (1, tokens, width)
    return query_grad.reshape(shape), key_grad.reshape(shape), value_grad.reshape(shape)


def solution(mesh):
    return jax.shard_map(
        on_device,
        mesh=mesh,
        in_specs=(
            P("dp", "ctx", None),
            P("dp", "ctx", None),
            P("dp", "ctx", None),
            P("dp", "ctx", None),
            P("dp", None),
            P("dp", "ctx", None),
            P("dp", None, "ctx"),
            P("dp", None),
        ),
        out_specs=(P("dp", "ctx", None), P("dp", "ctx", None), P("dp", "ctx", None)),
        check_vma=False,
    )
```

time: 139 us -> 53.3 us (0.38)
  waiting for transfers between devices: 64.9 us -> 16.6 us
  matrix products: 25.2 us -> 0 us
  Pallas kernels: 0 us -> 16.1 us
  local copies, waits for them, and re-layouts: 16.9 us -> 1.16 us
  between operations: 14.2 us -> 0.79 us
  starting transfers between devices: 12.1 us -> 17.3 us
  other arithmetic: 5.06 us -> 1.11 us
    all_gather x1 -> x0, waiting for transfers between devices: 38.3 us -> none  [on_device(): lax.all_gather(out_proj, 'dp', axis=0, tiled=True)]
    dot_general x11 -> x0, matrix products: 25.2 us -> none  [the longest x2 5.34 us: pair_grads(): jnp.einsum('qhd,khd->hqk', query_blk, key_blk, preferred_element_type=jnp...]
    pallas_call x0 -> x13, Pallas kernels: none -> 16.1 us  [the longest x12 14.5 us: call(): pl.pallas_call(kernel, in_specs=[here_in(pltpu.SMEM)] * len(scalars) + [h...]
    ppermute x5 -> x9, waiting for transfers between devices: 26 us -> 16.6 us  [the longest x5 16.5 us: along_ctx(): return lax.ppermute(array, 'ctx', [(i, (i + by) % ctx) for i in range(ctx)])]
    unnamed x13 -> x12, local copies, waits for them, and re-layouts: 6.91 us -> 0.03 us
    ppermute x5 -> x9, starting transfers between devices: 12.1 us -> 17.3 us  [the longest x5 12 us: along_ctx(): return lax.ppermute(array, 'ctx', [(i, (i + by) % ctx) for i in range(ctx)])]
    mul x2 -> x0, local copies, waits for them, and re-layouts: 5.09 us -> none  [pair_grads(): jnp.einsum('hqk,khd->qhd', dscores, key_blk, preferred_element_type=jnp.f...]
    another operation x2 -> x0, local copies, waits for them, and re-layouts: 2.51 us -> none  [the longest x1 2.04 us: on_device(): query_blk = queries[0].reshape(tokens, heads, head_size)]
  transfers between devices with their start and end apart: 6 -> 9, of which waited for: 4 -> 6; matrix products, arithmetic and copies ran while one was open for 23% -> 4% of each run, Pallas kernels for 0% -> 29%
where the time goes in v2:
time: 53.3 us; the launch traced here: 53.1 us
  starting transfers between devices  17.3 us (32%)
  waiting for transfers between devices  16.6 us (31%)
  Pallas kernels  16.1 us (30%)
  local copies, waits for them, and re-layouts  1.16 us (2%)
  other arithmetic  1.11 us (2%)
  between operations  0.79 us (1%)
    ppermute x5, waiting for transfers between devices, along_ctx(): return lax.ppermute(array, 'ctx', [(i, (i + by) % ctx) for i in range(ctx)])  16.5 us
    pallas_call x12, Pallas kernels, call(): pl.pallas_call(kernel, in_specs=[here_in(pltpu.SMEM)] * len(scalars) + [h...  14.5 us
    ppermute x5, starting transfers between devices, along_ctx(): return lax.ppermute(array, 'ctx', [(i, (i + by) % ctx) for i in range(ctx)])  12 us
    ppermute x3, starting transfers between devices, along_dp(): return lax.ppermute(array, 'dp', [(i, (i + by) % dp) for i in range(dp)])  4.77 us
    pallas_call x1, Pallas kernels, stage(): pl.pallas_call(kernel, in_specs=[here_in(pl.ANY)] * (n + n_after), out_sp...  1.6 us
  transfers between devices with their start and end apart: 9, of which 6 were waited for; matrix products, arithmetic and copies ran while one was open for 4% of the time, Pallas kernels for 29%

profile of v2, /device:TPU:0, one launch (start us, length us, event | category | flops | bytes accessed | tf_op | source)
XLA Modules:
  0.0 53.1 jit_solution(11066003559305313523)
XLA Ops:
  0.6 0.5 collective-permute-start
  1.1 1.0 %dynamic-slice_bitcast_fusion.refs_1_ = bf16[128,1024]{1,0:T(8,128)(2,1)S(1)} fusion(bf16[1,128,2048]{2,1,0:T(8,128)(2,1)} %param.11, s32[]{:T(128)S(6)} %select_n.40), kind=kLoop, calls=%fused_computation | loop fusion | bytes 524292 | tf_op jit(solution)/shard_map/dynamic_slice | solution.py:275
  2.1 2.6 %collective-permute-start.2 = (bf16[128,1024]{1,0:T(8,128)(2,1)S(1)}, bf16[128,1024]{1,0:T(8,128)(2,1)S(1)}, u32[]{:S(2)}, u32[]{:S(2)}) collective-permute-start(bf16[128,1024]{1,0:T(8,128)(2,1)S(1)} %dynamic-slice_bitcast_fusion.refs_1_), channel_id=1, source_target_pairs={{0,16},{8,24},{16,0},{24,8},{1,17},{9,25},{17,1},{25,9},{2,18},{10... | collective-permute-start | bytes 786440 | tf_op jit(solution)/shard_map/ppermute | solution.py:269
  4.7 4.6 %collective-permute-start.1 = (bf16[128,2048]{1,0:T(8,128)(2,1)}, bf16[128,2048]{1,0:T(8,128)(2,1)S(1)}, u32[]{:S(2)}, u32[]{:S(2)}) collective-permute-start(bf16[128,2048]{1,0:T(8,128)(2,1)} %bitcast.31), channel_id=1, source_target_pairs={{0,7},{1,0},{2,1},{3,2},{4,3},{5,4},{6,5},{7,6},{8,15},{9,8},{10,9... | collective-permute-start | bytes 1572872 | tf_op jit(solution)/shard_map/ppermute | solution.py:272
  9.3 0.8 %fusion.3 = (s32[4]{0:T(128)S(1)}, s32[4]{0:T(128)S(1)}) fusion(s32[1,32]{1,0:T(1,128)} %param.15, s32[]{:T(128)S(6)} %select_n.44, s32[]{:T(128)S(6)} %select_n.41), kind=kLoop, calls=%fused_computation.10 | loop fusion | flops 8 | bytes 72 | tf_op jit(solution)/shard_map/mul | solution.py:291
  10.3 1.6 %stage.1.refs_2_ = bf16[512,2048]{1,0:T(8,128)(2,1)S(1)} custom-call(bf16[512,2048]{1,0:T(8,128)(2,1)} %refs_0_.1, bf16[128,1024]{1,0:T(8,128)(2,1)S(1)} %dynamic-slice_bitcast_fusion.refs_1_), custom_call_target="tpu_custom_call" | custom-call | flops 1000000000 | bytes 4194304 | tf_op jit(solution)/shard_map/stage/pallas_call | solution.py:67
  12.0 1.0 %project.4.refs_4_ = bf16[128,1024]{1,0:T(8,128)(2,1)S(1)} custom-call(s32[2]{0:T(128)S(1)} %pad_add_fusion.1.refs_0_, bf16[128,1024]{1,0:T(8,128)(2,1)S(1)} %collective-permute-done.2.refs_1_, bf16[512,2048]{1,0:T(8,128)(2,1)S(1)} %stage.1.refs_2_, bf16[512,2048]{1,0:T(8,128)(2,1)S(1)} %collective-permute-done.refs_3_), custom_call_target="tpu_custom_call" | custom-call | flops 1000000000 | bytes 4718592 | tf_op jit(solution)/shard_map/project/pallas_call | solution.py:39
  13.0 1.5 %collective-permute-start.3 = (bf16[128,1024]{1,0:T(8,128)(2,1)S(1)}, bf16[128,1024]{1,0:T(8,128)(2,1)S(1)}, u32[]{:S(2)}, u32[]{:S(2)}) collective-permute-start(bf16[128,1024]{1,0:T(8,128)(2,1)S(1)} %project.4.refs_4_), channel_id=1, source_target_pairs={{0,16},{8,24},{16,0},{24,8},{1,17},{9,25},{17,1},{25,9},{2,18},{10... | collective-permute-start | bytes 786440 | tf_op jit(solution)/shard_map/ppermute | solution.py:269
  14.5 1.0 %project.5.refs_5_ = bf16[128,1024]{1,0:T(8,128)(2,1)S(1)} custom-call(s32[2]{0:T(128)S(1)} %pad_add_fusion.1.refs_0_, bf16[128,1024]{1,0:T(8,128)(2,1)S(1)} %collective-permute-done.2.refs_1_, bf16[512,2048]{1,0:T(8,128)(2,1)S(1)} %stage.1.refs_2_, bf16[512,2048]{1,0:T(8,128)(2,1)S(1)} %collective-permute-done.refs_3_, bf16[128,1024]{1,0:T(8,128)(2,1)S(1)} %project.4.refs_4_), custom_call_target="tpu_custom_call" | custom-call | flops 1000000000 | bytes 4718592 | tf_op jit(solution)/shard_map/project/pallas_call | solution.py:39
  15.5 0.7 %collective-permute-start.5 = (bf16[128,1024]{1,0:T(8,128)(2,1)S(1)}, bf16[128,1024]{1,0:T(8,128)(2,1)S(1)}, u32[]{:S(2)}, u32[]{:S(2)}) collective-permute-start(bf16[128,1024]{1,0:T(8,128)(2,1)S(1)} %project.5.refs_5_), channel_id=1, source_target_pairs={{0,16},{8,24},{16,0},{24,8},{1,17},{9,25},{17,1},{25,9},{2,18},{10... | collective-permute-start | bytes 786440 | tf_op jit(solution)/shard_map/ppermute | solution.py:269
  16.2 4.9 %collective-permute-done.1.refs_4_.refs_0_ = bf16[128,2048]{1,0:T(8,128)(2,1)S(1)} collective-permute-done((bf16[128,2048]{1,0:T(8,128)(2,1)}, bf16[128,2048]{1,0:T(8,128)(2,1)S(1)}, u32[]{:S(2)}, u32[]{:S(2)}) %collective-permute-start.1) | collective-permute-done | bytes 524320 | tf_op jit(solution)/shard_map/ppermute | solution.py:272
  21.1 1.0 %project.6.refs_0_ = f32[128,1024]{1,0:T(8,128)S(1)} custom-call(s32[2]{0:T(128)S(1)} %pad_add_fusion.refs_0_, bf16[128,2048]{1,0:T(8,128)(2,1)S(1)} %bitcast.17, bf16[512,2048]{1,0:T(8,128)(2,1)S(1)} %stage.1.refs_2_, bf16[512,2048]{1,0:T(8,128)(2,1)S(1)} %collective-permute-done.refs_3_, bf16[128,2048]{1,0:T(8,128)(2,1)S(1)} %collective-permute-done.1.refs_4_.refs_0_, ...), custom_call_target="tpu_custom_call" | custom-call | flops 1000000000 | bytes 5242880 | tf_op jit(solution)/shard_map/project/pallas_call | solution.py:39
  22.7 5.0 %collective-permute-start.4 = (bf16[144,1024]{1,0:T(8,128)(2,1)S(1)}, bf16[144,1024]{1,0:T(8,128)(2,1)S(1)}, u32[]{:S(2)}, u32[]{:S(2)}) collective-permute-start(bf16[144,1024]{1,0:T(8,128)(2,1)S(1)} %combine.2.refs_4_.refs_3_), channel_id=1, source_target_pairs={{0,7},{1,0},{2,1},{3,2},{4,3},{5,4},{6,5},{7,6},{8,15},{9,8},{10,9... | collective-permute-start | bytes 884744 | tf_op jit(solution)/shard_map/ppermute | solution.py:272
  27.7 1.0 %project.7.refs_0_ = f32[128,1024]{1,0:T(8,128)S(1)} custom-call(s32[2]{0:T(128)S(1)} %pad_add_fusion.refs_0_, bf16[128,2048]{1,0:T(8,128)(2,1)S(1)} %bitcast.18, bf16[512,2048]{1,0:T(8,128)(2,1)S(1)} %stage.1.refs_2_, bf16[512,2048]{1,0:T(8,128)(2,1)S(1)} %collective-permute-done.refs_3_, bf16[144,1024]{1,0:T(8,128)(2,1)S(1)} %combine.2.refs_4_.refs_3_, ...), custom_call_target="tpu_custom_call" | custom-call | flops 1000000000 | bytes 5242880 | tf_op jit(solution)/shard_map/project/pallas_call | solution.py:39
  29.2 2.3 %collective-permute-start.6 = (bf16[144,1024]{1,0:T(8,128)(2,1)S(1)}, bf16[144,1024]{1,0:T(8,128)(2,1)S(1)}, u32[]{:S(2)}, u32[]{:S(2)}) collective-permute-start(bf16[144,1024]{1,0:T(8,128)(2,1)S(1)} %combine.3.refs_3_), channel_id=1, source_target_pairs={{0,7},{1,0},{2,1},{3,2},{4,3},{5,4},{6,5},{7,6},{8,15},{9,8},{10,9... | collective-permute-start | bytes 884744 | tf_op jit(solution)/shard_map/ppermute | solution.py:272
  31.6 3.6 %collective-permute-done.4.refs_3_.refs_4_ = bf16[144,1024]{1,0:T(8,128)(2,1)S(1)} collective-permute-done((bf16[144,1024]{1,0:T(8,128)(2,1)S(1)}, bf16[144,1024]{1,0:T(8,128)(2,1)S(1)}, u32[]{:S(2)}, u32[]{:S(2)}) %collective-permute-start.4) | collective-permute-done | bytes 294944 | tf_op jit(solution)/shard_map/ppermute | solution.py:272
  35.2 1.8 %cross_pair.2 = (bf16[128,1024]{1,0:T(8,128)(2,1)S(1)}, bf16[128,1024]{1,0:T(8,128)(2,1)S(1)}, bf16[128,1024]{1,0:T(8,128)(2,1)S(1)}) custom-call(bf16[128,2048]{1,0:T(8,128)(2,1)S(1)} %collective-permute-done.1.refs_4_.refs_0_, bf16[128,2048]{1,0:T(8,128)(2,1)S(1)} %bitcast.19, bf16[128,2048]{1,0:T(8,128)(2,1)S(1)} %bitcast.24, ...), custom_call_target="tpu_custom_call" | custom-call | flops 1000000000 | bytes 2719744 | tf_op jit(solution)/shard_map/cross_pair/pallas_call | solution.py:39
  37.1 2.7 %collective-permute-done.6.refs_3_.refs_9_ = bf16[144,1024]{1,0:T(8,128)(2,1)S(1)} collective-permute-done((bf16[144,1024]{1,0:T(8,128)(2,1)S(1)}, bf16[144,1024]{1,0:T(8,128)(2,1)S(1)}, u32[]{:S(2)}, u32[]{:S(2)}) %collective-permute-start.6) | collective-permute-done | bytes 294944 | tf_op jit(solution)/shard_map/ppermute | solution.py:272
  39.8 1.8 %cross_pair.3 = (bf16[128,1024]{1,0:T(8,128)(2,1)S(1)}, bf16[128,1024]{1,0:T(8,128)(2,1)S(1)}, bf16[128,1024]{1,0:T(8,128)(2,1)S(1)}) custom-call(bf16[128,2048]{1,0:T(8,128)(2,1)S(1)} %collective-permute-done.1.refs_4_.refs_0_, bf16[128,2048]{1,0:T(8,128)(2,1)S(1)} %bitcast.20, bf16[128,2048]{1,0:T(8,128)(2,1)S(1)} %bitcast.25, ...), custom_call_target="tpu_custom_call" | custom-call | flops 1000000000 | bytes 2719744 | tf_op jit(solution)/shard_map/cross_pair/pallas_call | solution.py:39
  41.7 1.8 %own_pair.3 = (f32[128,1024]{1,0:T(8,128)S(1)}, f32[128,1024]{1,0:T(8,128)S(1)}, f32[128,1024]{1,0:T(8,128)S(1)}) custom-call(bf16[128,2048]{1,0:T(8,128)(2,1)S(1)} %bitcast.32, bf16[128,2048]{1,0:T(8,128)(2,1)S(1)} %bitcast.21, bf16[128,2048]{1,0:T(8,128)(2,1)S(1)} %bitcast.26, bf16[144,1024]{1,0:T(8,128)(2,1)S(1)} %combine.3.refs_3_, ...), custom_call_target="tpu_custom_call" | custom-call | flops 1000000000 | bytes 3506176 | tf_op jit(solution)/shard_map/own_pair/pallas_call | solution.py:39
  43.6 1.8 %own_pair.2 = (f32[128,1024]{1,0:T(8,128)S(1)}, f32[128,1024]{1,0:T(8,128)S(1)}, f32[128,1024]{1,0:T(8,128)S(1)}) custom-call(bf16[128,2048]{1,0:T(8,128)(2,1)S(1)} %bitcast.33, bf16[128,2048]{1,0:T(8,128)(2,1)S(1)} %bitcast.22, bf16[128,2048]{1,0:T(8,128)(2,1)S(1)} %bitcast.27, bf16[144,1024]{1,0:T(8,128)(2,1)S(1)} %combine.2.refs_4_.refs_3_, ...), custom_call_target="tpu_custom_call" | custom-call | flops 1000000000 | bytes 3506176 | tf_op jit(solution)/shard_map/own_pair/pallas_call | solution.py:39
  45.4 1.5 %key_grads.1 = (bf16[128,2048]{1,0:T(8,128)(2,1)}, bf16[128,2048]{1,0:T(8,128)(2,1)}) custom-call(bf16[128,2048]{1,0:T(8,128)(2,1)S(1)} %collective-permute-done.1.refs_4_.refs_0_, bf16[128,2048]{1,0:T(8,128)(2,1)S(1)} %bitcast.23, bf16[128,2048]{1,0:T(8,128)(2,1)S(1)} %bitcast.28, f32[128,128]{1,0:T(8,128)S(1)} %get-tuple-element.33.refs_4_.refs_3_, ...), custom_call_target="tpu_custom_call" | custom-call | flops 1000000000 | bytes 6422528 | tf_op jit(solution)/shard_map/key_grads/pallas_call | solution.py:39
  47.0 5.2 %collective-permute-done.8.refs_3_ = bf16[128,1024]{1,0:T(8,128)(2,1)S(1)} collective-permute-done((bf16[128,1024]{1,0:T(8,128)(2,1)S(1)}, bf16[128,1024]{1,0:T(8,128)(2,1)S(1)}, u32[]{:S(2)}, u32[]{:S(2)}) %collective-permute-start.8) | collective-permute-done | bytes 262176 | tf_op jit(solution)/shard_map/ppermute | solution.py:272
  52.2 0.9 %query_grads.1 = bf16[128,2048]{1,0:T(8,128)(2,1)} custom-call(f32[128,1024]{1,0:T(8,128)S(1)} %get-tuple-element.21.refs_0_, bf16[128,1024]{1,0:T(8,128)(2,1)S(1)} %collective-permute-done.7.refs_1_, f32[128,1024]{1,0:T(8,128)S(1)} %get-tuple-element.22.refs_2_, bf16[128,1024]{1,0:T(8,128)(2,1)S(1)} %collective-permute-done.8.refs_3_), custom_call_target="tpu_custom_call" | custom-call | flops 1000000000 | bytes 2097152 | tf_op jit(solution)/shard_map/query_grads/pallas_call | solution.py:39
  (27 shorter events, 1.6 us)
Async XLA Ops:
  0.6 11.4 %collective-permute-start = (bf16[512,2048]{1,0:T(8,128)(2,1)}, bf16[512,2048]{1,0:T(8,128)(2,1)S(1)}, u32[]{:S(2)}, u32[]{:S(2)}) collective-permute-start(bf16[512,2048]{1,0:T(8,128)(2,1)} %refs_0_.1), channel_id=1, source_target_pairs={{0,8},{8,0},{16,24},{24,16},{1,9},{9,1},{17,25},{25,17},{2,10},{10... | collective-permute-start | bytes 6291464 | tf_op jit(solution)/shard_map/ppermute | solution.py:283
  2.1 9.9 %collective-permute-start.2 = (bf16[128,1024]{1,0:T(8,128)(2,1)S(1)}, bf16[128,1024]{1,0:T(8,128)(2,1)S(1)}, u32[]{:S(2)}, u32[]{:S(2)}) collective-permute-start(bf16[128,1024]{1,0:T(8,128)(2,1)S(1)} %dynamic-slice_bitcast_fusion.refs_1_), channel_id=1, source_target_pairs={{0,16},{8,24},{16,0},{24,8},{1,17},{9,25},{17,1},{25,9},{2,18},{10... | collective-permute-start | bytes 786440 | tf_op jit(solution)/shard_map/ppermute | solution.py:269
  4.7 16.4 %collective-permute-start.1 = (bf16[128,2048]{1,0:T(8,128)(2,1)}, bf16[128,2048]{1,0:T(8,128)(2,1)S(1)}, u32[]{:S(2)}, u32[]{:S(2)}) collective-permute-start(bf16[128,2048]{1,0:T(8,128)(2,1)} %bitcast.31), channel_id=1, source_target_pairs={{0,7},{1,0},{2,1},{3,2},{4,3},{5,4},{6,5},{7,6},{8,15},{9,8},{10,9... | collective-permute-start | bytes 1572872 | tf_op jit(solution)/shard_map/ppermute | solution.py:272
  13.0 9.2 %collective-permute-start.3 = (bf16[128,1024]{1,0:T(8,128)(2,1)S(1)}, bf16[128,1024]{1,0:T(8,128)(2,1)S(1)}, u32[]{:S(2)}, u32[]{:S(2)}) collective-permute-start(bf16[128,1024]{1,0:T(8,128)(2,1)S(1)} %project.4.refs_4_), channel_id=1, source_target_pairs={{0,16},{8,24},{16,0},{24,8},{1,17},{9,25},{17,1},{25,9},{2,18},{10... | collective-permute-start | bytes 786440 | tf_op jit(solution)/shard_map/ppermute | solution.py:269
  14.5 6.6 %copy-start = (bf16[1,128,2048]{2,1,0:T(8,128)(2,1)S(1)}, bf16[1,128,2048]{2,1,0:T(8,128)(2,1)}, u32[]{:S(2)}) copy-start(bf16[1,128,2048]{2,1,0:T(8,128)(2,1)} %param.11) | copy-start | bytes 1572868
  15.5 13.2 %collective-permute-start.5 = (bf16[128,1024]{1,0:T(8,128)(2,1)S(1)}, bf16[128,1024]{1,0:T(8,128)(2,1)S(1)}, u32[]{:S(2)}, u32[]{:S(2)}) collective-permute-start(bf16[128,1024]{1,0:T(8,128)(2,1)S(1)} %project.5.refs_5_), channel_id=1, source_target_pairs={{0,16},{8,24},{16,0},{24,8},{1,17},{9,25},{17,1},{25,9},{2,18},{10... | collective-permute-start | bytes 786440 | tf_op jit(solution)/shard_map/ppermute | solution.py:269
  21.1 1.1 %copy-start.3 = (bf16[1,128,2048]{2,1,0:T(8,128)(2,1)S(1)}, bf16[1,128,2048]{2,1,0:T(8,128)(2,1)}, u32[]{:S(2)}) copy-start(bf16[1,128,2048]{2,1,0:T(8,128)(2,1)} %param.13) | copy-start | bytes 1572868
  21.1 1.1 %copy-start.5 = (f32[1,16,128]{2,1,0:T(8,128)S(1)}, f32[1,16,128]{2,1,0:T(8,128)}, u32[]{:S(2)}) copy-start(f32[1,16,128]{2,1,0:T(8,128)} %param.14) | copy-start | bytes 24580
  22.7 12.5 %collective-permute-start.4 = (bf16[144,1024]{1,0:T(8,128)(2,1)S(1)}, bf16[144,1024]{1,0:T(8,128)(2,1)S(1)}, u32[]{:S(2)}, u32[]{:S(2)}) collective-permute-start(bf16[144,1024]{1,0:T(8,128)(2,1)S(1)} %combine.2.refs_4_.refs_3_), channel_id=1, source_target_pairs={{0,7},{1,0},{2,1},{3,2},{4,3},{5,4},{6,5},{7,6},{8,15},{9,8},{10,9... | collective-permute-start | bytes 884744 | tf_op jit(solution)/shard_map/ppermute | solution.py:272
  28.7 6.5 %copy-start.1 = (bf16[1,128,2048]{2,1,0:T(8,128)(2,1)S(1)}, bf16[1,128,2048]{2,1,0:T(8,128)(2,1)}, u32[]{:S(2)}) copy-start(bf16[1,128,2048]{2,1,0:T(8,128)(2,1)} %param.9) | copy-start | bytes 1572868
  28.7 6.5 %copy-start.2 = (bf16[1,128,2048]{2,1,0:T(8,128)(2,1)S(1)}, bf16[1,128,2048]{2,1,0:T(8,128)(2,1)}, u32[]{:S(2)}) copy-start(bf16[1,128,2048]{2,1,0:T(8,128)(2,1)} %param.10) | copy-start | bytes 1572868
  29.2 10.6 %collective-permute-start.6 = (bf16[144,1024]{1,0:T(8,128)(2,1)S(1)}, bf16[144,1024]{1,0:T(8,128)(2,1)S(1)}, u32[]{:S(2)}, u32[]{:S(2)}) collective-permute-start(bf16[144,1024]{1,0:T(8,128)(2,1)S(1)} %combine.3.refs_3_), channel_id=1, source_target_pairs={{0,7},{1,0},{2,1},{3,2},{4,3},{5,4},{6,5},{7,6},{8,15},{9,8},{10,9... | collective-permute-start | bytes 884744 | tf_op jit(solution)/shard_map/ppermute | solution.py:272
  37.0 4.7 %copy-start.4 = (bf16[1,128,2048]{2,1,0:T(8,128)(2,1)S(1)}, bf16[1,128,2048]{2,1,0:T(8,128)(2,1)}, u32[]{:S(2)}) copy-start(bf16[1,128,2048]{2,1,0:T(8,128)(2,1)} %param.8) | copy-start | bytes 1572868
  37.0 10.0 %collective-permute-start.7 = (bf16[128,1024]{1,0:T(8,128)(2,1)S(1)}, bf16[128,1024]{1,0:T(8,128)(2,1)S(1)}, u32[]{:S(2)}, u32[]{:S(2)}) collective-permute-start(bf16[128,1024]{1,0:T(8,128)(2,1)S(1)} %get-tuple-element.19.refs_5_), channel_id=1, source_target_pairs={{0,1},{1,2},{2,3},{3,4},{4,5},{5,6},{6,7},{7,0},{8,9},{9,10},{10,1... | collective-permute-start | bytes 786440 | tf_op jit(solution)/shard_map/ppermute | solution.py:272
  41.6 10.6 %collective-permute-start.8 = (bf16[128,1024]{1,0:T(8,128)(2,1)S(1)}, bf16[128,1024]{1,0:T(8,128)(2,1)S(1)}, u32[]{:S(2)}, u32[]{:S(2)}) collective-permute-start(bf16[128,1024]{1,0:T(8,128)(2,1)S(1)} %get-tuple-element.20.refs_6_), channel_id=1, source_target_pairs={{0,1},{1,2},{2,3},{3,4},{4,5},{5,6},{6,7},{7,0},{8,9},{9,10},{10,1... | collective-permute-start | bytes 786440 | tf_op jit(solution)/shard_map/ppermute | solution.py:272

commit v3 on v2

--- a/solution.py
+++ b/solution.py
@@ -9,9 +9,9 @@
 
 GROUP = 32
 CHUNKS = (8, 8)
-REPEAT = False
+BOTH = 3
 LANES = 256
-EXTRA = 16
+EXTRA = 8
 VMEM_MIB = 20
 F32 = jnp.float32
 BF16 = jnp.bfloat16
@@ -49,6 +49,8 @@
 
 def stage(parts, first, width, after=()):
     rows, n, n_after = parts[0].shape[0], len(parts), len(after)
+    cuts = 4 if rows % 64 == 0 else 1
+    height = rows // cuts
 
     def kernel(*refs):
         out = refs[n + n_after]
@@ -56,13 +58,16 @@
         def copy(semaphores):
             moves = []
             for i in range(n):
-                source = refs[i].at[:, pl.ds(first, width)]
-                moves.append(pltpu.make_async_copy(source, out.at[:, pl.ds(i * width, width)], semaphores.at[i]))
-                moves[i].start()
+                for j in range(cuts):
+                    lines = pl.ds(j * height, height)
+                    source = refs[i].at[lines, pl.ds(first, width)]
+                    target = out.at[lines, pl.ds(i * width, width)]
+                    moves.append(pltpu.make_async_copy(source, target, semaphores.at[i * cuts + j]))
+                    moves[-1].start()
             for move in moves:
                 move.wait()
 
-        pl.run_scoped(copy, pltpu.SemaphoreType.DMA((n,)))
+        pl.run_scoped(copy, pltpu.SemaphoreType.DMA((n * cuts,)))
 
     return pl.pallas_call(
         kernel,
@@ -133,7 +138,7 @@
         third = rest - second
         turn = jnp.where(pick < 3, pick, pick - 3)
         kept = jnp.where(turn == 0, first_part, jnp.where(turn == 1, second, third))
-        msg[tokens:, :] = jnp.concatenate([kept, kept], axis=0).astype(BF16)
+        msg[tokens:, :] = kept.astype(BF16)
 
     (msg,) = call(
         body, "combine", [local, *parts, attn_out, lse], [(tokens + EXTRA, width, BF16, True)], after,
@@ -156,7 +161,7 @@
     return [(slice(h * size, (h + 1) * size), slice(first + h * size, first + (h + 1) * size)) for h in range(heads)]
 
 
-def own_pair(query, key, value, msg, bias, first, heads, before=(), after=()):
+def own_pair(query, key, value, msg, bias, first, heads, extra=0, before=(), after=()):
     tokens, width = query.shape[0], msg.shape[1]
     size = width // heads
     factor = size ** -0.5
@@ -164,30 +169,28 @@
     def body(ins, outs):
         query, key, value, msg, bias = ins[:5]
         dq, dk, dv = outs
-        for cols, place in places(first, heads, size):
+        for h, (cols, place) in enumerate(places(first, heads, size)):
             q, k, v, g = query[:, place], key[:, place], value[:, place], msg[:tokens, cols]
             rows = rows_of(msg, tokens, cols)
             probs, dscores = weights_of(q, k, v, g, rows, bias[...])
             dv[:, cols] = dot(probs, g, 1, 0)
             dk[:, cols] = dot(dscores, q, 1, 0)
             total = dot(dscores, k, 0, 0)
-            if before:
+            if h >= heads - extra:
                 pairs, bias_before = ins[5:]
-                k_old, v_old = pairs[:, cols], pairs[:, slice(width + cols.start, width + cols.stop)]
+                at = (h - (heads - extra)) * size
+                k_old, v_old = pairs[:, at : at + size], pairs[:, extra * size + at : extra * size + at + size]
                 _, dscores = weights_of(q, k_old, v_old, g, rows, bias_before[...])
                 total += dot(dscores, k_old, 0, 0)
-            dq[:, cols] = (total * factor).astype(dq.dtype)
-
-    kind = BF16 if before else F32
+            dq[:, cols] = total * factor
+
     return call(
-        body, "own_pair", [query, key, value, msg, bias, *before],
-        [(tokens, width, kind, True), (tokens, width, F32, True), (tokens, width, F32, True)], after,
-    )
-
-
-def cross_pair(query, key, value, msg, bias, first, heads, after=()):
-    tokens, width = query.shape[0], msg.shape[1]
-    size = width // heads
+        body, "own_pair", [query, key, value, msg, bias, *before], [(tokens, width, F32, True)] * 3, after,
+    )
+
+
+def cross_pair(query, key, value, msg, bias, first, heads, size, after=()):
+    tokens, width = query.shape[0], heads * size
     factor = size ** -0.5
 
     def body(ins, outs):
@@ -212,16 +215,16 @@
         query, key, value, bias = ins[:4]
         dk_out, dv_out = outs
         at = 4
-        for (first, part, heads), group in zip(plan, groups):
+        for (first, part, heads, extra), group in zip(plan, groups):
             size = part // heads
             factor = size ** -0.5
-            refs = ins[at : at + len(group)]
+            msg, dk, dv = ins[at : at + 3]
+            known = ins[at + 3 : at + len(group)]
             at += len(group)
-            msg, dk, dv = refs[:3]
-            for cols, place in places(first, heads, size):
+            for h, (cols, place) in enumerate(places(first, heads, size)):
                 q, g = query[:, place], msg[:tokens, cols]
-                if len(refs) > 3:
-                    probs, dscores = refs[3][:, cols], refs[4][:, cols]
+                if h < heads - extra:
+                    probs, dscores = known[0][:, cols], known[1][:, cols]
                 else:
                     rows = rows_of(msg, tokens, cols)
                     probs, dscores = weights_of(q, key[:, place], value[:, place], g, rows, bias[...])
@@ -234,20 +237,20 @@
     )
 
 
-def query_grads(groups, plan, after=()):
-    tokens, width = groups[0][0].shape[0], sum(part for _, part, _ in plan)
+def query_grads(owns, backs, plan, after=()):
+    tokens, width = owns[0].shape[0], sum(step[1] for step in plan)
 
     def body(ins, outs):
         (out,) = outs
-        at = 0
-        for (first, part, _), group in zip(plan, groups):
-            total = ins[at][...]
-            if len(group) > 1:
-                total = (total + ins[at + 1][...].astype(F32)).astype(BF16)
-            out[:, first : first + part] = total
-            at += len(group)
-
-    (out,) = call(body, "query_grads", [a for group in groups for a in group], [(tokens, width, BF16, False)], after)
+        owns, backs = ins[: len(plan)], list(ins[len(plan) :])
+        for (first, part, heads, extra), own in zip(plan, owns):
+            sent = part - extra * (part // heads)
+            if sent:
+                out[:, first : first + sent] = (own[:, :sent] + backs.pop(0)[...].astype(F32)).astype(BF16)
+            if extra:
+                out[:, first + sent : first + part] = own[:, sent:].astype(BF16)
+
+    (out,) = call(body, "query_grads", [*owns, *backs], [(tokens, width, BF16, False)], after)
     return out
 
 
@@ -280,7 +283,7 @@
     at_cut = jnp.stack([jnp.zeros_like(core), core]).astype(jnp.int32)
     weights = [stage([out_proj], 0, width, pieces)]
     if pair == 2:
-        weights.append(lax.ppermute(out_proj, "dp", [(i, i ^ 1) for i in range(dp)]))
+        weights.append(stage([lax.ppermute(out_proj, "dp", [(i, i ^ 1) for i in range(dp)])], 0, width))
     query_sent, _ = lax.optimization_barrier((query, pieces))
     query_next = along_ctx(query_sent, -1)
 
@@ -298,51 +301,45 @@
     bias_next = bias_of(here, (here + 1) % ctx)
     bias_before = bias_of((here + ctx - 1) % ctx, here)
 
-    shares = CHUNKS if heads % sum(CHUNKS) == 0 else (1, 0)
-    counts = [share * heads // sum(shares) for share in shares]
+    shares = CHUNKS if heads == sum(CHUNKS) else (heads,)
     plan, done = [], 0
-    for count in counts:
-        if count:
-            plan.append((done * size, count * size, count))
-            done += count
+    for c, count in enumerate(shares):
+        plan.append((done * size, count * size, count, BOTH if c > 0 and c == len(shares) - 1 else 0))
+        done += count
 
     backs, held = [], []
-    for first, part, _ in plan:
+    for first, part, _, _ in plan:
         remote = project(at_cut, arrived, weights, first, part, BF16, after=held) if arrived else []
         held = list(remote[:1])
         backs.append([along_dp(remote[j - 1], -pair * j) for j in range(1, chips)])
 
+    extra = plan[-1][3]
     before = []
-    if REPEAT and len(plan) > 1:
-        first, part, _ = plan[1]
-        before = [along_ctx(stage([key, value], first, part, held), 1)]
+    if extra:
+        before = [along_ctx(stage([key, value], width - extra * size, extra * size, held), 1)]
 
     msgs, nexts = [], []
-    for c, (first, part, count) in enumerate(plan):
-        waits = [query_next] if c == 0 else before + msgs
+    for c, (first, part, count, _) in enumerate(plan):
+        waits = [query_next] if c == 0 else msgs
         (local,) = project(at_own, [upstream], weights, first, part, F32, after=waits + held)
-        msgs.append(combine(local, backs[c], output, lse, first, count))
+        msgs.append(combine(local, backs[c], output, lse, first, count, after=before if c else []))
         nexts.append(along_ctx(msgs[c], -1))
 
-    crosses = []
-    for c, (first, part, count) in enumerate(plan):
-        if not (c and before):
-            crosses.append(cross_pair(query_next, key, value, nexts[c], bias_next, first, count))
-    sent = [cross[0] for cross in crosses]
-    backs = [along_ctx(dq, 1) for dq in sent]
-    key_parts, query_parts = [], []
-    for c, (first, part, count) in enumerate(plan):
-        if c and before:
-            extra = (before[0], bias_before)
-            own = own_pair(query, key, value, msgs[c], bias_own, first, count, before=extra, after=sent)
-            key_parts.append((nexts[c], own[1], own[2]))
-            query_parts.append((own[0],))
-        else:
-            own = own_pair(query, key, value, msgs[c], bias_own, first, count, after=sent)
-            key_parts.append((nexts[c], own[1], own[2], crosses[c][1], crosses[c][2]))
-            query_parts.append((own[0], backs[c]))
+    crosses, sent, owns = [], [], []
+    for c, (first, part, count, extra) in enumerate(plan):
+        cross = ()
+        if count > extra:
+            waits = sent[-1:] + [own[0] for own in owns[-1:]]
+            cross = cross_pair(query_next, key, value, nexts[c], bias_next, first, count - extra, size, after=waits)
+            sent.append(cross[0])
+        crosses.append(cross)
+        both = (before[0], bias_before) if extra else ()
+        owns.append(own_pair(query, key, value, msgs[c], bias_own, first, count, extra, both, after=sent[-1:]))
+    returned = [along_ctx(dq, 1) for dq in sent]
+    key_parts = [(nexts[c], own[1], own[2], *crosses[c][1:]) for c, own in enumerate(owns)]
+    owns = [own[0] for own in owns]
     key_grad, value_grad = key_grads(query_next, key, value, bias_next, key_parts, plan)
-    query_grad = query_grads(query_parts, plan)
+    query_grad = query_grads(owns, returned, plan)
     shape = (1, tokens, width)
     return query_grad.reshape(shape), key_grad.reshape(shape), value_grad.reshape(shape)
 

time: 53.3 us -> 51 us (0.957)
  waiting for transfers between devices: 16.6 us -> 13.1 us
  Pallas kernels: 16.1 us -> 18.7 us
  starting transfers between devices: 17.3 us -> 15.6 us
    ppermute x5 -> x6, waiting for transfers between devices: 16.5 us -> 11.3 us  [along_ctx(): return lax.ppermute(array, 'ctx', [(i, (i + by) % ctx) for i in range(ctx)])]
    pallas_call x1 -> x3, Pallas kernels: 1.6 us -> 3.89 us  [stage(): pl.pallas_call(kernel, in_specs=[here_in(pl.ANY)] * (n + n_after), out_sp...]
    ppermute x5 -> x6, starting transfers between devices: 12 us -> 10.3 us  [along_ctx(): return lax.ppermute(array, 'ctx', [(i, (i + by) % ctx) for i in range(ctx)])]
    ppermute x3, waiting for transfers between devices: 0.12 us -> 1.84 us  [along_dp(): return lax.ppermute(array, 'dp', [(i, (i + by) % dp) for i in range(dp)])]
  transfers between devices with their start and end apart: 9 -> 10, of which waited for: 6 -> 5; matrix products, arithmetic and copies ran while one was open for 4% -> 5% of each run, Pallas kernels for 29% -> 35%
where the time goes in v3:
time: 51 us; the launch traced here: 50.7 us
  Pallas kernels  18.7 us (37%)
  starting transfers between devices  15.6 us (31%)
  waiting for transfers between devices  13.1 us (26%)
  local copies, waits for them, and re-layouts  1.25 us (2%)
  other arithmetic  1.23 us (2%)
  between operations  0.8 us (2%)
    pallas_call x12, Pallas kernels, call(): pl.pallas_call(kernel, in_specs=[here_in(pltpu.SMEM)] * len(scalars) + [h...  14.8 us
    ppermute x6, waiting for transfers between devices, along_ctx(): return lax.ppermute(array, 'ctx', [(i, (i + by) % ctx) for i in range(ctx)])  11.3 us
    ppermute x6, starting transfers between devices, along_ctx(): return lax.ppermute(array, 'ctx', [(i, (i + by) % ctx) for i in range(ctx)])  10.3 us
    ppermute x3, starting transfers between devices, along_dp(): return lax.ppermute(array, 'dp', [(i, (i + by) % dp) for i in range(dp)])  4.77 us
    pallas_call x3, Pallas kernels, stage(): pl.pallas_call(kernel, in_specs=[here_in(pl.ANY)] * (n + n_after), out_sp...  3.89 us
    ppermute x3, waiting for transfers between devices, along_dp(): return lax.ppermute(array, 'dp', [(i, (i + by) % dp) for i in range(dp)])  1.84 us
  transfers between devices with their start and end apart: 10, of which 5 were waited for; matrix products, arithmetic and copies ran while one was open for 5% of the time, Pallas kernels for 35%

profile of v3, /device:TPU:0, one launch (start us, length us, event | category | flops | bytes accessed | tf_op | source)
XLA Modules:
  0.0 50.7 jit_solution(8981950184979797281)
XLA Ops:
  1.1 1.0 %dynamic-slice_bitcast_fusion.refs_1_ = bf16[128,1024]{1,0:T(8,128)(2,1)S(1)} fusion(bf16[1,128,2048]{2,1,0:T(8,128)(2,1)} %param.11, s32[]{:T(128)S(6)} %select_n.51), kind=kLoop, calls=%fused_computation | loop fusion | bytes 524292 | tf_op jit(solution)/shard_map/dynamic_slice | solution.py:278
  2.1 2.6 %collective-permute-start.2 = (bf16[128,1024]{1,0:T(8,128)(2,1)S(1)}, bf16[128,1024]{1,0:T(8,128)(2,1)S(1)}, u32[]{:S(2)}, u32[]{:S(2)}) collective-permute-start(bf16[128,1024]{1,0:T(8,128)(2,1)S(1)} %dynamic-slice_bitcast_fusion.refs_1_), channel_id=1, source_target_pairs={{0,16},{8,24},{16,0},{24,8},{1,17},{9,25},{17,1},{25,9},{2,18},{10... | collective-permute-start | bytes 786440 | tf_op jit(solution)/shard_map/ppermute | solution.py:272
  4.7 4.6 %collective-permute-start.1 = (bf16[128,2048]{1,0:T(8,128)(2,1)}, bf16[128,2048]{1,0:T(8,128)(2,1)S(1)}, u32[]{:S(2)}, u32[]{:S(2)}) collective-permute-start(bf16[128,2048]{1,0:T(8,128)(2,1)} %bitcast.35), channel_id=1, source_target_pairs={{0,7},{1,0},{2,1},{3,2},{4,3},{5,4},{6,5},{7,6},{8,15},{9,8},{10,9... | collective-permute-start | bytes 1572872 | tf_op jit(solution)/shard_map/ppermute | solution.py:275
  9.4 0.8 %fusion.5 = (s32[4]{0:T(128)S(1)}, s32[4]{0:T(128)S(1)}, s32[4]{0:T(128)S(1)}) fusion(s32[1,32]{1,0:T(1,128)} %param.15, s32[]{:T(128)S(6)} %select_n.58, s32[]{:T(128)S(6)} %select_n.52, s32[]{:T(128)S(6)} %select_n.55), kind=kLoop, calls=%fused_computation.15 | loop fusion | flops 12 | bytes 108 | tf_op jit(solution)/shard_map/mul | solution.py:294
  10.3 1.5 %stage.3.refs_2_ = bf16[512,2048]{1,0:T(8,128)(2,1)S(1)} custom-call(bf16[512,2048]{1,0:T(8,128)(2,1)} %refs_0_.1, bf16[128,1024]{1,0:T(8,128)(2,1)S(1)} %dynamic-slice_bitcast_fusion.refs_1_), custom_call_target="tpu_custom_call" | custom-call | flops 1000000000 | bytes 4194304 | tf_op jit(solution)/shard_map/stage/pallas_call | solution.py:72
  12.2 1.5 %stage.4.refs_3_ = bf16[512,2048]{1,0:T(8,128)(2,1)S(1)} custom-call(bf16[512,2048]{1,0:T(8,128)(2,1)} %collective-permute-done.refs_0_), custom_call_target="tpu_custom_call" | custom-call | flops 1000000000 | bytes 4194304 | tf_op jit(solution)/shard_map/stage/pallas_call | solution.py:72
  13.7 1.0 %project.4.refs_4_ = bf16[128,1024]{1,0:T(8,128)(2,1)S(1)} custom-call(s32[2]{0:T(128)S(1)} %pad_add_fusion.1.refs_0_, bf16[128,1024]{1,0:T(8,128)(2,1)S(1)} %collective-permute-done.2.refs_1_, bf16[512,2048]{1,0:T(8,128)(2,1)S(1)} %stage.3.refs_2_, bf16[512,2048]{1,0:T(8,128)(2,1)S(1)} %stage.4.refs_3_), custom_call_target="tpu_custom_call" | custom-call | flops 1000000000 | bytes 4718592 | tf_op jit(solution)/shard_map/project/pallas_call | solution.py:39
  15.3 1.0 %project.5.refs_5_.refs_2_ = bf16[128,1024]{1,0:T(8,128)(2,1)S(1)} custom-call(s32[2]{0:T(128)S(1)} %pad_add_fusion.1.refs_0_, bf16[128,1024]{1,0:T(8,128)(2,1)S(1)} %collective-permute-done.2.refs_1_, bf16[512,2048]{1,0:T(8,128)(2,1)S(1)} %stage.3.refs_2_, bf16[512,2048]{1,0:T(8,128)(2,1)S(1)} %stage.4.refs_3_, bf16[128,1024]{1,0:T(8,128)(2,1)S(1)} %project.4.refs_4_), custom_call_target="tpu_custom_call" | custom-call | flops 1000000000 | bytes 4718592 | tf_op jit(solution)/shard_map/project/pallas_call | solution.py:39
  16.3 1.6 %collective-permute-start.5 = (bf16[128,1024]{1,0:T(8,128)(2,1)S(1)}, bf16[128,1024]{1,0:T(8,128)(2,1)S(1)}, u32[]{:S(2)}, u32[]{:S(2)}) collective-permute-start(bf16[128,1024]{1,0:T(8,128)(2,1)S(1)} %project.5.refs_5_.refs_2_), channel_id=1, source_target_pairs={{0,16},{8,24},{16,0},{24,8},{1,17},{9,25},{17,1},{25,9},{2,18},{10... | collective-permute-start | bytes 786440 | tf_op jit(solution)/shard_map/ppermute | solution.py:272
  17.9 0.9 %stage.5 = bf16[128,768]{1,0:T(8,128)(2,1)S(1)} custom-call(bf16[128,2048]{1,0:T(8,128)(2,1)} %bitcast.21, bf16[128,2048]{1,0:T(8,128)(2,1)} %bitcast.27, bf16[128,1024]{1,0:T(8,128)(2,1)S(1)} %project.5.refs_5_.refs_2_), custom_call_target="tpu_custom_call" | custom-call | flops 1000000000 | bytes 393216 | tf_op jit(solution)/shard_map/stage/pallas_call | solution.py:72
  18.7 2.4 %collective-permute-done.1.refs_4_.refs_0_ = bf16[128,2048]{1,0:T(8,128)(2,1)S(1)} collective-permute-done((bf16[128,2048]{1,0:T(8,128)(2,1)}, bf16[128,2048]{1,0:T(8,128)(2,1)S(1)}, u32[]{:S(2)}, u32[]{:S(2)}) %collective-permute-start.1) | collective-permute-done | bytes 524320 | tf_op jit(solution)/shard_map/ppermute | solution.py:275
  21.1 1.0 %project.6.refs_0_ = f32[128,1024]{1,0:T(8,128)S(1)} custom-call(s32[2]{0:T(128)S(1)} %pad_add_fusion.refs_0_, bf16[128,2048]{1,0:T(8,128)(2,1)S(1)} %bitcast.19, bf16[512,2048]{1,0:T(8,128)(2,1)S(1)} %stage.3.refs_2_, bf16[512,2048]{1,0:T(8,128)(2,1)S(1)} %stage.4.refs_3_, bf16[128,2048]{1,0:T(8,128)(2,1)S(1)} %collective-permute-done.1.refs_4_.refs_0_, ...), custom_call_target="tpu_custom_call" | custom-call | flops 1000000000 | bytes 5242880 | tf_op jit(solution)/shard_map/project/pallas_call | solution.py:39
  22.1 1.8 %collective-permute-done.3.refs_1_ = bf16[128,1024]{1,0:T(8,128)(2,1)S(1)} collective-permute-done((bf16[128,1024]{1,0:T(8,128)(2,1)S(1)}, bf16[128,1024]{1,0:T(8,128)(2,1)S(1)}, u32[]{:S(2)}, u32[]{:S(2)}) %collective-permute-start.3) | collective-permute-done | bytes 262176 | tf_op jit(solution)/shard_map/ppermute | solution.py:272
  24.4 3.4 %collective-permute-start.4 = (bf16[136,1024]{1,0:T(8,128)(2,1)S(1)}, bf16[136,1024]{1,0:T(8,128)(2,1)S(1)}, u32[]{:S(2)}, u32[]{:S(2)}) collective-permute-start(bf16[136,1024]{1,0:T(8,128)(2,1)S(1)} %combine.2.refs_3_.refs_4_), channel_id=1, source_target_pairs={{0,7},{1,0},{2,1},{3,2},{4,3},{5,4},{6,5},{7,6},{8,15},{9,8},{10,9... | collective-permute-start | bytes 835592 | tf_op jit(solution)/shard_map/ppermute | solution.py:275
  27.8 1.0 %project.7.refs_0_ = f32[128,1024]{1,0:T(8,128)S(1)} custom-call(s32[2]{0:T(128)S(1)} %pad_add_fusion.refs_0_, bf16[128,2048]{1,0:T(8,128)(2,1)S(1)} %bitcast.20, bf16[512,2048]{1,0:T(8,128)(2,1)S(1)} %stage.3.refs_2_, bf16[512,2048]{1,0:T(8,128)(2,1)S(1)} %stage.4.refs_3_, bf16[136,1024]{1,0:T(8,128)(2,1)S(1)} %combine.2.refs_3_.refs_4_, ...), custom_call_target="tpu_custom_call" | custom-call | flops 1000000000 | bytes 5242880 | tf_op jit(solution)/shard_map/project/pallas_call | solution.py:39
  29.3 2.2 %collective-permute-start.7 = (bf16[136,1024]{1,0:T(8,128)(2,1)S(1)}, bf16[136,1024]{1,0:T(8,128)(2,1)S(1)}, u32[]{:S(2)}, u32[]{:S(2)}) collective-permute-start(bf16[136,1024]{1,0:T(8,128)(2,1)S(1)} %combine.3.refs_3_), channel_id=1, source_target_pairs={{0,7},{1,0},{2,1},{3,2},{4,3},{5,4},{6,5},{7,6},{8,15},{9,8},{10,9... | collective-permute-start | bytes 835592 | tf_op jit(solution)/shard_map/ppermute | solution.py:275
  31.6 3.3 %collective-permute-done.4.refs_3_.refs_4_ = bf16[136,1024]{1,0:T(8,128)(2,1)S(1)} collective-permute-done((bf16[136,1024]{1,0:T(8,128)(2,1)S(1)}, bf16[136,1024]{1,0:T(8,128)(2,1)S(1)}, u32[]{:S(2)}, u32[]{:S(2)}) %collective-permute-start.4) | collective-permute-done | bytes 278560 | tf_op jit(solution)/shard_map/ppermute | solution.py:275
  34.9 1.8 %cross_pair.2 = (bf16[128,1024]{1,0:T(8,128)(2,1)S(1)}, bf16[128,1024]{1,0:T(8,128)(2,1)S(1)}, bf16[128,1024]{1,0:T(8,128)(2,1)S(1)}) custom-call(bf16[128,2048]{1,0:T(8,128)(2,1)S(1)} %collective-permute-done.1.refs_4_.refs_0_, bf16[128,2048]{1,0:T(8,128)(2,1)S(1)} %bitcast.22, bf16[128,2048]{1,0:T(8,128)(2,1)S(1)} %bitcast.28, ...), custom_call_target="tpu_custom_call" | custom-call | flops 1000000000 | bytes 2703360 | tf_op jit(solution)/shard_map/cross_pair/pallas_call | solution.py:39
  36.8 1.8 %own_pair.2 = (f32[128,1024]{1,0:T(8,128)S(1)}, f32[128,1024]{1,0:T(8,128)S(1)}, f32[128,1024]{1,0:T(8,128)S(1)}) custom-call(bf16[128,2048]{1,0:T(8,128)(2,1)S(1)} %bitcast.36, bf16[128,2048]{1,0:T(8,128)(2,1)S(1)} %bitcast.23, bf16[128,2048]{1,0:T(8,128)(2,1)S(1)} %bitcast.29, bf16[136,1024]{1,0:T(8,128)(2,1)S(1)} %combine.2.refs_3_.refs_4_, ...), custom_call_target="tpu_custom_call" | custom-call | flops 1000000000 | bytes 3489792 | tf_op jit(solution)/shard_map/own_pair/pallas_call | solution.py:39
  39.5 1.2 %cross_pair.3 = (bf16[128,640]{1,0:T(8,128)(2,1)S(1)}, bf16[128,640]{1,0:T(8,128)(2,1)S(1)}, bf16[128,640]{1,0:T(8,128)(2,1)S(1)}) custom-call(bf16[128,2048]{1,0:T(8,128)(2,1)S(1)} %collective-permute-done.1.refs_4_.refs_0_, bf16[128,2048]{1,0:T(8,128)(2,1)S(1)} %bitcast.24, bf16[128,2048]{1,0:T(8,128)(2,1)S(1)} %bitcast.30, ...), custom_call_target="tpu_custom_call" | custom-call | flops 1000000000 | bytes 2408448 | tf_op jit(solution)/shard_map/cross_pair/pallas_call | solution.py:39
  40.8 2.4 %own_pair.3 = (f32[128,1024]{1,0:T(8,128)S(1)}, f32[128,1024]{1,0:T(8,128)S(1)}, f32[128,1024]{1,0:T(8,128)S(1)}) custom-call(bf16[128,2048]{1,0:T(8,128)(2,1)S(1)} %bitcast.37, bf16[128,2048]{1,0:T(8,128)(2,1)S(1)} %bitcast.25, bf16[128,2048]{1,0:T(8,128)(2,1)S(1)} %bitcast.31, bf16[136,1024]{1,0:T(8,128)(2,1)S(1)} %combine.3.refs_3_, ...), custom_call_target="tpu_custom_call" | custom-call | flops 1000000000 | bytes 3751936 | tf_op jit(solution)/shard_map/own_pair/pallas_call | solution.py:39
  43.1 2.0 %key_grads.1 = (bf16[128,2048]{1,0:T(8,128)(2,1)}, bf16[128,2048]{1,0:T(8,128)(2,1)}) custom-call(bf16[128,2048]{1,0:T(8,128)(2,1)S(1)} %collective-permute-done.1.refs_4_.refs_0_, bf16[128,2048]{1,0:T(8,128)(2,1)S(1)} %bitcast.26, bf16[128,2048]{1,0:T(8,128)(2,1)S(1)} %bitcast.32, f32[128,128]{1,0:T(8,128)S(1)} %get-tuple-element.35.refs_4_.refs_3_, ...), custom_call_target="tpu_custom_call" | custom-call | flops 1000000000 | bytes 6193152 | tf_op jit(solution)/shard_map/key_grads/pallas_call | solution.py:39
  45.1 4.8 %collective-permute-done.9.refs_3_ = bf16[128,640]{1,0:T(8,128)(2,1)S(1)} collective-permute-done((bf16[128,640]{1,0:T(8,128)(2,1)S(1)}, bf16[128,640]{1,0:T(8,128)(2,1)S(1)}, u32[]{:S(2)}, u32[]{:S(2)}) %collective-permute-start.9) | collective-permute-done | bytes 163872 | tf_op jit(solution)/shard_map/ppermute | solution.py:275
  49.9 0.9 %query_grads.1 = bf16[128,2048]{1,0:T(8,128)(2,1)} custom-call(f32[128,1024]{1,0:T(8,128)S(1)} %get-tuple-element.20.refs_6_.refs_0_, f32[128,1024]{1,0:T(8,128)S(1)} %get-tuple-element.22.refs_1_, bf16[128,1024]{1,0:T(8,128)(2,1)S(1)} %collective-permute-done.8.refs_2_, bf16[128,640]{1,0:T(8,128)(2,1)S(1)} %collective-permute-done.9.refs_3_), custom_call_target="tpu_custom_call" | custom-call | flops 1000000000 | bytes 1998848 | tf_op jit(solution)/shard_map/query_grads/pallas_call | solution.py:39
  (33 shorter events, 3.5 us)
Async XLA Ops:
  0.6 11.6 %collective-permute-start = (bf16[512,2048]{1,0:T(8,128)(2,1)}, bf16[512,2048]{1,0:T(8,128)(2,1)}, u32[]{:S(2)}, u32[]{:S(2)}) collective-permute-start(bf16[512,2048]{1,0:T(8,128)(2,1)} %refs_0_.1), channel_id=1, source_target_pairs={{0,8},{8,0},{16,24},{24,16},{1,9},{9,1},{17,25},{25,17},{2,10},{10... | collective-permute-start | bytes 6291464 | tf_op jit(solution)/shard_map/ppermute | solution.py:286
  2.1 11.6 %collective-permute-start.2 = (bf16[128,1024]{1,0:T(8,128)(2,1)S(1)}, bf16[128,1024]{1,0:T(8,128)(2,1)S(1)}, u32[]{:S(2)}, u32[]{:S(2)}) collective-permute-start(bf16[128,1024]{1,0:T(8,128)(2,1)S(1)} %dynamic-slice_bitcast_fusion.refs_1_), channel_id=1, source_target_pairs={{0,16},{8,24},{16,0},{24,8},{1,17},{9,25},{17,1},{25,9},{2,18},{10... | collective-permute-start | bytes 786440 | tf_op jit(solution)/shard_map/ppermute | solution.py:272
  4.7 16.4 %collective-permute-start.1 = (bf16[128,2048]{1,0:T(8,128)(2,1)}, bf16[128,2048]{1,0:T(8,128)(2,1)S(1)}, u32[]{:S(2)}, u32[]{:S(2)}) collective-permute-start(bf16[128,2048]{1,0:T(8,128)(2,1)} %bitcast.35), channel_id=1, source_target_pairs={{0,7},{1,0},{2,1},{3,2},{4,3},{5,4},{6,5},{7,6},{8,15},{9,8},{10,9... | collective-permute-start | bytes 1572872 | tf_op jit(solution)/shard_map/ppermute | solution.py:275
  14.7 9.3 %collective-permute-start.3 = (bf16[128,1024]{1,0:T(8,128)(2,1)S(1)}, bf16[128,1024]{1,0:T(8,128)(2,1)S(1)}, u32[]{:S(2)}, u32[]{:S(2)}) collective-permute-start(bf16[128,1024]{1,0:T(8,128)(2,1)S(1)} %project.4.refs_4_), channel_id=1, source_target_pairs={{0,16},{8,24},{16,0},{24,8},{1,17},{9,25},{17,1},{25,9},{2,18},{10... | collective-permute-start | bytes 786440 | tf_op jit(solution)/shard_map/ppermute | solution.py:272
  16.3 4.8 %copy-start = (bf16[1,128,2048]{2,1,0:T(8,128)(2,1)S(1)}, bf16[1,128,2048]{2,1,0:T(8,128)(2,1)}, u32[]{:S(2)}) copy-start(bf16[1,128,2048]{2,1,0:T(8,128)(2,1)} %param.11) | copy-start | bytes 1572868
  16.3 12.5 %collective-permute-start.5 = (bf16[128,1024]{1,0:T(8,128)(2,1)S(1)}, bf16[128,1024]{1,0:T(8,128)(2,1)S(1)}, u32[]{:S(2)}, u32[]{:S(2)}) collective-permute-start(bf16[128,1024]{1,0:T(8,128)(2,1)S(1)} %project.5.refs_5_.refs_2_), channel_id=1, source_target_pairs={{0,16},{8,24},{16,0},{24,8},{1,17},{9,25},{17,1},{25,9},{2,18},{10... | collective-permute-start | bytes 786440 | tf_op jit(solution)/shard_map/ppermute | solution.py:272
  18.7 10.1 %collective-permute-start.6 = (bf16[128,768]{1,0:T(8,128)(2,1)S(1)}, bf16[128,768]{1,0:T(8,128)(2,1)S(1)}, u32[]{:S(2)}, u32[]{:S(2)}) collective-permute-start(bf16[128,768]{1,0:T(8,128)(2,1)S(1)} %stage.5), channel_id=1, source_target_pairs={{0,1},{1,2},{2,3},{3,4},{4,5},{5,6},{6,7},{7,0},{8,9},{9,10},{10,1... | collective-permute-start | bytes 589832 | tf_op jit(solution)/shard_map/ppermute | solution.py:275
  21.1 2.8 %copy-start.3 = (bf16[1,128,2048]{2,1,0:T(8,128)(2,1)S(1)}, bf16[1,128,2048]{2,1,0:T(8,128)(2,1)}, u32[]{:S(2)}) copy-start(bf16[1,128,2048]{2,1,0:T(8,128)(2,1)} %param.13) | copy-start | bytes 1572868
  21.1 2.8 %copy-start.5 = (f32[1,16,128]{2,1,0:T(8,128)S(1)}, f32[1,16,128]{2,1,0:T(8,128)}, u32[]{:S(2)}) copy-start(f32[1,16,128]{2,1,0:T(8,128)} %param.14) | copy-start | bytes 24580
  24.4 10.5 %collective-permute-start.4 = (bf16[136,1024]{1,0:T(8,128)(2,1)S(1)}, bf16[136,1024]{1,0:T(8,128)(2,1)S(1)}, u32[]{:S(2)}, u32[]{:S(2)}) collective-permute-start(bf16[136,1024]{1,0:T(8,128)(2,1)S(1)} %combine.2.refs_3_.refs_4_), channel_id=1, source_target_pairs={{0,7},{1,0},{2,1},{3,2},{4,3},{5,4},{6,5},{7,6},{8,15},{9,8},{10,9... | collective-permute-start | bytes 835592 | tf_op jit(solution)/shard_map/ppermute | solution.py:275
  28.8 6.1 %copy-start.1 = (bf16[1,128,2048]{2,1,0:T(8,128)(2,1)S(1)}, bf16[1,128,2048]{2,1,0:T(8,128)(2,1)}, u32[]{:S(2)}) copy-start(bf16[1,128,2048]{2,1,0:T(8,128)(2,1)} %param.9) | copy-start | bytes 1572868
  28.8 6.1 %copy-start.2 = (bf16[1,128,2048]{2,1,0:T(8,128)(2,1)S(1)}, bf16[1,128,2048]{2,1,0:T(8,128)(2,1)}, u32[]{:S(2)}) copy-start(bf16[1,128,2048]{2,1,0:T(8,128)(2,1)} %param.10) | copy-start | bytes 1572868
  29.3 7.6 %copy-start.4 = (bf16[1,128,2048]{2,1,0:T(8,128)(2,1)S(1)}, bf16[1,128,2048]{2,1,0:T(8,128)(2,1)}, u32[]{:S(2)}) copy-start(bf16[1,128,2048]{2,1,0:T(8,128)(2,1)} %param.8) | copy-start | bytes 1572868
  29.3 10.2 %collective-permute-start.7 = (bf16[136,1024]{1,0:T(8,128)(2,1)S(1)}, bf16[136,1024]{1,0:T(8,128)(2,1)S(1)}, u32[]{:S(2)}, u32[]{:S(2)}) collective-permute-start(bf16[136,1024]{1,0:T(8,128)(2,1)S(1)} %combine.3.refs_3_), channel_id=1, source_target_pairs={{0,7},{1,0},{2,1},{3,2},{4,3},{5,4},{6,5},{7,6},{8,15},{9,8},{10,9... | collective-permute-start | bytes 835592 | tf_op jit(solution)/shard_map/ppermute | solution.py:275
  36.8 13.1 %collective-permute-start.8 = (bf16[128,1024]{1,0:T(8,128)(2,1)S(1)}, bf16[128,1024]{1,0:T(8,128)(2,1)S(1)}, u32[]{:S(2)}, u32[]{:S(2)}) collective-permute-start(bf16[128,1024]{1,0:T(8,128)(2,1)S(1)} %get-tuple-element.19.refs_5_), channel_id=1, source_target_pairs={{0,1},{1,2},{2,3},{3,4},{4,5},{5,6},{6,7},{7,0},{8,9},{9,10},{10,1... | collective-permute-start | bytes 786440 | tf_op jit(solution)/shard_map/ppermute | solution.py:275
  40.7 9.2 %collective-permute-start.9 = (bf16[128,640]{1,0:T(8,128)(2,1)S(1)}, bf16[128,640]{1,0:T(8,128)(2,1)S(1)}, u32[]{:S(2)}, u32[]{:S(2)}) collective-permute-start(bf16[128,640]{1,0:T(8,128)(2,1)S(1)} %get-tuple-element.21.refs_7_), channel_id=1, source_target_pairs={{0,1},{1,2},{2,3},{3,4},{4,5},{5,6},{6,7},{7,0},{8,9},{9,10},{10,1... | collective-permute-start | bytes 491528 | tf_op jit(solution)/shard_map/ppermute | solution.py:275

commit v4 on v3

v4 whole, which is shorter than its diff:
```python
import functools

import jax
import jax.numpy as jnp
from jax import lax
from jax.experimental import pallas as pl
from jax.experimental.pallas import tpu as pltpu
from jax.sharding import PartitionSpec as P

GROUP = 32
CHUNKS = ((8,), (5, 3))
BOTH = 3
LANES = 256
EARLY = False
EXTRA = 8
VMEM_MIB = 20
F32 = jnp.float32
BF16 = jnp.bfloat16


def dot(a, b, ca, cb):
    return lax.dot_general(a, b, (((ca,), (cb,)), ((), ())), preferred_element_type=F32)


def here_in(space):
    return pl.BlockSpec(memory_space=space)


def pin(array):
    return pltpu.with_memory_space_constraint(array, pltpu.VMEM)


def call(body, name, ins, outs, after=(), scalars=(), free=()):
    n_in, n_after = len(scalars) + len(ins), len(after)

    def kernel(*refs):
        body(refs[:n_in], refs[n_in + n_after :])

    moved = sum(a.size * a.dtype.itemsize for a in ins) + sum(jnp.dtype(t).itemsize * r * c for r, c, t, _ in outs)
    return pl.pallas_call(
        kernel,
        in_specs=[here_in(pltpu.SMEM)] * len(scalars) + [here_in(pltpu.VMEM)] * len(ins) + [here_in(pl.ANY)] * n_after,
        out_specs=[here_in(pltpu.VMEM)] * len(outs),
        out_shape=[pltpu.VMEM((r, c), t) if kept else jax.ShapeDtypeStruct((r, c), t) for r, c, t, kept in outs],
        compiler_params=pltpu.CompilerParams(vmem_limit_bytes=VMEM_MIB * 1024 * 1024),
        cost_estimate=pl.CostEstimate(flops=int(1e9), bytes_accessed=int(1 * moved), transcendentals=0),
        name=name,
    )(*scalars, *[a if i in free else pin(a) for i, a in enumerate(ins)], *after)


def stage(parts, first, width, after=()):
    rows, n, n_after = parts[0].shape[0], len(parts), len(after)
    cuts = 4 if rows % 64 == 0 else 1
    height = rows // cuts

    def kernel(*refs):
        out = refs[n + n_after]

        def copy(semaphores):
            moves = []
            for i in range(n):
                for j in range(cuts):
                    lines = pl.ds(j * height, height)
                    source = refs[i].at[lines, pl.ds(first, width)]
                    target = out.at[lines, pl.ds(i * width, width)]
                    moves.append(pltpu.make_async_copy(source, target, semaphores.at[i * cuts + j]))
                    moves[-1].start()
            for move in moves:
                move.wait()

        pl.run_scoped(copy, pltpu.SemaphoreType.DMA((n * cuts,)))

    return pl.pallas_call(
        kernel,
        in_specs=[here_in(pl.ANY)] * (n + n_after),
        out_specs=here_in(pltpu.VMEM),
        out_shape=pltpu.VMEM((rows, n * width), parts[0].dtype),
        compiler_params=pltpu.CompilerParams(vmem_limit_bytes=VMEM_MIB * 1024 * 1024),
        cost_estimate=pl.CostEstimate(flops=int(1e9), bytes_accessed=4 * rows * n * width, transcendentals=0),
        name="stage",
    )(*[pltpu.with_memory_space_constraint(a, pltpu.HBM) for a in parts], *after)


def project(place, sources, weights, first, width, kind, after=()):
    pair = len(weights)
    tokens = sources[0].shape[0]
    rows = weights[0].shape[0]

    def body(ins, outs):
        place, sources, weights = ins[0], ins[1 : 1 + len(sources_in)], ins[1 + len(sources_in) :]
        lhs = []
        for i in range(pair):
            start = (place[0] * pair + (place[1] + i) % pair) * rows
            part = pl.ds(pl.multiple_of(start, rows), rows)
            blocks = [ref[:, part] for ref in sources]
            lhs.append(blocks[0] if len(blocks) == 1 else jnp.concatenate(blocks, axis=0))
        for at in range(0, width, LANES):
            cols = slice(at, at + LANES)
            from_cols = slice(first + at, first + at + LANES)
            total = dot(lhs[0], weights[0][:, from_cols], 1, 0)
            for i in range(1, pair):
                total += dot(lhs[i], weights[i][:, from_cols], 1, 0)
            for j, ref in enumerate(outs):
                ref[:, cols] = total[j * tokens : (j + 1) * tokens].astype(kind)

    sources_in = list(sources)
    return call(
        body, "project", [*sources, *weights], [(tokens, width, kind, True)] * len(sources), after, (place,), (len(sources), len(sources) + 1),
    )


def combine(local, parts, attn_out, lse, first, cuts, size, after=()):
    tokens, width = local.shape
    head0 = first // size

    def body(ins, outs):
        local, parts, attn_out, lse = ins[0], ins[1:-2], ins[-2], ins[-1]
        done = 0
        for msg, heads in zip(outs, cuts):
            here = slice(done * size, (done + heads) * size)
            place = slice(first + here.start, first + here.stop)
            total = local[:, here]
            for ref in parts:
                total += ref[:, here].astype(F32)
            grad = total.astype(BF16)
            msg[:tokens, :] = grad
            product = grad.astype(F32) * attn_out[:, place].astype(F32)
            high = product.astype(BF16)
            low = (product - high.astype(F32)).astype(BF16)
            ones = jnp.ones((8, size), BF16)
            rows, lses = [], []
            for h in range(heads):
                cols = slice(h * size, (h + 1) * size)
                line = slice(head0 + done + h, head0 + done + h + 1)
                rows.append(dot(ones, high[:, cols], 1, 1) + dot(ones, low[:, cols], 1, 1))
                lses.append(jnp.broadcast_to(lse[line, :], (8, tokens)))
            pick = lax.broadcasted_iota(jnp.int32, (8, heads * size), 0)
            both = jnp.where(pick < 3, jnp.concatenate(rows, axis=1), jnp.concatenate(lses, axis=1))
            first_part = both.astype(BF16).astype(F32)
            rest = both - first_part
            second = rest.astype(BF16).astype(F32)
            third = rest - second
            turn = jnp.where(pick < 3, pick, pick - 3)
            kept = jnp.where(turn == 0, first_part, jnp.where(turn == 1, second, third))
            msg[tokens:, :] = kept.astype(BF16)
            done += heads

    return call(
        body, "combine", [local, *parts, attn_out, lse],
        [(tokens + EXTRA, heads * size, BF16, True) for heads in cuts], after,
    )


def rows_of(msg, tokens, cols):
    tail = msg[tokens:, cols].astype(F32)
    return tail[0:1] + tail[1:2] + tail[2:3], tail[3:4] + tail[4:5] + tail[5:6]


def bias_of(order, key_block, query_block, tokens):
    def position(block, axis):
        at = lax.broadcasted_iota(jnp.int32, (tokens, tokens), axis)
        count = tokens // GROUP
        base = jnp.full((tokens, tokens), order[block * count] * GROUP, jnp.int32)
        for g in range(1, count):
            base = jnp.where(at >= g * GROUP, (order[block * count + g] - g) * GROUP, base)
        return base + at

    return jnp.where(position(key_block, 0) <= position(query_block, 1), 0.0, -jnp.inf).astype(F32)


def masks(scalars, tokens, after=()):
    def body(ins, outs):
        order, spots = ins
        for out, (key_block, query_block) in zip(outs, ((0, 0), (0, 1), (2, 0))):
            out[...] = bias_of(order, spots[key_block], spots[query_block], tokens)

    return call(body, "masks", [], [(tokens, tokens, F32, True)] * 3, after, scalars)


def weights_of(q, k, v, g, rows, bias):
    delta, lse = rows
    probs = jnp.exp(dot(k, q, 1, 1) * (q.shape[1] ** -0.5) - lse + bias)
    return probs.astype(BF16), (probs * (dot(v, g, 1, 1) - delta)).astype(BF16)


def places(first, heads, size):
    return [(slice(h * size, (h + 1) * size), slice(first + h * size, first + (h + 1) * size)) for h in range(heads)]


def own_pair(query, key, value, bias, msgs, first, size, extra=0, before=(), after=()):
    tokens = query.shape[0]
    width = sum(msg.shape[1] for msg in msgs)
    factor = size ** -0.5

    def body(ins, outs):
        query, key, value, bias = ins[:4]
        msgs_in, pairs = ins[4 : 4 + len(msgs)], ins[4 + len(msgs) :]
        dq, dk, dv = outs
        done = 0
        for msg in msgs_in:
            for cols, _ in places(0, msg.shape[1] // size, size):
                here = slice(done, done + size)
                place = slice(first + done, first + done + size)
                q, k, v, g = query[:, place], key[:, place], value[:, place], msg[:tokens, cols]
                rows = rows_of(msg, tokens, cols)
                probs, dscores = weights_of(q, k, v, g, rows, bias[...])
                dv[:, here] = dot(probs, g, 1, 0)
                dk[:, here] = dot(dscores, q, 1, 0)
                total = dot(dscores, k, 0, 0)
                at = done - (width - extra * size)
                if at >= 0:
                    k_old = pairs[0][:, at : at + size]
                    v_old = pairs[0][:, extra * size + at : extra * size + at + size]
                    _, dscores = weights_of(q, k_old, v_old, g, rows, pairs[1][...])
                    total += dot(dscores, k_old, 0, 0)
                dq[:, here] = total * factor
                done += size

    return call(
        body, "own_pair", [query, key, value, bias, *msgs, *before], [(tokens, width, F32, True)] * 3, after,
    )


def cross_pair(query, key, value, bias, msg, first, heads, size, after=()):
    tokens, width = query.shape[0], heads * size
    factor = size ** -0.5

    def body(ins, outs):
        query, key, value, bias, msg = ins
        dq, probs_out, dscores_out = outs
        for cols, place in places(first, heads, size):
            q, k, v, g = query[:, place], key[:, place], value[:, place], msg[:tokens, cols]
            probs, dscores = weights_of(q, k, v, g, rows_of(msg, tokens, cols), bias[...])
            probs_out[:, cols] = probs
            dscores_out[:, cols] = dscores
            dq[:, cols] = (dot(dscores, k, 0, 0) * factor).astype(BF16)

    return call(
        body, "cross_pair", [query, key, value, bias, msg], [(tokens, width, BF16, True)] * 3, after,
    )


def key_grads(query, key, value, bias, nexts, owns, knowns, plan, after=()):
    tokens, width = query.shape

    def body(ins, outs):
        query, key, value, bias = ins[:4]
        refs = list(ins[4:])
        dk_out, dv_out = outs
        msgs = [refs.pop(0) for _ in nexts]
        sums = [[refs.pop(0) for _ in own] for own in owns]
        pairs = [[refs.pop(0) for _ in known] for known in knowns]
        for (first, part, heads, extra, step, offset), msg, known in zip(plan, msgs, pairs):
            size = part // heads
            factor = size ** -0.5
            dk, dv = sums[step]
            for h, (cols, place) in enumerate(places(first, heads, size)):
                here = slice(offset + cols.start, offset + cols.stop)
                q, g = query[:, place], msg[:tokens, cols]
                if h < heads - extra:
                    probs, dscores = known[0][:, cols], known[1][:, cols]
                else:
                    rows = rows_of(msg, tokens, cols)
                    probs, dscores = weights_of(q, key[:, place], value[:, place], g, rows, bias[...])
                dk_out[:, place] = ((dk[:, here] + dot(dscores, q, 1, 0)) * factor).astype(BF16)
                dv_out[:, place] = (dv[:, here] + dot(probs, g, 1, 0)).astype(BF16)

    flat = [a for group in (*owns, *knowns) for a in group]
    return call(
        body, "key_grads", [query, key, value, bias, *nexts, *flat], [(tokens, width, BF16, False)] * 2, after,
    )


def query_grads(owns, backs, plan, after=()):
    tokens, width = owns[0].shape[0], sum(step[1] for step in plan)

    def body(ins, outs):
        (out,) = outs
        owns_in, backs_in = ins[: len(owns)], list(ins[len(owns) :])
        for first, part, heads, extra, step, offset in plan:
            sent = part - extra * (part // heads)
            own = owns_in[step]
            if sent:
                out[:, first : first + sent] = (own[:, offset : offset + sent] + backs_in.pop(0)[...].astype(F32)).astype(BF16)
            if extra:
                out[:, first + sent : first + part] = own[:, offset + sent : offset + part].astype(BF16)

    (out,) = call(body, "query_grads", [*owns, *backs], [(tokens, width, BF16, False)], after)
    return out


def on_device(queries, keys, values, out_grad, out_proj, attn_out, log_sum, group_order):
    tokens, width = queries.shape[1:]
    heads = log_sum.shape[1]
    size = width // heads
    rows = out_proj.shape[0]
    query, key, value, upstream, output = queries[0], keys[0], values[0], out_grad[0], attn_out[0]
    lse = log_sum[0]
    dp, ctx = lax.axis_size("dp"), lax.axis_size("ctx")
    me, here = lax.axis_index("dp"), lax.axis_index("ctx")
    pair = 2 if dp % 2 == 0 else 1
    chips = dp // pair
    core, chip = me % pair, me // pair

    def along_dp(array, by):
        return lax.ppermute(array, "dp", [(i, (i + by) % dp) for i in range(dp)])

    def along_ctx(array, by):
        return lax.ppermute(array, "ctx", [(i, (i + by) % ctx) for i in range(ctx)])

    def columns_for(there):
        return lax.dynamic_slice_in_dim(upstream, there * (pair * rows), pair * rows, axis=1)

    pieces = [columns_for((chip + j) % chips) for j in range(1, chips)]
    arrived = [along_dp(piece, pair * (j + 1)) for j, piece in enumerate(pieces)]
    at_own = jnp.stack([chip, core]).astype(jnp.int32)
    at_cut = jnp.stack([jnp.zeros_like(core), core]).astype(jnp.int32)
    weights = [stage([out_proj], 0, width, pieces)]
    if pair == 2:
        weights.append(stage([lax.ppermute(out_proj, "dp", [(i, i ^ 1) for i in range(dp)])], 0, width))
    query_sent, _ = lax.optimization_barrier((query, pieces))
    query_next = along_ctx(query_sent, -1)

    order = group_order[0]
    spots = jnp.stack([here, (here + 1) % ctx, (here + ctx - 1) % ctx]).astype(jnp.int32)
    scalars = (order, spots)

    chunks = CHUNKS if heads == sum(sum(cuts) for cuts in CHUNKS) else ((heads,),)
    both = BOTH if chunks is CHUNKS else 0
    plan, steps, done = [], [], 0
    for cuts in chunks:
        steps.append((done * size, sum(cuts) * size, cuts))
        for count in cuts:
            plan.append((done * size, count * size, count, 0, len(steps) - 1, done * size - steps[-1][0]))
            done += count
    plan[-1] = (*plan[-1][:3], both, *plan[-1][4:])

    backs, held = [], []
    for first, part, _ in steps:
        remote = project(at_cut, arrived, weights, first, part, BF16, after=held) if arrived else []
        held = list(remote[:1])
        backs.append([along_dp(remote[j - 1], -pair * j) for j in range(1, chips)])

    extra = plan[-1][3]
    before = []
    if extra:
        before = [along_ctx(stage([key, value], width - extra * size, extra * size, held), 1)]

    bias_own, bias_next, bias_before = masks(scalars, tokens, held)
    locals_ = []
    if EARLY:
        for c, (first, part, cuts) in enumerate(steps):
            waits = [query_next] if c == 0 else locals_[-1:]
            locals_ += project(at_own, [upstream], weights, first, part, F32, after=waits + held)
    msgs = []
    for c, (first, part, cuts) in enumerate(steps):
        if not EARLY:
            waits = [query_next] if c == 0 else msgs[-1]
            locals_ += project(at_own, [upstream], weights, first, part, F32, after=list(waits) + held)
        waits = (before if c else []) + locals_[c + 1 :]
        msgs.append(combine(locals_[c], backs[c], output, lse, first, cuts, size, after=waits))
    nexts = [along_ctx(msg, -1) for group in msgs for msg in group]

    crosses, sent, owns = [], [], []
    for c, (first, part, count, extra, step, _) in enumerate(plan):
        cross = ()
        if count > extra:
            waits = sent[-1:] + [own[0] for own in owns[-1:]]
            cross = cross_pair(query_next, key, value, bias_next, nexts[c], first, count - extra, size, after=waits)
            sent.append(cross[0])
        crosses.append(cross[1:])
        if c + 1 == len(plan) or plan[c + 1][4] > step:
            last = c + 1 == len(plan) and extra
            owns.append(
                own_pair(
                    query, key, value, bias_own, msgs[step], steps[step][0], size, extra if last else 0,
                    (*before, bias_before) if last else (), after=sent[-1:],
                )
            )
    returned = [along_ctx(dq, 1) for dq in sent]
    sums = [own[1:] for own in owns]
    key_grad, value_grad = key_grads(query_next, key, value, bias_next, nexts, sums, crosses, plan)
    query_grad = query_grads([own[0] for own in owns], returned, plan)
    shape = (1, tokens, width)
    return query_grad.reshape(shape), key_grad.reshape(shape), value_grad.reshape(shape)


def solution(mesh):
    return jax.shard_map(
        on_device,
        mesh=mesh,
        in_specs=(
            P("dp", "ctx", None),
            P("dp", "ctx", None),
            P("dp", "ctx", None),
            P("dp", "ctx", None),
            P("dp", None),
            P("dp", "ctx", None),
            P("dp", None, "ctx"),
            P("dp", None),
        ),
        out_specs=(P("dp", "ctx", None), P("dp", "ctx", None), P("dp", "ctx", None)),
        check_vma=False,
    )
```

time: 51 us -> 50 us (0.980)
  waiting for transfers between devices: 13.1 us -> 10.8 us
  starting transfers between devices: 15.6 us -> 17.6 us
  other arithmetic: 1.23 us -> 0.22 us
  Pallas kernels: 18.7 us -> 19.3 us
    ppermute x6 -> x7, starting transfers between devices: 10.3 us -> 12.3 us  [along_ctx(): return lax.ppermute(array, 'ctx', [(i, (i + by) % ctx) for i in range(ctx)])]
    ppermute x3, waiting for transfers between devices: 1.84 us -> 0.67 us  [along_dp(): return lax.ppermute(array, 'dp', [(i, (i + by) % dp) for i in range(dp)])]
    ppermute x6 -> x7, waiting for transfers between devices: 11.3 us -> 10.1 us  [along_ctx(): return lax.ppermute(array, 'ctx', [(i, (i + by) % ctx) for i in range(ctx)])]
    mul x1 -> x0, other arithmetic: 0.84 us -> none  [positions(): ids[:, None] * GROUP + jnp.arange(GROUP, dtype=jnp.int32)[None, :]]
    pallas_call x12 -> x13, Pallas kernels: 14.8 us -> 15.4 us  [call(): pl.pallas_call(kernel, in_specs=[here_in(pltpu.SMEM)] * len(scalars) + [h...]
  transfers between devices with their start and end apart: 10 -> 11, of which waited for: 5 -> 4; matrix products, arithmetic and copies ran while one was open for 5% -> 2% of each run, Pallas kernels for 35% -> 37%
where the time goes in v4:
time: 50 us; the launch traced here: 49.7 us
  Pallas kernels  19.3 us (39%)
  starting transfers between devices  17.6 us (35%)
  waiting for transfers between devices  10.8 us (22%)
  local copies, waits for them, and re-layouts  1.01 us (2%)
  between operations  0.83 us (2%)
    pallas_call x13, Pallas kernels, call(): pl.pallas_call(kernel, in_specs=[here_in(pltpu.SMEM)] * len(scalars) + [h...  15.4 us
    ppermute x7, starting transfers between devices, along_ctx(): return lax.ppermute(array, 'ctx', [(i, (i + by) % ctx) for i in range(ctx)])  12.3 us
    ppermute x7, waiting for transfers between devices, along_ctx(): return lax.ppermute(array, 'ctx', [(i, (i + by) % ctx) for i in range(ctx)])  10.1 us
    ppermute x3, starting transfers between devices, along_dp(): return lax.ppermute(array, 'dp', [(i, (i + by) % dp) for i in range(dp)])  4.77 us
    pallas_call x3, Pallas kernels, stage(): pl.pallas_call(kernel, in_specs=[here_in(pl.ANY)] * (n + n_after), out_sp...  3.89 us
  transfers between devices with their start and end apart: 11, of which 4 were waited for; matrix products, arithmetic and copies ran while one was open for 2% of the time, Pallas kernels for 37%

profile of v4, /device:TPU:0, one launch (start us, length us, event | category | flops | bytes accessed | tf_op | source)
XLA Modules:
  0.0 49.7 jit_solution(1850768773607659845)
XLA Ops:
  1.1 1.0 %dynamic-slice_bitcast_fusion.refs_1_ = bf16[128,1024]{1,0:T(8,128)(2,1)S(1)} fusion(bf16[1,128,2048]{2,1,0:T(8,128)(2,1)} %param.11, s32[]{:T(128)S(6)} %select_n.31), kind=kLoop, calls=%fused_computation | loop fusion | bytes 524292 | tf_op jit(solution)/shard_map/dynamic_slice | solution.py:312
  2.1 2.6 %collective-permute-start = (bf16[128,1024]{1,0:T(8,128)(2,1)S(1)}, bf16[128,1024]{1,0:T(8,128)(2,1)S(1)}, u32[]{:S(2)}, u32[]{:S(2)}) collective-permute-start(bf16[128,1024]{1,0:T(8,128)(2,1)S(1)} %dynamic-slice_bitcast_fusion.refs_1_), channel_id=1, source_target_pairs={{0,16},{8,24},{16,0},{24,8},{1,17},{9,25},{17,1},{25,9},{2,18},{10... | collective-permute-start | bytes 786440 | tf_op jit(solution)/shard_map/ppermute | solution.py:306
  4.7 4.6 %collective-permute-start.2 = (bf16[128,2048]{1,0:T(8,128)(2,1)}, bf16[128,2048]{1,0:T(8,128)(2,1)S(1)}, u32[]{:S(2)}, u32[]{:S(2)}) collective-permute-start(bf16[128,2048]{1,0:T(8,128)(2,1)} %bitcast.33), channel_id=1, source_target_pairs={{0,7},{1,0},{2,1},{3,2},{4,3},{5,4},{6,5},{7,6},{8,15},{9,8},{10,9... | collective-permute-start | bytes 1572872 | tf_op jit(solution)/shard_map/ppermute | solution.py:309
  9.4 1.5 %stage.3.refs_2_ = bf16[512,2048]{1,0:T(8,128)(2,1)S(1)} custom-call(bf16[512,2048]{1,0:T(8,128)(2,1)} %refs_0_.1, bf16[128,1024]{1,0:T(8,128)(2,1)S(1)} %dynamic-slice_bitcast_fusion.refs_1_), custom_call_target="tpu_custom_call" | custom-call | flops 1000000000 | bytes 4194304 | tf_op jit(solution)/shard_map/stage/pallas_call | solution.py:73
  11.0 1.5 %stage.4.refs_3_ = bf16[512,2048]{1,0:T(8,128)(2,1)S(1)} custom-call(bf16[512,2048]{1,0:T(8,128)(2,1)} %collective-permute-done.1.refs_0_), custom_call_target="tpu_custom_call" | custom-call | flops 1000000000 | bytes 4194304 | tf_op jit(solution)/shard_map/stage/pallas_call | solution.py:73
  12.5 1.0 %project.4.refs_4_ = bf16[128,1024]{1,0:T(8,128)(2,1)S(1)} custom-call(s32[2]{0:T(128)S(1)} %pad_add_fusion.1.refs_0_, bf16[128,1024]{1,0:T(8,128)(2,1)S(1)} %collective-permute-done.refs_1_, bf16[512,2048]{1,0:T(8,128)(2,1)S(1)} %stage.3.refs_2_, bf16[512,2048]{1,0:T(8,128)(2,1)S(1)} %stage.4.refs_3_), custom_call_target="tpu_custom_call" | custom-call | flops 1000000000 | bytes 4718592 | tf_op jit(solution)/shard_map/project/pallas_call | solution.py:40
  13.5 0.9 %collective-permute-start.3 = (bf16[128,1024]{1,0:T(8,128)(2,1)S(1)}, bf16[128,1024]{1,0:T(8,128)(2,1)S(1)}, u32[]{:S(2)}, u32[]{:S(2)}) collective-permute-start(bf16[128,1024]{1,0:T(8,128)(2,1)S(1)} %project.4.refs_4_), channel_id=1, source_target_pairs={{0,16},{8,24},{16,0},{24,8},{1,17},{9,25},{17,1},{25,9},{2,18},{10... | collective-permute-start | bytes 786440 | tf_op jit(solution)/shard_map/ppermute | solution.py:306
  14.5 1.0 %project.5.refs_2_.refs_5_ = bf16[128,1024]{1,0:T(8,128)(2,1)S(1)} custom-call(s32[2]{0:T(128)S(1)} %pad_add_fusion.1.refs_0_, bf16[128,1024]{1,0:T(8,128)(2,1)S(1)} %collective-permute-done.refs_1_, bf16[512,2048]{1,0:T(8,128)(2,1)S(1)} %stage.3.refs_2_, bf16[512,2048]{1,0:T(8,128)(2,1)S(1)} %stage.4.refs_3_, bf16[128,1024]{1,0:T(8,128)(2,1)S(1)} %project.4.refs_4_), custom_call_target="tpu_custom_call" | custom-call | flops 1000000000 | bytes 4718592 | tf_op jit(solution)/shard_map/project/pallas_call | solution.py:40
  15.5 1.2 %collective-permute-start.5 = (bf16[128,1024]{1,0:T(8,128)(2,1)S(1)}, bf16[128,1024]{1,0:T(8,128)(2,1)S(1)}, u32[]{:S(2)}, u32[]{:S(2)}) collective-permute-start(bf16[128,1024]{1,0:T(8,128)(2,1)S(1)} %project.5.refs_2_.refs_5_), channel_id=1, source_target_pairs={{0,16},{8,24},{16,0},{24,8},{1,17},{9,25},{17,1},{25,9},{2,18},{10... | collective-permute-start | bytes 786440 | tf_op jit(solution)/shard_map/ppermute | solution.py:306
  16.7 0.9 %stage.5 = bf16[128,768]{1,0:T(8,128)(2,1)S(1)} custom-call(bf16[128,2048]{1,0:T(8,128)(2,1)} %bitcast.19, bf16[128,2048]{1,0:T(8,128)(2,1)} %bitcast.25, bf16[128,1024]{1,0:T(8,128)(2,1)S(1)} %project.5.refs_2_.refs_5_), custom_call_target="tpu_custom_call" | custom-call | flops 1000000000 | bytes 393216 | tf_op jit(solution)/shard_map/stage/pallas_call | solution.py:73
  17.6 0.9 %collective-permute-start.6 = (bf16[128,768]{1,0:T(8,128)(2,1)S(1)}, bf16[128,768]{1,0:T(8,128)(2,1)S(1)}, u32[]{:S(2)}, u32[]{:S(2)}) collective-permute-start(bf16[128,768]{1,0:T(8,128)(2,1)S(1)} %stage.5), channel_id=1, source_target_pairs={{0,1},{1,2},{2,3},{3,4},{4,5},{5,6},{6,7},{7,0},{8,9},{9,10},{10,1... | collective-permute-start | bytes 589832 | tf_op jit(solution)/shard_map/ppermute | solution.py:309
  18.4 2.7 %collective-permute-done.2.refs_4_.refs_0_ = bf16[128,2048]{1,0:T(8,128)(2,1)S(1)} collective-permute-done((bf16[128,2048]{1,0:T(8,128)(2,1)}, bf16[128,2048]{1,0:T(8,128)(2,1)S(1)}, u32[]{:S(2)}, u32[]{:S(2)}) %collective-permute-start.2) | collective-permute-done | bytes 524320 | tf_op jit(solution)/shard_map/ppermute | solution.py:309
  21.1 1.0 %project.6.refs_0_ = f32[128,1024]{1,0:T(8,128)S(1)} custom-call(s32[2]{0:T(128)S(1)} %pad_add_fusion.2.refs_0_, bf16[128,2048]{1,0:T(8,128)(2,1)S(1)} %bitcast.17, bf16[512,2048]{1,0:T(8,128)(2,1)S(1)} %stage.3.refs_2_, bf16[512,2048]{1,0:T(8,128)(2,1)S(1)} %stage.4.refs_3_, bf16[128,2048]{1,0:T(8,128)(2,1)S(1)} %collective-permute-done.2.refs_4_.refs_0_, ...), custom_call_target="tpu_custom_call" | custom-call | flops 1000000000 | bytes 5242880 | tf_op jit(solution)/shard_map/project/pallas_call | solution.py:40
  23.2 4.6 %collective-permute-start.4 = (bf16[136,1024]{1,0:T(8,128)(2,1)S(1)}, bf16[136,1024]{1,0:T(8,128)(2,1)S(1)}, u32[]{:S(2)}, u32[]{:S(2)}) collective-permute-start(bf16[136,1024]{1,0:T(8,128)(2,1)S(1)} %combine.2.refs_4_), channel_id=1, source_target_pairs={{0,7},{1,0},{2,1},{3,2},{4,3},{5,4},{6,5},{7,6},{8,15},{9,8},{10,9... | collective-permute-start | bytes 835592 | tf_op jit(solution)/shard_map/ppermute | solution.py:309
  28.4 1.0 %project.7.refs_0_ = f32[128,1024]{1,0:T(8,128)S(1)} custom-call(s32[2]{0:T(128)S(1)} %pad_add_fusion.2.refs_0_, bf16[128,2048]{1,0:T(8,128)(2,1)S(1)} %bitcast.18, bf16[512,2048]{1,0:T(8,128)(2,1)S(1)} %stage.3.refs_2_, bf16[512,2048]{1,0:T(8,128)(2,1)S(1)} %stage.4.refs_3_, bf16[136,1024]{1,0:T(8,128)(2,1)S(1)} %combine.2.refs_4_, ...), custom_call_target="tpu_custom_call" | custom-call | flops 1000000000 | bytes 5242880 | tf_op jit(solution)/shard_map/project/pallas_call | solution.py:40
  29.9 1.6 %collective-permute-start.7 = (bf16[136,640]{1,0:T(8,128)(2,1)S(1)}, bf16[136,640]{1,0:T(8,128)(2,1)S(1)}, u32[]{:S(2)}, u32[]{:S(2)}) collective-permute-start(bf16[136,640]{1,0:T(8,128)(2,1)S(1)} %get-tuple-element.28.refs_4_), channel_id=1, source_target_pairs={{0,7},{1,0},{2,1},{3,2},{4,3},{5,4},{6,5},{7,6},{8,15},{9,8},{10,9... | collective-permute-start | bytes 522248 | tf_op jit(solution)/shard_map/ppermute | solution.py:309
  32.0 2.9 %collective-permute-done.4.refs_4_ = bf16[136,1024]{1,0:T(8,128)(2,1)S(1)} collective-permute-done((bf16[136,1024]{1,0:T(8,128)(2,1)S(1)}, bf16[136,1024]{1,0:T(8,128)(2,1)S(1)}, u32[]{:S(2)}, u32[]{:S(2)}) %collective-permute-start.4) | collective-permute-done | bytes 278560 | tf_op jit(solution)/shard_map/ppermute | solution.py:309
  34.9 1.8 %cross_pair.2 = (bf16[128,1024]{1,0:T(8,128)(2,1)S(1)}, bf16[128,1024]{1,0:T(8,128)(2,1)S(1)}, bf16[128,1024]{1,0:T(8,128)(2,1)S(1)}) custom-call(bf16[128,2048]{1,0:T(8,128)(2,1)S(1)} %collective-permute-done.2.refs_4_.refs_0_, bf16[128,2048]{1,0:T(8,128)(2,1)S(1)} %bitcast.20, bf16[128,2048]{1,0:T(8,128)(2,1)S(1)} %bitcast.26, ...), custom_call_target="tpu_custom_call" | custom-call | flops 1000000000 | bytes 2703360 | tf_op jit(solution)/shard_map/cross_pair/pallas_call | solution.py:40
  36.8 1.8 %own_pair.2 = (f32[128,1024]{1,0:T(8,128)S(1)}, f32[128,1024]{1,0:T(8,128)S(1)}, f32[128,1024]{1,0:T(8,128)S(1)}) custom-call(bf16[128,2048]{1,0:T(8,128)(2,1)S(1)} %bitcast.34, bf16[128,2048]{1,0:T(8,128)(2,1)S(1)} %bitcast.21, bf16[128,2048]{1,0:T(8,128)(2,1)S(1)} %bitcast.27, f32[128,128]{1,0:T(8,128)S(1)} %get-tuple-element.23.refs_3_, ...), custom_call_target="tpu_custom_call" | custom-call | flops 1000000000 | bytes 3489792 | tf_op jit(solution)/shard_map/own_pair/pallas_call | solution.py:40
  38.7 1.2 %cross_pair.3 = (bf16[128,640]{1,0:T(8,128)(2,1)S(1)}, bf16[128,640]{1,0:T(8,128)(2,1)S(1)}, bf16[128,640]{1,0:T(8,128)(2,1)S(1)}) custom-call(bf16[128,2048]{1,0:T(8,128)(2,1)S(1)} %collective-permute-done.2.refs_4_.refs_0_, bf16[128,2048]{1,0:T(8,128)(2,1)S(1)} %bitcast.22, bf16[128,2048]{1,0:T(8,128)(2,1)S(1)} %bitcast.28, ...), custom_call_target="tpu_custom_call" | custom-call | flops 1000000000 | bytes 2304000 | tf_op jit(solution)/shard_map/cross_pair/pallas_call | solution.py:40
  40.0 2.4 %own_pair.3 = (f32[128,1024]{1,0:T(8,128)S(1)}, f32[128,1024]{1,0:T(8,128)S(1)}, f32[128,1024]{1,0:T(8,128)S(1)}) custom-call(bf16[128,2048]{1,0:T(8,128)(2,1)S(1)} %bitcast.35, bf16[128,2048]{1,0:T(8,128)(2,1)S(1)} %bitcast.23, bf16[128,2048]{1,0:T(8,128)(2,1)S(1)} %bitcast.29, f32[128,128]{1,0:T(8,128)S(1)} %get-tuple-element.23.refs_3_, ...), custom_call_target="tpu_custom_call" | custom-call | flops 1000000000 | bytes 3751936 | tf_op jit(solution)/shard_map/own_pair/pallas_call | solution.py:40
  42.4 2.0 %key_grads.1 = (bf16[128,2048]{1,0:T(8,128)(2,1)}, bf16[128,2048]{1,0:T(8,128)(2,1)}) custom-call(bf16[128,2048]{1,0:T(8,128)(2,1)S(1)} %collective-permute-done.2.refs_4_.refs_0_, bf16[128,2048]{1,0:T(8,128)(2,1)S(1)} %bitcast.24, bf16[128,2048]{1,0:T(8,128)(2,1)S(1)} %bitcast.30, f32[128,128]{1,0:T(8,128)S(1)} %get-tuple-element.25.refs_3_, ...), custom_call_target="tpu_custom_call" | custom-call | flops 1000000000 | bytes 6193152 | tf_op jit(solution)/shard_map/key_grads/pallas_call | solution.py:40
  44.3 4.5 %collective-permute-done.9.refs_3_ = bf16[128,640]{1,0:T(8,128)(2,1)S(1)} collective-permute-done((bf16[128,640]{1,0:T(8,128)(2,1)S(1)}, bf16[128,640]{1,0:T(8,128)(2,1)S(1)}, u32[]{:S(2)}, u32[]{:S(2)}) %collective-permute-start.9) | collective-permute-done | bytes 163872 | tf_op jit(solution)/shard_map/ppermute | solution.py:309
  48.9 0.9 %query_grads.1 = bf16[128,2048]{1,0:T(8,128)(2,1)} custom-call(f32[128,1024]{1,0:T(8,128)S(1)} %get-tuple-element.27.refs_6_.refs_0_, f32[128,1024]{1,0:T(8,128)S(1)} %get-tuple-element.32.refs_1_, bf16[128,1024]{1,0:T(8,128)(2,1)S(1)} %collective-permute-done.8.refs_2_, bf16[128,640]{1,0:T(8,128)(2,1)S(1)} %collective-permute-done.9.refs_3_), custom_call_target="tpu_custom_call" | custom-call | flops 1000000000 | bytes 1998848 | tf_op jit(solution)/shard_map/query_grads/pallas_call | solution.py:40
  (32 shorter events, 3.5 us)
Async XLA Ops:
  0.6 10.4 %collective-permute-start.1 = (bf16[512,2048]{1,0:T(8,128)(2,1)}, bf16[512,2048]{1,0:T(8,128)(2,1)}, u32[]{:S(2)}, u32[]{:S(2)}) collective-permute-start(bf16[512,2048]{1,0:T(8,128)(2,1)} %refs_0_.1), channel_id=1, source_target_pairs={{0,8},{8,0},{16,24},{24,16},{1,9},{9,1},{17,25},{25,17},{2,10},{10... | collective-permute-start | bytes 6291464 | tf_op jit(solution)/shard_map/ppermute | solution.py:320
  2.1 10.4 %collective-permute-start = (bf16[128,1024]{1,0:T(8,128)(2,1)S(1)}, bf16[128,1024]{1,0:T(8,128)(2,1)S(1)}, u32[]{:S(2)}, u32[]{:S(2)}) collective-permute-start(bf16[128,1024]{1,0:T(8,128)(2,1)S(1)} %dynamic-slice_bitcast_fusion.refs_1_), channel_id=1, source_target_pairs={{0,16},{8,24},{16,0},{24,8},{1,17},{9,25},{17,1},{25,9},{2,18},{10... | collective-permute-start | bytes 786440 | tf_op jit(solution)/shard_map/ppermute | solution.py:306
  4.7 16.4 %collective-permute-start.2 = (bf16[128,2048]{1,0:T(8,128)(2,1)}, bf16[128,2048]{1,0:T(8,128)(2,1)S(1)}, u32[]{:S(2)}, u32[]{:S(2)}) collective-permute-start(bf16[128,2048]{1,0:T(8,128)(2,1)} %bitcast.33), channel_id=1, source_target_pairs={{0,7},{1,0},{2,1},{3,2},{4,3},{5,4},{6,5},{7,6},{8,15},{9,8},{10,9... | collective-permute-start | bytes 1572872 | tf_op jit(solution)/shard_map/ppermute | solution.py:309
  13.5 9.3 %collective-permute-start.3 = (bf16[128,1024]{1,0:T(8,128)(2,1)S(1)}, bf16[128,1024]{1,0:T(8,128)(2,1)S(1)}, u32[]{:S(2)}, u32[]{:S(2)}) collective-permute-start(bf16[128,1024]{1,0:T(8,128)(2,1)S(1)} %project.4.refs_4_), channel_id=1, source_target_pairs={{0,16},{8,24},{16,0},{24,8},{1,17},{9,25},{17,1},{25,9},{2,18},{10... | collective-permute-start | bytes 786440 | tf_op jit(solution)/shard_map/ppermute | solution.py:306
  15.5 5.7 %copy-start = (bf16[1,128,2048]{2,1,0:T(8,128)(2,1)S(1)}, bf16[1,128,2048]{2,1,0:T(8,128)(2,1)}, u32[]{:S(2)}) copy-start(bf16[1,128,2048]{2,1,0:T(8,128)(2,1)} %param.11) | copy-start | bytes 1572868
  15.5 14.0 %collective-permute-start.5 = (bf16[128,1024]{1,0:T(8,128)(2,1)S(1)}, bf16[128,1024]{1,0:T(8,128)(2,1)S(1)}, u32[]{:S(2)}, u32[]{:S(2)}) collective-permute-start(bf16[128,1024]{1,0:T(8,128)(2,1)S(1)} %project.5.refs_2_.refs_5_), channel_id=1, source_target_pairs={{0,16},{8,24},{16,0},{24,8},{1,17},{9,25},{17,1},{25,9},{2,18},{10... | collective-permute-start | bytes 786440 | tf_op jit(solution)/shard_map/ppermute | solution.py:306
  17.6 11.9 %collective-permute-start.6 = (bf16[128,768]{1,0:T(8,128)(2,1)S(1)}, bf16[128,768]{1,0:T(8,128)(2,1)S(1)}, u32[]{:S(2)}, u32[]{:S(2)}) collective-permute-start(bf16[128,768]{1,0:T(8,128)(2,1)S(1)} %stage.5), channel_id=1, source_target_pairs={{0,1},{1,2},{2,3},{3,4},{4,5},{5,6},{6,7},{7,0},{8,9},{9,10},{10,1... | collective-permute-start | bytes 589832 | tf_op jit(solution)/shard_map/ppermute | solution.py:309
  21.1 1.7 %copy-start.3 = (bf16[1,128,2048]{2,1,0:T(8,128)(2,1)S(1)}, bf16[1,128,2048]{2,1,0:T(8,128)(2,1)}, u32[]{:S(2)}) copy-start(bf16[1,128,2048]{2,1,0:T(8,128)(2,1)} %param.13) | copy-start | bytes 1572868
  21.1 1.7 %copy-start.5 = (f32[1,16,128]{2,1,0:T(8,128)S(1)}, f32[1,16,128]{2,1,0:T(8,128)}, u32[]{:S(2)}) copy-start(f32[1,16,128]{2,1,0:T(8,128)} %param.14) | copy-start | bytes 24580
  22.1 5.7 %copy-start.6 = (s32[1,32]{1,0:T(1,128)S(1)}, s32[1,32]{1,0:T(1,128)}, u32[]{:S(2)}) copy-start(s32[1,32]{1,0:T(1,128)} %param.15) | copy-start | bytes 388
  23.2 11.7 %collective-permute-start.4 = (bf16[136,1024]{1,0:T(8,128)(2,1)S(1)}, bf16[136,1024]{1,0:T(8,128)(2,1)S(1)}, u32[]{:S(2)}, u32[]{:S(2)}) collective-permute-start(bf16[136,1024]{1,0:T(8,128)(2,1)S(1)} %combine.2.refs_4_), channel_id=1, source_target_pairs={{0,7},{1,0},{2,1},{3,2},{4,3},{5,4},{6,5},{7,6},{8,15},{9,8},{10,9... | collective-permute-start | bytes 835592 | tf_op jit(solution)/shard_map/ppermute | solution.py:309
  29.4 5.5 %copy-start.1 = (bf16[1,128,2048]{2,1,0:T(8,128)(2,1)S(1)}, bf16[1,128,2048]{2,1,0:T(8,128)(2,1)}, u32[]{:S(2)}) copy-start(bf16[1,128,2048]{2,1,0:T(8,128)(2,1)} %param.9) | copy-start | bytes 1572868
  29.4 5.5 %copy-start.2 = (bf16[1,128,2048]{2,1,0:T(8,128)(2,1)S(1)}, bf16[1,128,2048]{2,1,0:T(8,128)(2,1)}, u32[]{:S(2)}) copy-start(bf16[1,128,2048]{2,1,0:T(8,128)(2,1)} %param.10) | copy-start | bytes 1572868
  29.9 7.0 %copy-start.4 = (bf16[1,128,2048]{2,1,0:T(8,128)(2,1)S(1)}, bf16[1,128,2048]{2,1,0:T(8,128)(2,1)}, u32[]{:S(2)}) copy-start(bf16[1,128,2048]{2,1,0:T(8,128)(2,1)} %param.8) | copy-start | bytes 1572868
  29.9 8.8 %collective-permute-start.7 = (bf16[136,640]{1,0:T(8,128)(2,1)S(1)}, bf16[136,640]{1,0:T(8,128)(2,1)S(1)}, u32[]{:S(2)}, u32[]{:S(2)}) collective-permute-start(bf16[136,640]{1,0:T(8,128)(2,1)S(1)} %get-tuple-element.28.refs_4_), channel_id=1, source_target_pairs={{0,7},{1,0},{2,1},{3,2},{4,3},{5,4},{6,5},{7,6},{8,15},{9,8},{10,9... | collective-permute-start | bytes 522248 | tf_op jit(solution)/shard_map/ppermute | solution.py:309
  31.5 10.9 %collective-permute-start.10 = (bf16[136,384]{1,0:T(8,128)(2,1)S(1)}, bf16[136,384]{1,0:T(8,128)(2,1)S(1)}, u32[]{:S(2)}, u32[]{:S(2)}) collective-permute-start(bf16[136,384]{1,0:T(8,128)(2,1)S(1)} %get-tuple-element.29.refs_5_), channel_id=1, source_target_pairs={{0,7},{1,0},{2,1},{3,2},{4,3},{5,4},{6,5},{7,6},{8,15},{9,8},{10,9... | collective-permute-start | bytes 313352 | tf_op jit(solution)/shard_map/ppermute | solution.py:309
  36.8 12.1 %collective-permute-start.8 = (bf16[128,1024]{1,0:T(8,128)(2,1)S(1)}, bf16[128,1024]{1,0:T(8,128)(2,1)S(1)}, u32[]{:S(2)}, u32[]{:S(2)}) collective-permute-start(bf16[128,1024]{1,0:T(8,128)(2,1)S(1)} %get-tuple-element.26.refs_5_), channel_id=1, source_target_pairs={{0,1},{1,2},{2,3},{3,4},{4,5},{5,6},{6,7},{7,0},{8,9},{9,10},{10,1... | collective-permute-start | bytes 786440 | tf_op jit(solution)/shard_map/ppermute | solution.py:309
  39.9 8.9 %collective-permute-start.9 = (bf16[128,640]{1,0:T(8,128)(2,1)S(1)}, bf16[128,640]{1,0:T(8,128)(2,1)S(1)}, u32[]{:S(2)}, u32[]{:S(2)}) collective-permute-start(bf16[128,640]{1,0:T(8,128)(2,1)S(1)} %get-tuple-element.31.refs_8_), channel_id=1, source_target_pairs={{0,1},{1,2},{2,3},{3,4},{4,5},{5,6},{6,7},{7,0},{8,9},{9,10},{10,1... | collective-permute-start | bytes 491528 | tf_op jit(solution)/shard_map/ppermute | solution.py:309

commit v5 on v4

--- a/solution.py
+++ b/solution.py
@@ -11,8 +11,7 @@
 CHUNKS = ((8,), (5, 3))
 BOTH = 3
 LANES = 256
-EARLY = False
-EXTRA = 8
+EXTRA = 16
 VMEM_MIB = 20
 F32 = jnp.float32
 BF16 = jnp.bfloat16
@@ -142,7 +141,7 @@
             third = rest - second
             turn = jnp.where(pick < 3, pick, pick - 3)
             kept = jnp.where(turn == 0, first_part, jnp.where(turn == 1, second, third))
-            msg[tokens:, :] = kept.astype(BF16)
+            msg[tokens:, :] = jnp.concatenate([kept, kept], axis=0).astype(BF16)
             done += heads
 
     return call(
@@ -347,18 +346,11 @@
         before = [along_ctx(stage([key, value], width - extra * size, extra * size, held), 1)]
 
     bias_own, bias_next, bias_before = masks(scalars, tokens, held)
-    locals_ = []
-    if EARLY:
-        for c, (first, part, cuts) in enumerate(steps):
-            waits = [query_next] if c == 0 else locals_[-1:]
-            locals_ += project(at_own, [upstream], weights, first, part, F32, after=waits + held)
     msgs = []
     for c, (first, part, cuts) in enumerate(steps):
-        if not EARLY:
-            waits = [query_next] if c == 0 else msgs[-1]
-            locals_ += project(at_own, [upstream], weights, first, part, F32, after=list(waits) + held)
-        waits = (before if c else []) + locals_[c + 1 :]
-        msgs.append(combine(locals_[c], backs[c], output, lse, first, cuts, size, after=waits))
+        waits = [query_next] if c == 0 else msgs[-1]
+        (local,) = project(at_own, [upstream], weights, first, part, F32, after=list(waits) + held)
+        msgs.append(combine(local, backs[c], output, lse, first, cuts, size, after=before if c else []))
     nexts = [along_ctx(msg, -1) for group in msgs for msg in group]
 
     crosses, sent, owns = [], [], []

time: 50 us -> 50.5 us (1.010)
    ppermute x7, waiting for transfers between devices: 10.1 us -> 10.7 us  [along_ctx(): return lax.ppermute(array, 'ctx', [(i, (i + by) % ctx) for i in range(ctx)])]
where the time goes in v5:
time: 50.5 us; the launch traced here: 50.3 us
  Pallas kernels  19.3 us (38%)
  starting transfers between devices  17.6 us (35%)
  waiting for transfers between devices  11.2 us (22%)
  local copies, waits for them, and re-layouts  1.01 us (2%)
  between operations  0.83 us (2%)
    pallas_call x13, Pallas kernels, call(): pl.pallas_call(kernel, in_specs=[here_in(pltpu.SMEM)] * len(scalars) + [h...  15.5 us
    ppermute x7, starting transfers between devices, along_ctx(): return lax.ppermute(array, 'ctx', [(i, (i + by) % ctx) for i in range(ctx)])  12.3 us
    ppermute x7, waiting for transfers between devices, along_ctx(): return lax.ppermute(array, 'ctx', [(i, (i + by) % ctx) for i in range(ctx)])  10.7 us
    ppermute x3, starting transfers between devices, along_dp(): return lax.ppermute(array, 'dp', [(i, (i + by) % dp) for i in range(dp)])  4.77 us
    pallas_call x3, Pallas kernels, stage(): pl.pallas_call(kernel, in_specs=[here_in(pl.ANY)] * (n + n_after), out_sp...  3.88 us
  transfers between devices with their start and end apart: 11, of which 4 were waited for; matrix products, arithmetic and copies ran while one was open for 2% of the time, Pallas kernels for 37%

profile of v5, /device:TPU:0, one launch (start us, length us, event | category | flops | bytes accessed | tf_op | source)
XLA Modules:
  0.0 50.3 jit_solution(14317684821541740654)
XLA Ops:
  1.1 1.0 %dynamic-slice_bitcast_fusion.refs_1_ = bf16[128,1024]{1,0:T(8,128)(2,1)S(1)} fusion(bf16[1,128,2048]{2,1,0:T(8,128)(2,1)} %param.11, s32[]{:T(128)S(6)} %select_n.31), kind=kLoop, calls=%fused_computation | loop fusion | bytes 524292 | tf_op jit(solution)/shard_map/dynamic_slice | solution.py:311
  2.1 2.6 %collective-permute-start = (bf16[128,1024]{1,0:T(8,128)(2,1)S(1)}, bf16[128,1024]{1,0:T(8,128)(2,1)S(1)}, u32[]{:S(2)}, u32[]{:S(2)}) collective-permute-start(bf16[128,1024]{1,0:T(8,128)(2,1)S(1)} %dynamic-slice_bitcast_fusion.refs_1_), channel_id=1, source_target_pairs={{0,16},{8,24},{16,0},{24,8},{1,17},{9,25},{17,1},{25,9},{2,18},{10... | collective-permute-start | bytes 786440 | tf_op jit(solution)/shard_map/ppermute | solution.py:305
  4.7 4.6 %collective-permute-start.2 = (bf16[128,2048]{1,0:T(8,128)(2,1)}, bf16[128,2048]{1,0:T(8,128)(2,1)S(1)}, u32[]{:S(2)}, u32[]{:S(2)}) collective-permute-start(bf16[128,2048]{1,0:T(8,128)(2,1)} %bitcast.33), channel_id=1, source_target_pairs={{0,7},{1,0},{2,1},{3,2},{4,3},{5,4},{6,5},{7,6},{8,15},{9,8},{10,9... | collective-permute-start | bytes 1572872 | tf_op jit(solution)/shard_map/ppermute | solution.py:308
  9.4 1.5 %stage.3.refs_2_ = bf16[512,2048]{1,0:T(8,128)(2,1)S(1)} custom-call(bf16[512,2048]{1,0:T(8,128)(2,1)} %refs_0_.1, bf16[128,1024]{1,0:T(8,128)(2,1)S(1)} %dynamic-slice_bitcast_fusion.refs_1_), custom_call_target="tpu_custom_call" | custom-call | flops 1000000000 | bytes 4194304 | tf_op jit(solution)/shard_map/stage/pallas_call | solution.py:72
  11.0 1.5 %stage.4.refs_3_ = bf16[512,2048]{1,0:T(8,128)(2,1)S(1)} custom-call(bf16[512,2048]{1,0:T(8,128)(2,1)} %collective-permute-done.1.refs_0_), custom_call_target="tpu_custom_call" | custom-call | flops 1000000000 | bytes 4194304 | tf_op jit(solution)/shard_map/stage/pallas_call | solution.py:72
  12.5 1.0 %project.4.refs_4_ = bf16[128,1024]{1,0:T(8,128)(2,1)S(1)} custom-call(s32[2]{0:T(128)S(1)} %pad_add_fusion.1.refs_0_, bf16[128,1024]{1,0:T(8,128)(2,1)S(1)} %collective-permute-done.refs_1_, bf16[512,2048]{1,0:T(8,128)(2,1)S(1)} %stage.3.refs_2_, bf16[512,2048]{1,0:T(8,128)(2,1)S(1)} %stage.4.refs_3_), custom_call_target="tpu_custom_call" | custom-call | flops 1000000000 | bytes 4718592 | tf_op jit(solution)/shard_map/project/pallas_call | solution.py:39
  13.5 1.0 %collective-permute-start.3 = (bf16[128,1024]{1,0:T(8,128)(2,1)S(1)}, bf16[128,1024]{1,0:T(8,128)(2,1)S(1)}, u32[]{:S(2)}, u32[]{:S(2)}) collective-permute-start(bf16[128,1024]{1,0:T(8,128)(2,1)S(1)} %project.4.refs_4_), channel_id=1, source_target_pairs={{0,16},{8,24},{16,0},{24,8},{1,17},{9,25},{17,1},{25,9},{2,18},{10... | collective-permute-start | bytes 786440 | tf_op jit(solution)/shard_map/ppermute | solution.py:305
  14.5 1.0 %project.5.refs_2_.refs_5_ = bf16[128,1024]{1,0:T(8,128)(2,1)S(1)} custom-call(s32[2]{0:T(128)S(1)} %pad_add_fusion.1.refs_0_, bf16[128,1024]{1,0:T(8,128)(2,1)S(1)} %collective-permute-done.refs_1_, bf16[512,2048]{1,0:T(8,128)(2,1)S(1)} %stage.3.refs_2_, bf16[512,2048]{1,0:T(8,128)(2,1)S(1)} %stage.4.refs_3_, bf16[128,1024]{1,0:T(8,128)(2,1)S(1)} %project.4.refs_4_), custom_call_target="tpu_custom_call" | custom-call | flops 1000000000 | bytes 4718592 | tf_op jit(solution)/shard_map/project/pallas_call | solution.py:39
  15.5 1.2 %collective-permute-start.5 = (bf16[128,1024]{1,0:T(8,128)(2,1)S(1)}, bf16[128,1024]{1,0:T(8,128)(2,1)S(1)}, u32[]{:S(2)}, u32[]{:S(2)}) collective-permute-start(bf16[128,1024]{1,0:T(8,128)(2,1)S(1)} %project.5.refs_2_.refs_5_), channel_id=1, source_target_pairs={{0,16},{8,24},{16,0},{24,8},{1,17},{9,25},{17,1},{25,9},{2,18},{10... | collective-permute-start | bytes 786440 | tf_op jit(solution)/shard_map/ppermute | solution.py:305
  16.6 0.9 %stage.5 = bf16[128,768]{1,0:T(8,128)(2,1)S(1)} custom-call(bf16[128,2048]{1,0:T(8,128)(2,1)} %bitcast.19, bf16[128,2048]{1,0:T(8,128)(2,1)} %bitcast.25, bf16[128,1024]{1,0:T(8,128)(2,1)S(1)} %project.5.refs_2_.refs_5_), custom_call_target="tpu_custom_call" | custom-call | flops 1000000000 | bytes 393216 | tf_op jit(solution)/shard_map/stage/pallas_call | solution.py:72
  17.5 1.0 %collective-permute-start.6 = (bf16[128,768]{1,0:T(8,128)(2,1)S(1)}, bf16[128,768]{1,0:T(8,128)(2,1)S(1)}, u32[]{:S(2)}, u32[]{:S(2)}) collective-permute-start(bf16[128,768]{1,0:T(8,128)(2,1)S(1)} %stage.5), channel_id=1, source_target_pairs={{0,1},{1,2},{2,3},{3,4},{4,5},{5,6},{6,7},{7,0},{8,9},{9,10},{10,1... | collective-permute-start | bytes 589832 | tf_op jit(solution)/shard_map/ppermute | solution.py:308
  18.4 2.7 %collective-permute-done.2.refs_4_.refs_0_ = bf16[128,2048]{1,0:T(8,128)(2,1)S(1)} collective-permute-done((bf16[128,2048]{1,0:T(8,128)(2,1)}, bf16[128,2048]{1,0:T(8,128)(2,1)S(1)}, u32[]{:S(2)}, u32[]{:S(2)}) %collective-permute-start.2) | collective-permute-done | bytes 524320 | tf_op jit(solution)/shard_map/ppermute | solution.py:308
  21.1 1.0 %project.6.refs_0_ = f32[128,1024]{1,0:T(8,128)S(1)} custom-call(s32[2]{0:T(128)S(1)} %pad_add_fusion.2.refs_0_, bf16[128,2048]{1,0:T(8,128)(2,1)S(1)} %bitcast.17, bf16[512,2048]{1,0:T(8,128)(2,1)S(1)} %stage.3.refs_2_, bf16[512,2048]{1,0:T(8,128)(2,1)S(1)} %stage.4.refs_3_, bf16[128,2048]{1,0:T(8,128)(2,1)S(1)} %collective-permute-done.2.refs_4_.refs_0_, ...), custom_call_target="tpu_custom_call" | custom-call | flops 1000000000 | bytes 5242880 | tf_op jit(solution)/shard_map/project/pallas_call | solution.py:39
  23.1 4.7 %collective-permute-start.4 = (bf16[144,1024]{1,0:T(8,128)(2,1)S(1)}, bf16[144,1024]{1,0:T(8,128)(2,1)S(1)}, u32[]{:S(2)}, u32[]{:S(2)}) collective-permute-start(bf16[144,1024]{1,0:T(8,128)(2,1)S(1)} %combine.2.refs_4_), channel_id=1, source_target_pairs={{0,7},{1,0},{2,1},{3,2},{4,3},{5,4},{6,5},{7,6},{8,15},{9,8},{10,9... | collective-permute-start | bytes 884744 | tf_op jit(solution)/shard_map/ppermute | solution.py:308
  28.5 1.0 %project.7.refs_0_ = f32[128,1024]{1,0:T(8,128)S(1)} custom-call(s32[2]{0:T(128)S(1)} %pad_add_fusion.2.refs_0_, bf16[128,2048]{1,0:T(8,128)(2,1)S(1)} %bitcast.18, bf16[512,2048]{1,0:T(8,128)(2,1)S(1)} %stage.3.refs_2_, bf16[512,2048]{1,0:T(8,128)(2,1)S(1)} %stage.4.refs_3_, bf16[144,1024]{1,0:T(8,128)(2,1)S(1)} %combine.2.refs_4_, ...), custom_call_target="tpu_custom_call" | custom-call | flops 1000000000 | bytes 5242880 | tf_op jit(solution)/shard_map/project/pallas_call | solution.py:39
  30.0 1.5 %collective-permute-start.7 = (bf16[144,640]{1,0:T(8,128)(2,1)S(1)}, bf16[144,640]{1,0:T(8,128)(2,1)S(1)}, u32[]{:S(2)}, u32[]{:S(2)}) collective-permute-start(bf16[144,640]{1,0:T(8,128)(2,1)S(1)} %get-tuple-element.28.refs_4_), channel_id=1, source_target_pairs={{0,7},{1,0},{2,1},{3,2},{4,3},{5,4},{6,5},{7,6},{8,15},{9,8},{10,9... | collective-permute-start | bytes 552968 | tf_op jit(solution)/shard_map/ppermute | solution.py:308
  32.0 3.3 %collective-permute-done.4.refs_4_ = bf16[144,1024]{1,0:T(8,128)(2,1)S(1)} collective-permute-done((bf16[144,1024]{1,0:T(8,128)(2,1)S(1)}, bf16[144,1024]{1,0:T(8,128)(2,1)S(1)}, u32[]{:S(2)}, u32[]{:S(2)}) %collective-permute-start.4) | collective-permute-done | bytes 294944 | tf_op jit(solution)/shard_map/ppermute | solution.py:308
  35.3 1.8 %cross_pair.2 = (bf16[128,1024]{1,0:T(8,128)(2,1)S(1)}, bf16[128,1024]{1,0:T(8,128)(2,1)S(1)}, bf16[128,1024]{1,0:T(8,128)(2,1)S(1)}) custom-call(bf16[128,2048]{1,0:T(8,128)(2,1)S(1)} %collective-permute-done.2.refs_4_.refs_0_, bf16[128,2048]{1,0:T(8,128)(2,1)S(1)} %bitcast.20, bf16[128,2048]{1,0:T(8,128)(2,1)S(1)} %bitcast.26, ...), custom_call_target="tpu_custom_call" | custom-call | flops 1000000000 | bytes 2719744 | tf_op jit(solution)/shard_map/cross_pair/pallas_call | solution.py:39
  37.2 1.8 %own_pair.2 = (f32[128,1024]{1,0:T(8,128)S(1)}, f32[128,1024]{1,0:T(8,128)S(1)}, f32[128,1024]{1,0:T(8,128)S(1)}) custom-call(bf16[128,2048]{1,0:T(8,128)(2,1)S(1)} %bitcast.34, bf16[128,2048]{1,0:T(8,128)(2,1)S(1)} %bitcast.21, bf16[128,2048]{1,0:T(8,128)(2,1)S(1)} %bitcast.27, f32[128,128]{1,0:T(8,128)S(1)} %get-tuple-element.23.refs_3_, ...), custom_call_target="tpu_custom_call" | custom-call | flops 1000000000 | bytes 3506176 | tf_op jit(solution)/shard_map/own_pair/pallas_call | solution.py:39
  39.1 1.2 %cross_pair.3 = (bf16[128,640]{1,0:T(8,128)(2,1)S(1)}, bf16[128,640]{1,0:T(8,128)(2,1)S(1)}, bf16[128,640]{1,0:T(8,128)(2,1)S(1)}) custom-call(bf16[128,2048]{1,0:T(8,128)(2,1)S(1)} %collective-permute-done.2.refs_4_.refs_0_, bf16[128,2048]{1,0:T(8,128)(2,1)S(1)} %bitcast.22, bf16[128,2048]{1,0:T(8,128)(2,1)S(1)} %bitcast.28, ...), custom_call_target="tpu_custom_call" | custom-call | flops 1000000000 | bytes 2314240 | tf_op jit(solution)/shard_map/cross_pair/pallas_call | solution.py:39
  40.3 2.4 %own_pair.3 = (f32[128,1024]{1,0:T(8,128)S(1)}, f32[128,1024]{1,0:T(8,128)S(1)}, f32[128,1024]{1,0:T(8,128)S(1)}) custom-call(bf16[128,2048]{1,0:T(8,128)(2,1)S(1)} %bitcast.35, bf16[128,2048]{1,0:T(8,128)(2,1)S(1)} %bitcast.23, bf16[128,2048]{1,0:T(8,128)(2,1)S(1)} %bitcast.29, f32[128,128]{1,0:T(8,128)S(1)} %get-tuple-element.23.refs_3_, ...), custom_call_target="tpu_custom_call" | custom-call | flops 1000000000 | bytes 3768320 | tf_op jit(solution)/shard_map/own_pair/pallas_call | solution.py:39
  42.7 2.0 %key_grads.1 = (bf16[128,2048]{1,0:T(8,128)(2,1)}, bf16[128,2048]{1,0:T(8,128)(2,1)}) custom-call(bf16[128,2048]{1,0:T(8,128)(2,1)S(1)} %collective-permute-done.2.refs_4_.refs_0_, bf16[128,2048]{1,0:T(8,128)(2,1)S(1)} %bitcast.24, bf16[128,2048]{1,0:T(8,128)(2,1)S(1)} %bitcast.30, f32[128,128]{1,0:T(8,128)S(1)} %get-tuple-element.25.refs_3_, ...), custom_call_target="tpu_custom_call" | custom-call | flops 1000000000 | bytes 6225920 | tf_op jit(solution)/shard_map/key_grads/pallas_call | solution.py:39
  44.7 4.7 %collective-permute-done.9.refs_3_ = bf16[128,640]{1,0:T(8,128)(2,1)S(1)} collective-permute-done((bf16[128,640]{1,0:T(8,128)(2,1)S(1)}, bf16[128,640]{1,0:T(8,128)(2,1)S(1)}, u32[]{:S(2)}, u32[]{:S(2)}) %collective-permute-start.9) | collective-permute-done | bytes 163872 | tf_op jit(solution)/shard_map/ppermute | solution.py:308
  49.4 0.9 %query_grads.1 = bf16[128,2048]{1,0:T(8,128)(2,1)} custom-call(f32[128,1024]{1,0:T(8,128)S(1)} %get-tuple-element.27.refs_6_.refs_0_, f32[128,1024]{1,0:T(8,128)S(1)} %get-tuple-element.32.refs_1_, bf16[128,1024]{1,0:T(8,128)(2,1)S(1)} %collective-permute-done.8.refs_2_, bf16[128,640]{1,0:T(8,128)(2,1)S(1)} %collective-permute-done.9.refs_3_), custom_call_target="tpu_custom_call" | custom-call | flops 1000000000 | bytes 1998848 | tf_op jit(solution)/shard_map/query_grads/pallas_call | solution.py:39
  (32 shorter events, 3.4 us)
Async XLA Ops:
  0.6 10.3 %collective-permute-start.1 = (bf16[512,2048]{1,0:T(8,128)(2,1)}, bf16[512,2048]{1,0:T(8,128)(2,1)}, u32[]{:S(2)}, u32[]{:S(2)}) collective-permute-start(bf16[512,2048]{1,0:T(8,128)(2,1)} %refs_0_.1), channel_id=1, source_target_pairs={{0,8},{8,0},{16,24},{24,16},{1,9},{9,1},{17,25},{25,17},{2,10},{10... | collective-permute-start | bytes 6291464 | tf_op jit(solution)/shard_map/ppermute | solution.py:319
  2.1 10.4 %collective-permute-start = (bf16[128,1024]{1,0:T(8,128)(2,1)S(1)}, bf16[128,1024]{1,0:T(8,128)(2,1)S(1)}, u32[]{:S(2)}, u32[]{:S(2)}) collective-permute-start(bf16[128,1024]{1,0:T(8,128)(2,1)S(1)} %dynamic-slice_bitcast_fusion.refs_1_), channel_id=1, source_target_pairs={{0,16},{8,24},{16,0},{24,8},{1,17},{9,25},{17,1},{25,9},{2,18},{10... | collective-permute-start | bytes 786440 | tf_op jit(solution)/shard_map/ppermute | solution.py:305
  4.7 16.4 %collective-permute-start.2 = (bf16[128,2048]{1,0:T(8,128)(2,1)}, bf16[128,2048]{1,0:T(8,128)(2,1)S(1)}, u32[]{:S(2)}, u32[]{:S(2)}) collective-permute-start(bf16[128,2048]{1,0:T(8,128)(2,1)} %bitcast.33), channel_id=1, source_target_pairs={{0,7},{1,0},{2,1},{3,2},{4,3},{5,4},{6,5},{7,6},{8,15},{9,8},{10,9... | collective-permute-start | bytes 1572872 | tf_op jit(solution)/shard_map/ppermute | solution.py:308
  13.5 9.3 %collective-permute-start.3 = (bf16[128,1024]{1,0:T(8,128)(2,1)S(1)}, bf16[128,1024]{1,0:T(8,128)(2,1)S(1)}, u32[]{:S(2)}, u32[]{:S(2)}) collective-permute-start(bf16[128,1024]{1,0:T(8,128)(2,1)S(1)} %project.4.refs_4_), channel_id=1, source_target_pairs={{0,16},{8,24},{16,0},{24,8},{1,17},{9,25},{17,1},{25,9},{2,18},{10... | collective-permute-start | bytes 786440 | tf_op jit(solution)/shard_map/ppermute | solution.py:305
  15.5 5.7 %copy-start = (bf16[1,128,2048]{2,1,0:T(8,128)(2,1)S(1)}, bf16[1,128,2048]{2,1,0:T(8,128)(2,1)}, u32[]{:S(2)}) copy-start(bf16[1,128,2048]{2,1,0:T(8,128)(2,1)} %param.11) | copy-start | bytes 1572868
  15.5 14.0 %collective-permute-start.5 = (bf16[128,1024]{1,0:T(8,128)(2,1)S(1)}, bf16[128,1024]{1,0:T(8,128)(2,1)S(1)}, u32[]{:S(2)}, u32[]{:S(2)}) collective-permute-start(bf16[128,1024]{1,0:T(8,128)(2,1)S(1)} %project.5.refs_2_.refs_5_), channel_id=1, source_target_pairs={{0,16},{8,24},{16,0},{24,8},{1,17},{9,25},{17,1},{25,9},{2,18},{10... | collective-permute-start | bytes 786440 | tf_op jit(solution)/shard_map/ppermute | solution.py:305
  17.5 12.0 %collective-permute-start.6 = (bf16[128,768]{1,0:T(8,128)(2,1)S(1)}, bf16[128,768]{1,0:T(8,128)(2,1)S(1)}, u32[]{:S(2)}, u32[]{:S(2)}) collective-permute-start(bf16[128,768]{1,0:T(8,128)(2,1)S(1)} %stage.5), channel_id=1, source_target_pairs={{0,1},{1,2},{2,3},{3,4},{4,5},{5,6},{6,7},{7,0},{8,9},{9,10},{10,1... | collective-permute-start | bytes 589832 | tf_op jit(solution)/shard_map/ppermute | solution.py:308
  21.1 1.6 %copy-start.3 = (bf16[1,128,2048]{2,1,0:T(8,128)(2,1)S(1)}, bf16[1,128,2048]{2,1,0:T(8,128)(2,1)}, u32[]{:S(2)}) copy-start(bf16[1,128,2048]{2,1,0:T(8,128)(2,1)} %param.13) | copy-start | bytes 1572868
  21.1 1.6 %copy-start.5 = (f32[1,16,128]{2,1,0:T(8,128)S(1)}, f32[1,16,128]{2,1,0:T(8,128)}, u32[]{:S(2)}) copy-start(f32[1,16,128]{2,1,0:T(8,128)} %param.14) | copy-start | bytes 24580
  22.1 5.8 %copy-start.6 = (s32[1,32]{1,0:T(1,128)S(1)}, s32[1,32]{1,0:T(1,128)}, u32[]{:S(2)}) copy-start(s32[1,32]{1,0:T(1,128)} %param.15) | copy-start | bytes 388
  23.1 12.1 %collective-permute-start.4 = (bf16[144,1024]{1,0:T(8,128)(2,1)S(1)}, bf16[144,1024]{1,0:T(8,128)(2,1)S(1)}, u32[]{:S(2)}, u32[]{:S(2)}) collective-permute-start(bf16[144,1024]{1,0:T(8,128)(2,1)S(1)} %combine.2.refs_4_), channel_id=1, source_target_pairs={{0,7},{1,0},{2,1},{3,2},{4,3},{5,4},{6,5},{7,6},{8,15},{9,8},{10,9... | collective-permute-start | bytes 884744 | tf_op jit(solution)/shard_map/ppermute | solution.py:308
  29.5 5.8 %copy-start.1 = (bf16[1,128,2048]{2,1,0:T(8,128)(2,1)S(1)}, bf16[1,128,2048]{2,1,0:T(8,128)(2,1)}, u32[]{:S(2)}) copy-start(bf16[1,128,2048]{2,1,0:T(8,128)(2,1)} %param.9) | copy-start | bytes 1572868
  29.5 5.8 %copy-start.2 = (bf16[1,128,2048]{2,1,0:T(8,128)(2,1)S(1)}, bf16[1,128,2048]{2,1,0:T(8,128)(2,1)}, u32[]{:S(2)}) copy-start(bf16[1,128,2048]{2,1,0:T(8,128)(2,1)} %param.10) | copy-start | bytes 1572868
  29.9 7.2 %copy-start.4 = (bf16[1,128,2048]{2,1,0:T(8,128)(2,1)S(1)}, bf16[1,128,2048]{2,1,0:T(8,128)(2,1)}, u32[]{:S(2)}) copy-start(bf16[1,128,2048]{2,1,0:T(8,128)(2,1)} %param.8) | copy-start | bytes 1572868
  30.0 9.1 %collective-permute-start.7 = (bf16[144,640]{1,0:T(8,128)(2,1)S(1)}, bf16[144,640]{1,0:T(8,128)(2,1)S(1)}, u32[]{:S(2)}, u32[]{:S(2)}) collective-permute-start(bf16[144,640]{1,0:T(8,128)(2,1)S(1)} %get-tuple-element.28.refs_4_), channel_id=1, source_target_pairs={{0,7},{1,0},{2,1},{3,2},{4,3},{5,4},{6,5},{7,6},{8,15},{9,8},{10,9... | collective-permute-start | bytes 552968 | tf_op jit(solution)/shard_map/ppermute | solution.py:308
  31.5 11.2 %collective-permute-start.10 = (bf16[144,384]{1,0:T(8,128)(2,1)S(1)}, bf16[144,384]{1,0:T(8,128)(2,1)S(1)}, u32[]{:S(2)}, u32[]{:S(2)}) collective-permute-start(bf16[144,384]{1,0:T(8,128)(2,1)S(1)} %get-tuple-element.29.refs_5_), channel_id=1, source_target_pairs={{0,7},{1,0},{2,1},{3,2},{4,3},{5,4},{6,5},{7,6},{8,15},{9,8},{10,9... | collective-permute-start | bytes 331784 | tf_op jit(solution)/shard_map/ppermute | solution.py:308
  37.1 12.3 %collective-permute-start.8 = (bf16[128,1024]{1,0:T(8,128)(2,1)S(1)}, bf16[128,1024]{1,0:T(8,128)(2,1)S(1)}, u32[]{:S(2)}, u32[]{:S(2)}) collective-permute-start(bf16[128,1024]{1,0:T(8,128)(2,1)S(1)} %get-tuple-element.26.refs_5_), channel_id=1, source_target_pairs={{0,1},{1,2},{2,3},{3,4},{4,5},{5,6},{6,7},{7,0},{8,9},{9,10},{10,1... | collective-permute-start | bytes 786440 | tf_op jit(solution)/shard_map/ppermute | solution.py:308
  40.3 9.1 %collective-permute-start.9 = (bf16[128,640]{1,0:T(8,128)(2,1)S(1)}, bf16[128,640]{1,0:T(8,128)(2,1)S(1)}, u32[]{:S(2)}, u32[]{:S(2)}) collective-permute-start(bf16[128,640]{1,0:T(8,128)(2,1)S(1)} %get-tuple-element.31.refs_8_), channel_id=1, source_target_pairs={{0,1},{1,2},{2,3},{3,4},{4,5},{5,6},{6,7},{7,0},{8,9},{9,10},{10,1... | collective-permute-start | bytes 491528 | tf_op jit(solution)/shard_map/ppermute | solution.py:308

commit v6 on v5

--- a/solution.py
+++ b/solution.py
@@ -29,7 +29,7 @@
     return pltpu.with_memory_space_constraint(array, pltpu.VMEM)
 
 
-def call(body, name, ins, outs, after=(), scalars=(), free=()):
+def call(body, name, ins, outs, after=(), scalars=(), free=(), work=1e9):
     n_in, n_after = len(scalars) + len(ins), len(after)
 
     def kernel(*refs):
@@ -42,7 +42,7 @@
         out_specs=[here_in(pltpu.VMEM)] * len(outs),
         out_shape=[pltpu.VMEM((r, c), t) if kept else jax.ShapeDtypeStruct((r, c), t) for r, c, t, kept in outs],
         compiler_params=pltpu.CompilerParams(vmem_limit_bytes=VMEM_MIB * 1024 * 1024),
-        cost_estimate=pl.CostEstimate(flops=int(1e9), bytes_accessed=int(1 * moved), transcendentals=0),
+        cost_estimate=pl.CostEstimate(flops=int(work), bytes_accessed=int(1 * moved), transcendentals=0),
         name=name,
     )(*scalars, *[a if i in free else pin(a) for i, a in enumerate(ins)], *after)
 
@@ -216,7 +216,7 @@
                 done += size
 
     return call(
-        body, "own_pair", [query, key, value, bias, *msgs, *before], [(tokens, width, F32, True)] * 3, after,
+        body, "own_pair", [query, key, value, bias, *msgs, *before], [(tokens, width, F32, True)] * 3, after, work=2e9,
     )
 
 
@@ -266,7 +266,7 @@
 
     flat = [a for group in (*owns, *knowns) for a in group]
     return call(
-        body, "key_grads", [query, key, value, bias, *nexts, *flat], [(tokens, width, BF16, False)] * 2, after,
+        body, "key_grads", [query, key, value, bias, *nexts, *flat], [(tokens, width, BF16, False)] * 2, after, work=2e9,
     )
 
 
@@ -350,7 +350,7 @@
     for c, (first, part, cuts) in enumerate(steps):
         waits = [query_next] if c == 0 else msgs[-1]
         (local,) = project(at_own, [upstream], weights, first, part, F32, after=list(waits) + held)
-        msgs.append(combine(local, backs[c], output, lse, first, cuts, size, after=before if c else []))
+        msgs.append(combine(local, backs[c], output, lse, first, cuts, size))
     nexts = [along_ctx(msg, -1) for group in msgs for msg in group]
 
     crosses, sent, owns = [], [], []

time: 50.5 us -> 56.3 us (1.11)
  starting transfers between devices: 17.6 us -> 23.6 us
    ppermute x7, starting transfers between devices: 12.3 us -> 18.3 us  [along_ctx(): return lax.ppermute(array, 'ctx', [(i, (i + by) % ctx) for i in range(ctx)])]
  transfers between devices with their start and end apart: 11 -> 11, of which waited for: 4 -> 5; matrix products, arithmetic and copies ran while one was open for 2% -> 2% of each run, Pallas kernels for 37% -> 33%
where the time goes in v6:
time: 56.3 us; the launch traced here: 56 us
  starting transfers between devices  23.6 us (42%)
  Pallas kernels  19.3 us (34%)
  waiting for transfers between devices  11.1 us (20%)
  local copies, waits for them, and re-layouts  1 us (2%)
  between operations  0.78 us (1%)
    ppermute x7, starting transfers between devices, along_ctx(): return lax.ppermute(array, 'ctx', [(i, (i + by) % ctx) for i in range(ctx)])  18.3 us
    pallas_call x13, Pallas kernels, call(): pl.pallas_call(kernel, in_specs=[here_in(pltpu.SMEM)] * len(scalars) + [h...  15.4 us
    ppermute x7, waiting for transfers between devices, along_ctx(): return lax.ppermute(array, 'ctx', [(i, (i + by) % ctx) for i in range(ctx)])  10.5 us
    ppermute x3, starting transfers between devices, along_dp(): return lax.ppermute(array, 'dp', [(i, (i + by) % dp) for i in range(dp)])  4.77 us
    pallas_call x3, Pallas kernels, stage(): pl.pallas_call(kernel, in_specs=[here_in(pl.ANY)] * (n + n_after), out_sp...  3.88 us
  transfers between devices with their start and end apart: 11, of which 5 were waited for; matrix products, arithmetic and copies ran while one was open for 2% of the time, Pallas kernels for 33%

profile of v6, /device:TPU:0, one launch (start us, length us, event | category | flops | bytes accessed | tf_op | source)
XLA Modules:
  0.0 56.0 jit_solution(5581382035209564680)
XLA Ops:
  1.1 1.0 %dynamic-slice_bitcast_fusion.refs_1_ = bf16[128,1024]{1,0:T(8,128)(2,1)S(1)} fusion(bf16[1,128,2048]{2,1,0:T(8,128)(2,1)} %param.11, s32[]{:T(128)S(6)} %select_n.31), kind=kLoop, calls=%fused_computation | loop fusion | bytes 524292 | tf_op jit(solution)/shard_map/dynamic_slice | solution.py:311
  2.1 2.6 %collective-permute-start = (bf16[128,1024]{1,0:T(8,128)(2,1)S(1)}, bf16[128,1024]{1,0:T(8,128)(2,1)S(1)}, u32[]{:S(2)}, u32[]{:S(2)}) collective-permute-start(bf16[128,1024]{1,0:T(8,128)(2,1)S(1)} %dynamic-slice_bitcast_fusion.refs_1_), channel_id=1, source_target_pairs={{0,16},{8,24},{16,0},{24,8},{1,17},{9,25},{17,1},{25,9},{2,18},{10... | collective-permute-start | bytes 786440 | tf_op jit(solution)/shard_map/ppermute | solution.py:305
  4.7 4.6 %collective-permute-start.2 = (bf16[128,2048]{1,0:T(8,128)(2,1)}, bf16[128,2048]{1,0:T(8,128)(2,1)S(1)}, u32[]{:S(2)}, u32[]{:S(2)}) collective-permute-start(bf16[128,2048]{1,0:T(8,128)(2,1)} %bitcast.21), channel_id=1, source_target_pairs={{0,7},{1,0},{2,1},{3,2},{4,3},{5,4},{6,5},{7,6},{8,15},{9,8},{10,9... | collective-permute-start | bytes 1572872 | tf_op jit(solution)/shard_map/ppermute | solution.py:308
  9.4 1.5 %stage.3.refs_2_ = bf16[512,2048]{1,0:T(8,128)(2,1)S(1)} custom-call(bf16[512,2048]{1,0:T(8,128)(2,1)} %refs_0_.1, bf16[128,1024]{1,0:T(8,128)(2,1)S(1)} %dynamic-slice_bitcast_fusion.refs_1_), custom_call_target="tpu_custom_call" | custom-call | flops 1000000000 | bytes 4194304 | tf_op jit(solution)/shard_map/stage/pallas_call | solution.py:72
  11.0 1.5 %stage.4.refs_3_ = bf16[512,2048]{1,0:T(8,128)(2,1)S(1)} custom-call(bf16[512,2048]{1,0:T(8,128)(2,1)} %collective-permute-done.1.refs_0_), custom_call_target="tpu_custom_call" | custom-call | flops 1000000000 | bytes 4194304 | tf_op jit(solution)/shard_map/stage/pallas_call | solution.py:72
  12.5 1.0 %project.4.refs_4_ = bf16[128,1024]{1,0:T(8,128)(2,1)S(1)} custom-call(s32[2]{0:T(128)S(1)} %pad_add_fusion.1.refs_0_, bf16[128,1024]{1,0:T(8,128)(2,1)S(1)} %collective-permute-done.refs_1_, bf16[512,2048]{1,0:T(8,128)(2,1)S(1)} %stage.3.refs_2_, bf16[512,2048]{1,0:T(8,128)(2,1)S(1)} %stage.4.refs_3_), custom_call_target="tpu_custom_call" | custom-call | flops 1000000000 | bytes 4718592 | tf_op jit(solution)/shard_map/project/pallas_call | solution.py:39
  13.5 1.0 %collective-permute-start.3 = (bf16[128,1024]{1,0:T(8,128)(2,1)S(1)}, bf16[128,1024]{1,0:T(8,128)(2,1)S(1)}, u32[]{:S(2)}, u32[]{:S(2)}) collective-permute-start(bf16[128,1024]{1,0:T(8,128)(2,1)S(1)} %project.4.refs_4_), channel_id=1, source_target_pairs={{0,16},{8,24},{16,0},{24,8},{1,17},{9,25},{17,1},{25,9},{2,18},{10... | collective-permute-start | bytes 786440 | tf_op jit(solution)/shard_map/ppermute | solution.py:305
  14.5 1.0 %project.5.refs_2_.refs_5_ = bf16[128,1024]{1,0:T(8,128)(2,1)S(1)} custom-call(s32[2]{0:T(128)S(1)} %pad_add_fusion.1.refs_0_, bf16[128,1024]{1,0:T(8,128)(2,1)S(1)} %collective-permute-done.refs_1_, bf16[512,2048]{1,0:T(8,128)(2,1)S(1)} %stage.3.refs_2_, bf16[512,2048]{1,0:T(8,128)(2,1)S(1)} %stage.4.refs_3_, bf16[128,1024]{1,0:T(8,128)(2,1)S(1)} %project.4.refs_4_), custom_call_target="tpu_custom_call" | custom-call | flops 1000000000 | bytes 4718592 | tf_op jit(solution)/shard_map/project/pallas_call | solution.py:39
  15.5 1.2 %collective-permute-start.5 = (bf16[128,1024]{1,0:T(8,128)(2,1)S(1)}, bf16[128,1024]{1,0:T(8,128)(2,1)S(1)}, u32[]{:S(2)}, u32[]{:S(2)}) collective-permute-start(bf16[128,1024]{1,0:T(8,128)(2,1)S(1)} %project.5.refs_2_.refs_5_), channel_id=1, source_target_pairs={{0,16},{8,24},{16,0},{24,8},{1,17},{9,25},{17,1},{25,9},{2,18},{10... | collective-permute-start | bytes 786440 | tf_op jit(solution)/shard_map/ppermute | solution.py:305
  16.7 4.4 %collective-permute-done.2.refs_4_.refs_0_ = bf16[128,2048]{1,0:T(8,128)(2,1)S(1)} collective-permute-done((bf16[128,2048]{1,0:T(8,128)(2,1)}, bf16[128,2048]{1,0:T(8,128)(2,1)S(1)}, u32[]{:S(2)}, u32[]{:S(2)}) %collective-permute-start.2) | collective-permute-done | bytes 524320 | tf_op jit(solution)/shard_map/ppermute | solution.py:308
  21.1 1.0 %project.6.refs_0_ = f32[128,1024]{1,0:T(8,128)S(1)} custom-call(s32[2]{0:T(128)S(1)} %pad_add_fusion.2.refs_0_, bf16[128,2048]{1,0:T(8,128)(2,1)S(1)} %bitcast.17, bf16[512,2048]{1,0:T(8,128)(2,1)S(1)} %stage.3.refs_2_, bf16[512,2048]{1,0:T(8,128)(2,1)S(1)} %stage.4.refs_3_, bf16[128,2048]{1,0:T(8,128)(2,1)S(1)} %collective-permute-done.2.refs_4_.refs_0_, ...), custom_call_target="tpu_custom_call" | custom-call | flops 1000000000 | bytes 5242880 | tf_op jit(solution)/shard_map/project/pallas_call | solution.py:39
  23.2 4.6 %collective-permute-start.4 = (bf16[144,1024]{1,0:T(8,128)(2,1)S(1)}, bf16[144,1024]{1,0:T(8,128)(2,1)S(1)}, u32[]{:S(2)}, u32[]{:S(2)}) collective-permute-start(bf16[144,1024]{1,0:T(8,128)(2,1)S(1)} %combine.2.refs_4_), channel_id=1, source_target_pairs={{0,7},{1,0},{2,1},{3,2},{4,3},{5,4},{6,5},{7,6},{8,15},{9,8},{10,9... | collective-permute-start | bytes 884744 | tf_op jit(solution)/shard_map/ppermute | solution.py:308
  29.2 1.0 %project.7.refs_0_ = f32[128,1024]{1,0:T(8,128)S(1)} custom-call(s32[2]{0:T(128)S(1)} %pad_add_fusion.2.refs_0_, bf16[128,2048]{1,0:T(8,128)(2,1)S(1)} %bitcast.18, bf16[512,2048]{1,0:T(8,128)(2,1)S(1)} %stage.3.refs_2_, bf16[512,2048]{1,0:T(8,128)(2,1)S(1)} %stage.4.refs_3_, bf16[144,1024]{1,0:T(8,128)(2,1)S(1)} %combine.2.refs_4_, ...), custom_call_target="tpu_custom_call" | custom-call | flops 1000000000 | bytes 5242880 | tf_op jit(solution)/shard_map/project/pallas_call | solution.py:39
  30.6 4.8 %collective-permute-start.7 = (bf16[144,640]{1,0:T(8,128)(2,1)S(1)}, bf16[144,640]{1,0:T(8,128)(2,1)S(1)}, u32[]{:S(2)}, u32[]{:S(2)}) collective-permute-start(bf16[144,640]{1,0:T(8,128)(2,1)S(1)} %get-tuple-element.28.refs_4_), channel_id=1, source_target_pairs={{0,7},{1,0},{2,1},{3,2},{4,3},{5,4},{6,5},{7,6},{8,15},{9,8},{10,9... | collective-permute-start | bytes 552968 | tf_op jit(solution)/shard_map/ppermute | solution.py:308
  35.5 1.8 %cross_pair.2 = (bf16[128,1024]{1,0:T(8,128)(2,1)S(1)}, bf16[128,1024]{1,0:T(8,128)(2,1)S(1)}, bf16[128,1024]{1,0:T(8,128)(2,1)S(1)}) custom-call(bf16[128,2048]{1,0:T(8,128)(2,1)S(1)} %collective-permute-done.2.refs_4_.refs_0_, bf16[128,2048]{1,0:T(8,128)(2,1)S(1)} %bitcast.25, bf16[128,2048]{1,0:T(8,128)(2,1)S(1)} %bitcast.31, ...), custom_call_target="tpu_custom_call" | custom-call | flops 1000000000 | bytes 2719744 | tf_op jit(solution)/shard_map/cross_pair/pallas_call | solution.py:39
  37.3 2.0 %collective-permute-start.8 = (bf16[128,1024]{1,0:T(8,128)(2,1)S(1)}, bf16[128,1024]{1,0:T(8,128)(2,1)S(1)}, u32[]{:S(2)}, u32[]{:S(2)}) collective-permute-start(bf16[128,1024]{1,0:T(8,128)(2,1)S(1)} %get-tuple-element.26.refs_5_), channel_id=1, source_target_pairs={{0,1},{1,2},{2,3},{3,4},{4,5},{5,6},{6,7},{7,0},{8,9},{9,10},{10,1... | collective-permute-start | bytes 786440 | tf_op jit(solution)/shard_map/ppermute | solution.py:308
  39.3 1.8 %own_pair.2 = (f32[128,1024]{1,0:T(8,128)S(1)}, f32[128,1024]{1,0:T(8,128)S(1)}, f32[128,1024]{1,0:T(8,128)S(1)}) custom-call(bf16[128,2048]{1,0:T(8,128)(2,1)S(1)} %bitcast.22, bf16[128,2048]{1,0:T(8,128)(2,1)S(1)} %bitcast.26, bf16[128,2048]{1,0:T(8,128)(2,1)S(1)} %bitcast.32, f32[128,128]{1,0:T(8,128)S(1)} %get-tuple-element.23.refs_3_, ...), custom_call_target="tpu_custom_call" | custom-call | flops 2000000000 | bytes 3506176 | tf_op jit(solution)/shard_map/own_pair/pallas_call | solution.py:39
  41.3 1.2 %cross_pair.3 = (bf16[128,640]{1,0:T(8,128)(2,1)S(1)}, bf16[128,640]{1,0:T(8,128)(2,1)S(1)}, bf16[128,640]{1,0:T(8,128)(2,1)S(1)}) custom-call(bf16[128,2048]{1,0:T(8,128)(2,1)S(1)} %collective-permute-done.2.refs_4_.refs_0_, bf16[128,2048]{1,0:T(8,128)(2,1)S(1)} %bitcast.27, bf16[128,2048]{1,0:T(8,128)(2,1)S(1)} %bitcast.33, ...), custom_call_target="tpu_custom_call" | custom-call | flops 1000000000 | bytes 2314240 | tf_op jit(solution)/shard_map/cross_pair/pallas_call | solution.py:39
  42.5 2.3 %collective-permute-start.9 = (bf16[128,640]{1,0:T(8,128)(2,1)S(1)}, bf16[128,640]{1,0:T(8,128)(2,1)S(1)}, u32[]{:S(2)}, u32[]{:S(2)}) collective-permute-start(bf16[128,640]{1,0:T(8,128)(2,1)S(1)} %get-tuple-element.31.refs_8_), channel_id=1, source_target_pairs={{0,1},{1,2},{2,3},{3,4},{4,5},{5,6},{6,7},{7,0},{8,9},{9,10},{10,1... | collective-permute-start | bytes 491528 | tf_op jit(solution)/shard_map/ppermute | solution.py:308
  44.8 2.4 %own_pair.3 = (f32[128,1024]{1,0:T(8,128)S(1)}, f32[128,1024]{1,0:T(8,128)S(1)}, f32[128,1024]{1,0:T(8,128)S(1)}) custom-call(bf16[128,2048]{1,0:T(8,128)(2,1)S(1)} %bitcast.23, bf16[128,2048]{1,0:T(8,128)(2,1)S(1)} %bitcast.28, bf16[128,2048]{1,0:T(8,128)(2,1)S(1)} %bitcast.34, f32[128,128]{1,0:T(8,128)S(1)} %get-tuple-element.23.refs_3_, ...), custom_call_target="tpu_custom_call" | custom-call | flops 2000000000 | bytes 3768320 | tf_op jit(solution)/shard_map/own_pair/pallas_call | solution.py:39
  47.2 3.1 %collective-permute-done.10.refs_6_ = bf16[144,384]{1,0:T(8,128)(2,1)S(1)} collective-permute-done((bf16[144,384]{1,0:T(8,128)(2,1)S(1)}, bf16[144,384]{1,0:T(8,128)(2,1)S(1)}, u32[]{:S(2)}, u32[]{:S(2)}) %collective-permute-start.10) | collective-permute-done | bytes 110624 | tf_op jit(solution)/shard_map/ppermute | solution.py:308
  50.2 1.9 %key_grads.1 = (bf16[128,2048]{1,0:T(8,128)(2,1)}, bf16[128,2048]{1,0:T(8,128)(2,1)}) custom-call(bf16[128,2048]{1,0:T(8,128)(2,1)S(1)} %collective-permute-done.2.refs_4_.refs_0_, bf16[128,2048]{1,0:T(8,128)(2,1)S(1)} %bitcast.29, bf16[128,2048]{1,0:T(8,128)(2,1)S(1)} %bitcast.35, f32[128,128]{1,0:T(8,128)S(1)} %get-tuple-element.25.refs_3_, ...), custom_call_target="tpu_custom_call" | custom-call | flops 2000000000 | bytes 6225920 | tf_op jit(solution)/shard_map/key_grads/pallas_call | solution.py:39
  52.2 2.9 %collective-permute-done.9.refs_3_ = bf16[128,640]{1,0:T(8,128)(2,1)S(1)} collective-permute-done((bf16[128,640]{1,0:T(8,128)(2,1)S(1)}, bf16[128,640]{1,0:T(8,128)(2,1)S(1)}, u32[]{:S(2)}, u32[]{:S(2)}) %collective-permute-start.9) | collective-permute-done | bytes 163872 | tf_op jit(solution)/shard_map/ppermute | solution.py:308
  55.1 0.9 %query_grads.1 = bf16[128,2048]{1,0:T(8,128)(2,1)} custom-call(f32[128,1024]{1,0:T(8,128)S(1)} %get-tuple-element.27.refs_6_.refs_0_, f32[128,1024]{1,0:T(8,128)S(1)} %get-tuple-element.32.refs_1_, bf16[128,1024]{1,0:T(8,128)(2,1)S(1)} %collective-permute-done.8.refs_2_, bf16[128,640]{1,0:T(8,128)(2,1)S(1)} %collective-permute-done.9.refs_3_), custom_call_target="tpu_custom_call" | custom-call | flops 1000000000 | bytes 1998848 | tf_op jit(solution)/shard_map/query_grads/pallas_call | solution.py:39
  (32 shorter events, 3.8 us)
Async XLA Ops:
  0.6 10.3 %collective-permute-start.1 = (bf16[512,2048]{1,0:T(8,128)(2,1)}, bf16[512,2048]{1,0:T(8,128)(2,1)}, u32[]{:S(2)}, u32[]{:S(2)}) collective-permute-start(bf16[512,2048]{1,0:T(8,128)(2,1)} %refs_0_.1), channel_id=1, source_target_pairs={{0,8},{8,0},{16,24},{24,16},{1,9},{9,1},{17,25},{25,17},{2,10},{10... | collective-permute-start | bytes 6291464 | tf_op jit(solution)/shard_map/ppermute | solution.py:319
  2.1 10.4 %collective-permute-start = (bf16[128,1024]{1,0:T(8,128)(2,1)S(1)}, bf16[128,1024]{1,0:T(8,128)(2,1)S(1)}, u32[]{:S(2)}, u32[]{:S(2)}) collective-permute-start(bf16[128,1024]{1,0:T(8,128)(2,1)S(1)} %dynamic-slice_bitcast_fusion.refs_1_), channel_id=1, source_target_pairs={{0,16},{8,24},{16,0},{24,8},{1,17},{9,25},{17,1},{25,9},{2,18},{10... | collective-permute-start | bytes 786440 | tf_op jit(solution)/shard_map/ppermute | solution.py:305
  4.7 16.4 %collective-permute-start.2 = (bf16[128,2048]{1,0:T(8,128)(2,1)}, bf16[128,2048]{1,0:T(8,128)(2,1)S(1)}, u32[]{:S(2)}, u32[]{:S(2)}) collective-permute-start(bf16[128,2048]{1,0:T(8,128)(2,1)} %bitcast.21), channel_id=1, source_target_pairs={{0,7},{1,0},{2,1},{3,2},{4,3},{5,4},{6,5},{7,6},{8,15},{9,8},{10,9... | collective-permute-start | bytes 1572872 | tf_op jit(solution)/shard_map/ppermute | solution.py:308
  13.5 9.3 %collective-permute-start.3 = (bf16[128,1024]{1,0:T(8,128)(2,1)S(1)}, bf16[128,1024]{1,0:T(8,128)(2,1)S(1)}, u32[]{:S(2)}, u32[]{:S(2)}) collective-permute-start(bf16[128,1024]{1,0:T(8,128)(2,1)S(1)} %project.4.refs_4_), channel_id=1, source_target_pairs={{0,16},{8,24},{16,0},{24,8},{1,17},{9,25},{17,1},{25,9},{2,18},{10... | collective-permute-start | bytes 786440 | tf_op jit(solution)/shard_map/ppermute | solution.py:305
  14.5 6.6 %copy-start = (bf16[1,128,2048]{2,1,0:T(8,128)(2,1)S(1)}, bf16[1,128,2048]{2,1,0:T(8,128)(2,1)}, u32[]{:S(2)}) copy-start(bf16[1,128,2048]{2,1,0:T(8,128)(2,1)} %param.11) | copy-start | bytes 1572868
  15.5 14.7 %collective-permute-start.5 = (bf16[128,1024]{1,0:T(8,128)(2,1)S(1)}, bf16[128,1024]{1,0:T(8,128)(2,1)S(1)}, u32[]{:S(2)}, u32[]{:S(2)}) collective-permute-start(bf16[128,1024]{1,0:T(8,128)(2,1)S(1)} %project.5.refs_2_.refs_5_), channel_id=1, source_target_pairs={{0,16},{8,24},{16,0},{24,8},{1,17},{9,25},{17,1},{25,9},{2,18},{10... | collective-permute-start | bytes 786440 | tf_op jit(solution)/shard_map/ppermute | solution.py:305
  21.1 1.6 %copy-start.1 = (bf16[1,128,2048]{2,1,0:T(8,128)(2,1)S(1)}, bf16[1,128,2048]{2,1,0:T(8,128)(2,1)}, u32[]{:S(2)}) copy-start(bf16[1,128,2048]{2,1,0:T(8,128)(2,1)} %param.13) | copy-start | bytes 1572868
  21.1 1.6 %copy-start.5 = (f32[1,16,128]{2,1,0:T(8,128)S(1)}, f32[1,16,128]{2,1,0:T(8,128)}, u32[]{:S(2)}) copy-start(f32[1,16,128]{2,1,0:T(8,128)} %param.14) | copy-start | bytes 24580
  23.1 5.4 %copy-start.6 = (s32[1,32]{1,0:T(1,128)S(1)}, s32[1,32]{1,0:T(1,128)}, u32[]{:S(2)}) copy-start(s32[1,32]{1,0:T(1,128)} %param.15) | copy-start | bytes 388
  23.2 12.3 %collective-permute-start.4 = (bf16[144,1024]{1,0:T(8,128)(2,1)S(1)}, bf16[144,1024]{1,0:T(8,128)(2,1)S(1)}, u32[]{:S(2)}, u32[]{:S(2)}) collective-permute-start(bf16[144,1024]{1,0:T(8,128)(2,1)S(1)} %combine.2.refs_4_), channel_id=1, source_target_pairs={{0,7},{1,0},{2,1},{3,2},{4,3},{5,4},{6,5},{7,6},{8,15},{9,8},{10,9... | collective-permute-start | bytes 884744 | tf_op jit(solution)/shard_map/ppermute | solution.py:308
  28.6 16.2 %collective-permute-start.6 = (bf16[128,768]{1,0:T(8,128)(2,1)S(1)}, bf16[128,768]{1,0:T(8,128)(2,1)S(1)}, u32[]{:S(2)}, u32[]{:S(2)}) collective-permute-start(bf16[128,768]{1,0:T(8,128)(2,1)S(1)} %stage.5), channel_id=1, source_target_pairs={{0,1},{1,2},{2,3},{3,4},{4,5},{5,6},{6,7},{7,0},{8,9},{9,10},{10,1... | collective-permute-start | bytes 589832 | tf_op jit(solution)/shard_map/ppermute | solution.py:308
  30.2 5.3 %copy-start.3 = (bf16[1,128,2048]{2,1,0:T(8,128)(2,1)S(1)}, bf16[1,128,2048]{2,1,0:T(8,128)(2,1)}, u32[]{:S(2)}) copy-start(bf16[1,128,2048]{2,1,0:T(8,128)(2,1)} %param.9) | copy-start | bytes 1572868
  30.2 5.3 %copy-start.4 = (bf16[1,128,2048]{2,1,0:T(8,128)(2,1)S(1)}, bf16[1,128,2048]{2,1,0:T(8,128)(2,1)}, u32[]{:S(2)}) copy-start(bf16[1,128,2048]{2,1,0:T(8,128)(2,1)} %param.10) | copy-start | bytes 1572868
  30.6 8.7 %copy-start.2 = (bf16[1,128,2048]{2,1,0:T(8,128)(2,1)S(1)}, bf16[1,128,2048]{2,1,0:T(8,128)(2,1)}, u32[]{:S(2)}) copy-start(bf16[1,128,2048]{2,1,0:T(8,128)(2,1)} %param.8) | copy-start | bytes 1572868
  30.6 10.6 %collective-permute-start.7 = (bf16[144,640]{1,0:T(8,128)(2,1)S(1)}, bf16[144,640]{1,0:T(8,128)(2,1)S(1)}, u32[]{:S(2)}, u32[]{:S(2)}) collective-permute-start(bf16[144,640]{1,0:T(8,128)(2,1)S(1)} %get-tuple-element.28.refs_4_), channel_id=1, source_target_pairs={{0,7},{1,0},{2,1},{3,2},{4,3},{5,4},{6,5},{7,6},{8,15},{9,8},{10,9... | collective-permute-start | bytes 552968 | tf_op jit(solution)/shard_map/ppermute | solution.py:308
  35.4 14.8 %collective-permute-start.10 = (bf16[144,384]{1,0:T(8,128)(2,1)S(1)}, bf16[144,384]{1,0:T(8,128)(2,1)S(1)}, u32[]{:S(2)}, u32[]{:S(2)}) collective-permute-start(bf16[144,384]{1,0:T(8,128)(2,1)S(1)} %get-tuple-element.29.refs_5_), channel_id=1, source_target_pairs={{0,7},{1,0},{2,1},{3,2},{4,3},{5,4},{6,5},{7,6},{8,15},{9,8},{10,9... | collective-permute-start | bytes 331784 | tf_op jit(solution)/shard_map/ppermute | solution.py:308
  37.3 17.8 %collective-permute-start.8 = (bf16[128,1024]{1,0:T(8,128)(2,1)S(1)}, bf16[128,1024]{1,0:T(8,128)(2,1)S(1)}, u32[]{:S(2)}, u32[]{:S(2)}) collective-permute-start(bf16[128,1024]{1,0:T(8,128)(2,1)S(1)} %get-tuple-element.26.refs_5_), channel_id=1, source_target_pairs={{0,1},{1,2},{2,3},{3,4},{4,5},{5,6},{6,7},{7,0},{8,9},{9,10},{10,1... | collective-permute-start | bytes 786440 | tf_op jit(solution)/shard_map/ppermute | solution.py:308
  42.5 12.6 %collective-permute-start.9 = (bf16[128,640]{1,0:T(8,128)(2,1)S(1)}, bf16[128,640]{1,0:T(8,128)(2,1)S(1)}, u32[]{:S(2)}, u32[]{:S(2)}) collective-permute-start(bf16[128,640]{1,0:T(8,128)(2,1)S(1)} %get-tuple-element.31.refs_8_), channel_id=1, source_target_pairs={{0,1},{1,2},{2,3},{3,4},{4,5},{5,6},{6,7},{7,0},{8,9},{9,10},{10,1... | collective-permute-start | bytes 491528 | tf_op jit(solution)/shard_map/ppermute | solution.py:308

commit v7 on v5

--- a/solution.py
+++ b/solution.py
@@ -316,7 +316,7 @@
     at_cut = jnp.stack([jnp.zeros_like(core), core]).astype(jnp.int32)
     weights = [stage([out_proj], 0, width, pieces)]
     if pair == 2:
-        weights.append(stage([lax.ppermute(out_proj, "dp", [(i, i ^ 1) for i in range(dp)])], 0, width))
+        weights.append(stage([lax.ppermute(lax.optimization_barrier((out_proj, pieces))[0], "dp", [(i, i ^ 1) for i in range(dp)])], 0, width))
     query_sent, _ = lax.optimization_barrier((query, pieces))
     query_next = along_ctx(query_sent, -1)
 

time: 50.5 us -> 50.5 us (level)
  transfers between devices with their start and end apart: 11 -> 11, of which waited for: 4 -> 4; matrix products, arithmetic and copies ran while one was open for 2% -> 0% of each run, Pallas kernels for 37% -> 37%
where the time goes in v7:
time: 50.5 us; the launch traced here: 50.2 us
  Pallas kernels  19.3 us (38%)
  starting transfers between devices  17.5 us (35%)
  waiting for transfers between devices  11.2 us (22%)
  local copies, waits for them, and re-layouts  1.01 us (2%)
  between operations  0.86 us (2%)
    pallas_call x13, Pallas kernels, call(): pl.pallas_call(kernel, in_specs=[here_in(pltpu.SMEM)] * len(scalars) + [h...  15.5 us
    ppermute x7, starting transfers between devices, along_ctx(): return lax.ppermute(array, 'ctx', [(i, (i + by) % ctx) for i in range(ctx)])  12.3 us
    ppermute x7, waiting for transfers between devices, along_ctx(): return lax.ppermute(array, 'ctx', [(i, (i + by) % ctx) for i in range(ctx)])  10.6 us
    ppermute x3, starting transfers between devices, along_dp(): return lax.ppermute(array, 'dp', [(i, (i + by) % dp) for i in range(dp)])  4.72 us
    pallas_call x3, Pallas kernels, stage(): pl.pallas_call(kernel, in_specs=[here_in(pl.ANY)] * (n + n_after), out_sp...  3.88 us
  transfers between devices with their start and end apart: 11, of which 4 were waited for; matrix products, arithmetic and copies ran while one was open for 0% of the time, Pallas kernels for 37%

profile of v7, /device:TPU:0, one launch (start us, length us, event | category | flops | bytes accessed | tf_op | source)
XLA Modules:
  0.0 50.2 jit_solution(8478873691093890198)
XLA Ops:
  0.7 1.0 %dynamic-slice_bitcast_fusion.refs_1_ = bf16[128,1024]{1,0:T(8,128)(2,1)S(1)} fusion(bf16[1,128,2048]{2,1,0:T(8,128)(2,1)} %param.11, s32[]{:T(128)S(6)} %select_n.31), kind=kLoop, calls=%fused_computation | loop fusion | bytes 524292 | tf_op jit(solution)/shard_map/dynamic_slice | solution.py:311
  2.2 2.6 %collective-permute-start = (bf16[128,1024]{1,0:T(8,128)(2,1)S(1)}, bf16[128,1024]{1,0:T(8,128)(2,1)S(1)}, u32[]{:S(2)}, u32[]{:S(2)}) collective-permute-start(bf16[128,1024]{1,0:T(8,128)(2,1)S(1)} %dynamic-slice_bitcast_fusion.refs_1_), channel_id=1, source_target_pairs={{0,16},{8,24},{16,0},{24,8},{1,17},{9,25},{17,1},{25,9},{2,18},{10... | collective-permute-start | bytes 786440 | tf_op jit(solution)/shard_map/ppermute | solution.py:305
  4.7 4.6 %collective-permute-start.2 = (bf16[128,2048]{1,0:T(8,128)(2,1)}, bf16[128,2048]{1,0:T(8,128)(2,1)S(1)}, u32[]{:S(2)}, u32[]{:S(2)}) collective-permute-start(bf16[128,2048]{1,0:T(8,128)(2,1)} %bitcast.33), channel_id=1, source_target_pairs={{0,7},{1,0},{2,1},{3,2},{4,3},{5,4},{6,5},{7,6},{8,15},{9,8},{10,9... | collective-permute-start | bytes 1572872 | tf_op jit(solution)/shard_map/ppermute | solution.py:308
  9.4 1.5 %stage.3.refs_2_ = bf16[512,2048]{1,0:T(8,128)(2,1)S(1)} custom-call(bf16[512,2048]{1,0:T(8,128)(2,1)} %refs_0_.1, bf16[128,1024]{1,0:T(8,128)(2,1)S(1)} %dynamic-slice_bitcast_fusion.refs_1_), custom_call_target="tpu_custom_call" | custom-call | flops 1000000000 | bytes 4194304 | tf_op jit(solution)/shard_map/stage/pallas_call | solution.py:72
  11.0 1.5 %stage.4.refs_3_ = bf16[512,2048]{1,0:T(8,128)(2,1)S(1)} custom-call(bf16[512,2048]{1,0:T(8,128)(2,1)} %collective-permute-done.1.refs_0_), custom_call_target="tpu_custom_call" | custom-call | flops 1000000000 | bytes 4194304 | tf_op jit(solution)/shard_map/stage/pallas_call | solution.py:72
  12.5 1.0 %project.4.refs_4_ = bf16[128,1024]{1,0:T(8,128)(2,1)S(1)} custom-call(s32[2]{0:T(128)S(1)} %pad_add_fusion.1.refs_0_, bf16[128,1024]{1,0:T(8,128)(2,1)S(1)} %collective-permute-done.refs_1_, bf16[512,2048]{1,0:T(8,128)(2,1)S(1)} %stage.3.refs_2_, bf16[512,2048]{1,0:T(8,128)(2,1)S(1)} %stage.4.refs_3_), custom_call_target="tpu_custom_call" | custom-call | flops 1000000000 | bytes 4718592 | tf_op jit(solution)/shard_map/project/pallas_call | solution.py:39
  13.5 1.0 %collective-permute-start.3 = (bf16[128,1024]{1,0:T(8,128)(2,1)S(1)}, bf16[128,1024]{1,0:T(8,128)(2,1)S(1)}, u32[]{:S(2)}, u32[]{:S(2)}) collective-permute-start(bf16[128,1024]{1,0:T(8,128)(2,1)S(1)} %project.4.refs_4_), channel_id=1, source_target_pairs={{0,16},{8,24},{16,0},{24,8},{1,17},{9,25},{17,1},{25,9},{2,18},{10... | collective-permute-start | bytes 786440 | tf_op jit(solution)/shard_map/ppermute | solution.py:305
  14.4 1.0 %project.5.refs_2_.refs_5_ = bf16[128,1024]{1,0:T(8,128)(2,1)S(1)} custom-call(s32[2]{0:T(128)S(1)} %pad_add_fusion.1.refs_0_, bf16[128,1024]{1,0:T(8,128)(2,1)S(1)} %collective-permute-done.refs_1_, bf16[512,2048]{1,0:T(8,128)(2,1)S(1)} %stage.3.refs_2_, bf16[512,2048]{1,0:T(8,128)(2,1)S(1)} %stage.4.refs_3_, bf16[128,1024]{1,0:T(8,128)(2,1)S(1)} %project.4.refs_4_), custom_call_target="tpu_custom_call" | custom-call | flops 1000000000 | bytes 4718592 | tf_op jit(solution)/shard_map/project/pallas_call | solution.py:39
  15.5 1.2 %collective-permute-start.5 = (bf16[128,1024]{1,0:T(8,128)(2,1)S(1)}, bf16[128,1024]{1,0:T(8,128)(2,1)S(1)}, u32[]{:S(2)}, u32[]{:S(2)}) collective-permute-start(bf16[128,1024]{1,0:T(8,128)(2,1)S(1)} %project.5.refs_2_.refs_5_), channel_id=1, source_target_pairs={{0,16},{8,24},{16,0},{24,8},{1,17},{9,25},{17,1},{25,9},{2,18},{10... | collective-permute-start | bytes 786440 | tf_op jit(solution)/shard_map/ppermute | solution.py:305
  16.6 0.9 %stage.5 = bf16[128,768]{1,0:T(8,128)(2,1)S(1)} custom-call(bf16[128,2048]{1,0:T(8,128)(2,1)} %bitcast.19, bf16[128,2048]{1,0:T(8,128)(2,1)} %bitcast.25, bf16[128,1024]{1,0:T(8,128)(2,1)S(1)} %project.5.refs_2_.refs_5_), custom_call_target="tpu_custom_call" | custom-call | flops 1000000000 | bytes 393216 | tf_op jit(solution)/shard_map/stage/pallas_call | solution.py:72
  17.5 0.9 %collective-permute-start.6 = (bf16[128,768]{1,0:T(8,128)(2,1)S(1)}, bf16[128,768]{1,0:T(8,128)(2,1)S(1)}, u32[]{:S(2)}, u32[]{:S(2)}) collective-permute-start(bf16[128,768]{1,0:T(8,128)(2,1)S(1)} %stage.5), channel_id=1, source_target_pairs={{0,1},{1,2},{2,3},{3,4},{4,5},{5,6},{6,7},{7,0},{8,9},{9,10},{10,1... | collective-permute-start | bytes 589832 | tf_op jit(solution)/shard_map/ppermute | solution.py:308
  18.4 2.7 %collective-permute-done.2.refs_4_.refs_0_ = bf16[128,2048]{1,0:T(8,128)(2,1)S(1)} collective-permute-done((bf16[128,2048]{1,0:T(8,128)(2,1)}, bf16[128,2048]{1,0:T(8,128)(2,1)S(1)}, u32[]{:S(2)}, u32[]{:S(2)}) %collective-permute-start.2) | collective-permute-done | bytes 524320 | tf_op jit(solution)/shard_map/ppermute | solution.py:308
  21.1 1.0 %project.6.refs_0_ = f32[128,1024]{1,0:T(8,128)S(1)} custom-call(s32[2]{0:T(128)S(1)} %pad_add_fusion.2.refs_0_, bf16[128,2048]{1,0:T(8,128)(2,1)S(1)} %bitcast.17, bf16[512,2048]{1,0:T(8,128)(2,1)S(1)} %stage.3.refs_2_, bf16[512,2048]{1,0:T(8,128)(2,1)S(1)} %stage.4.refs_3_, bf16[128,2048]{1,0:T(8,128)(2,1)S(1)} %collective-permute-done.2.refs_4_.refs_0_, ...), custom_call_target="tpu_custom_call" | custom-call | flops 1000000000 | bytes 5242880 | tf_op jit(solution)/shard_map/project/pallas_call | solution.py:39
  23.2 4.7 %collective-permute-start.4 = (bf16[144,1024]{1,0:T(8,128)(2,1)S(1)}, bf16[144,1024]{1,0:T(8,128)(2,1)S(1)}, u32[]{:S(2)}, u32[]{:S(2)}) collective-permute-start(bf16[144,1024]{1,0:T(8,128)(2,1)S(1)} %combine.2.refs_4_), channel_id=1, source_target_pairs={{0,7},{1,0},{2,1},{3,2},{4,3},{5,4},{6,5},{7,6},{8,15},{9,8},{10,9... | collective-permute-start | bytes 884744 | tf_op jit(solution)/shard_map/ppermute | solution.py:308
  28.5 1.0 %project.7.refs_0_ = f32[128,1024]{1,0:T(8,128)S(1)} custom-call(s32[2]{0:T(128)S(1)} %pad_add_fusion.2.refs_0_, bf16[128,2048]{1,0:T(8,128)(2,1)S(1)} %bitcast.18, bf16[512,2048]{1,0:T(8,128)(2,1)S(1)} %stage.3.refs_2_, bf16[512,2048]{1,0:T(8,128)(2,1)S(1)} %stage.4.refs_3_, bf16[144,1024]{1,0:T(8,128)(2,1)S(1)} %combine.2.refs_4_, ...), custom_call_target="tpu_custom_call" | custom-call | flops 1000000000 | bytes 5242880 | tf_op jit(solution)/shard_map/project/pallas_call | solution.py:39
  29.9 1.5 %collective-permute-start.7 = (bf16[144,640]{1,0:T(8,128)(2,1)S(1)}, bf16[144,640]{1,0:T(8,128)(2,1)S(1)}, u32[]{:S(2)}, u32[]{:S(2)}) collective-permute-start(bf16[144,640]{1,0:T(8,128)(2,1)S(1)} %get-tuple-element.30.refs_4_), channel_id=1, source_target_pairs={{0,7},{1,0},{2,1},{3,2},{4,3},{5,4},{6,5},{7,6},{8,15},{9,8},{10,9... | collective-permute-start | bytes 552968 | tf_op jit(solution)/shard_map/ppermute | solution.py:308
  32.0 3.3 %collective-permute-done.4.refs_4_ = bf16[144,1024]{1,0:T(8,128)(2,1)S(1)} collective-permute-done((bf16[144,1024]{1,0:T(8,128)(2,1)S(1)}, bf16[144,1024]{1,0:T(8,128)(2,1)S(1)}, u32[]{:S(2)}, u32[]{:S(2)}) %collective-permute-start.4) | collective-permute-done | bytes 294944 | tf_op jit(solution)/shard_map/ppermute | solution.py:308
  35.3 1.8 %cross_pair.2 = (bf16[128,1024]{1,0:T(8,128)(2,1)S(1)}, bf16[128,1024]{1,0:T(8,128)(2,1)S(1)}, bf16[128,1024]{1,0:T(8,128)(2,1)S(1)}) custom-call(bf16[128,2048]{1,0:T(8,128)(2,1)S(1)} %collective-permute-done.2.refs_4_.refs_0_, bf16[128,2048]{1,0:T(8,128)(2,1)S(1)} %bitcast.20, bf16[128,2048]{1,0:T(8,128)(2,1)S(1)} %bitcast.26, ...), custom_call_target="tpu_custom_call" | custom-call | flops 1000000000 | bytes 2719744 | tf_op jit(solution)/shard_map/cross_pair/pallas_call | solution.py:39
  37.2 1.8 %own_pair.2 = (f32[128,1024]{1,0:T(8,128)S(1)}, f32[128,1024]{1,0:T(8,128)S(1)}, f32[128,1024]{1,0:T(8,128)S(1)}) custom-call(bf16[128,2048]{1,0:T(8,128)(2,1)S(1)} %bitcast.34, bf16[128,2048]{1,0:T(8,128)(2,1)S(1)} %bitcast.21, bf16[128,2048]{1,0:T(8,128)(2,1)S(1)} %bitcast.27, f32[128,128]{1,0:T(8,128)S(1)} %get-tuple-element.25.refs_3_, ...), custom_call_target="tpu_custom_call" | custom-call | flops 1000000000 | bytes 3506176 | tf_op jit(solution)/shard_map/own_pair/pallas_call | solution.py:39
  39.0 1.2 %cross_pair.3 = (bf16[128,640]{1,0:T(8,128)(2,1)S(1)}, bf16[128,640]{1,0:T(8,128)(2,1)S(1)}, bf16[128,640]{1,0:T(8,128)(2,1)S(1)}) custom-call(bf16[128,2048]{1,0:T(8,128)(2,1)S(1)} %collective-permute-done.2.refs_4_.refs_0_, bf16[128,2048]{1,0:T(8,128)(2,1)S(1)} %bitcast.22, bf16[128,2048]{1,0:T(8,128)(2,1)S(1)} %bitcast.28, ...), custom_call_target="tpu_custom_call" | custom-call | flops 1000000000 | bytes 2314240 | tf_op jit(solution)/shard_map/cross_pair/pallas_call | solution.py:39
  40.3 2.4 %own_pair.3 = (f32[128,1024]{1,0:T(8,128)S(1)}, f32[128,1024]{1,0:T(8,128)S(1)}, f32[128,1024]{1,0:T(8,128)S(1)}) custom-call(bf16[128,2048]{1,0:T(8,128)(2,1)S(1)} %bitcast.35, bf16[128,2048]{1,0:T(8,128)(2,1)S(1)} %bitcast.23, bf16[128,2048]{1,0:T(8,128)(2,1)S(1)} %bitcast.29, f32[128,128]{1,0:T(8,128)S(1)} %get-tuple-element.25.refs_3_, ...), custom_call_target="tpu_custom_call" | custom-call | flops 1000000000 | bytes 3768320 | tf_op jit(solution)/shard_map/own_pair/pallas_call | solution.py:39
  42.7 2.0 %key_grads.1 = (bf16[128,2048]{1,0:T(8,128)(2,1)}, bf16[128,2048]{1,0:T(8,128)(2,1)}) custom-call(bf16[128,2048]{1,0:T(8,128)(2,1)S(1)} %collective-permute-done.2.refs_4_.refs_0_, bf16[128,2048]{1,0:T(8,128)(2,1)S(1)} %bitcast.24, bf16[128,2048]{1,0:T(8,128)(2,1)S(1)} %bitcast.30, f32[128,128]{1,0:T(8,128)S(1)} %get-tuple-element.27.refs_3_, ...), custom_call_target="tpu_custom_call" | custom-call | flops 1000000000 | bytes 6225920 | tf_op jit(solution)/shard_map/key_grads/pallas_call | solution.py:39
  44.7 4.7 %collective-permute-done.9.refs_3_ = bf16[128,640]{1,0:T(8,128)(2,1)S(1)} collective-permute-done((bf16[128,640]{1,0:T(8,128)(2,1)S(1)}, bf16[128,640]{1,0:T(8,128)(2,1)S(1)}, u32[]{:S(2)}, u32[]{:S(2)}) %collective-permute-start.9) | collective-permute-done | bytes 163872 | tf_op jit(solution)/shard_map/ppermute | solution.py:308
  49.3 0.9 %query_grads.1 = bf16[128,2048]{1,0:T(8,128)(2,1)} custom-call(f32[128,1024]{1,0:T(8,128)S(1)} %get-tuple-element.29.refs_6_.refs_0_, f32[128,1024]{1,0:T(8,128)S(1)} %get-tuple-element.34.refs_1_, bf16[128,1024]{1,0:T(8,128)(2,1)S(1)} %collective-permute-done.8.refs_2_, bf16[128,640]{1,0:T(8,128)(2,1)S(1)} %collective-permute-done.9.refs_3_), custom_call_target="tpu_custom_call" | custom-call | flops 1000000000 | bytes 1998848 | tf_op jit(solution)/shard_map/query_grads/pallas_call | solution.py:39
  (32 shorter events, 3.4 us)
Async XLA Ops:
  1.6 9.3 %collective-permute-start.1 = (bf16[512,2048]{1,0:T(8,128)(2,1)}, bf16[512,2048]{1,0:T(8,128)(2,1)}, u32[]{:S(2)}, u32[]{:S(2)}) collective-permute-start(bf16[512,2048]{1,0:T(8,128)(2,1)} %refs_0_.1), channel_id=1, source_target_pairs={{0,8},{8,0},{16,24},{24,16},{1,9},{9,1},{17,25},{25,17},{2,10},{10... | collective-permute-start | bytes 6291464 | tf_op jit(solution)/shard_map/ppermute | solution.py:319
  2.2 10.3 %collective-permute-start = (bf16[128,1024]{1,0:T(8,128)(2,1)S(1)}, bf16[128,1024]{1,0:T(8,128)(2,1)S(1)}, u32[]{:S(2)}, u32[]{:S(2)}) collective-permute-start(bf16[128,1024]{1,0:T(8,128)(2,1)S(1)} %dynamic-slice_bitcast_fusion.refs_1_), channel_id=1, source_target_pairs={{0,16},{8,24},{16,0},{24,8},{1,17},{9,25},{17,1},{25,9},{2,18},{10... | collective-permute-start | bytes 786440 | tf_op jit(solution)/shard_map/ppermute | solution.py:305
  4.7 16.4 %collective-permute-start.2 = (bf16[128,2048]{1,0:T(8,128)(2,1)}, bf16[128,2048]{1,0:T(8,128)(2,1)S(1)}, u32[]{:S(2)}, u32[]{:S(2)}) collective-permute-start(bf16[128,2048]{1,0:T(8,128)(2,1)} %bitcast.33), channel_id=1, source_target_pairs={{0,7},{1,0},{2,1},{3,2},{4,3},{5,4},{6,5},{7,6},{8,15},{9,8},{10,9... | collective-permute-start | bytes 1572872 | tf_op jit(solution)/shard_map/ppermute | solution.py:308
  13.5 9.3 %collective-permute-start.3 = (bf16[128,1024]{1,0:T(8,128)(2,1)S(1)}, bf16[128,1024]{1,0:T(8,128)(2,1)S(1)}, u32[]{:S(2)}, u32[]{:S(2)}) collective-permute-start(bf16[128,1024]{1,0:T(8,128)(2,1)S(1)} %project.4.refs_4_), channel_id=1, source_target_pairs={{0,16},{8,24},{16,0},{24,8},{1,17},{9,25},{17,1},{25,9},{2,18},{10... | collective-permute-start | bytes 786440 | tf_op jit(solution)/shard_map/ppermute | solution.py:305
  15.4 5.7 %copy-start = (bf16[1,128,2048]{2,1,0:T(8,128)(2,1)S(1)}, bf16[1,128,2048]{2,1,0:T(8,128)(2,1)}, u32[]{:S(2)}) copy-start(bf16[1,128,2048]{2,1,0:T(8,128)(2,1)} %param.11) | copy-start | bytes 1572868
  15.5 14.1 %collective-permute-start.5 = (bf16[128,1024]{1,0:T(8,128)(2,1)S(1)}, bf16[128,1024]{1,0:T(8,128)(2,1)S(1)}, u32[]{:S(2)}, u32[]{:S(2)}) collective-permute-start(bf16[128,1024]{1,0:T(8,128)(2,1)S(1)} %project.5.refs_2_.refs_5_), channel_id=1, source_target_pairs={{0,16},{8,24},{16,0},{24,8},{1,17},{9,25},{17,1},{25,9},{2,18},{10... | collective-permute-start | bytes 786440 | tf_op jit(solution)/shard_map/ppermute | solution.py:305
  17.5 12.0 %collective-permute-start.6 = (bf16[128,768]{1,0:T(8,128)(2,1)S(1)}, bf16[128,768]{1,0:T(8,128)(2,1)S(1)}, u32[]{:S(2)}, u32[]{:S(2)}) collective-permute-start(bf16[128,768]{1,0:T(8,128)(2,1)S(1)} %stage.5), channel_id=1, source_target_pairs={{0,1},{1,2},{2,3},{3,4},{4,5},{5,6},{6,7},{7,0},{8,9},{9,10},{10,1... | collective-permute-start | bytes 589832 | tf_op jit(solution)/shard_map/ppermute | solution.py:308
  21.1 1.6 %copy-start.3 = (bf16[1,128,2048]{2,1,0:T(8,128)(2,1)S(1)}, bf16[1,128,2048]{2,1,0:T(8,128)(2,1)}, u32[]{:S(2)}) copy-start(bf16[1,128,2048]{2,1,0:T(8,128)(2,1)} %param.13) | copy-start | bytes 1572868
  21.1 1.6 %copy-start.5 = (f32[1,16,128]{2,1,0:T(8,128)S(1)}, f32[1,16,128]{2,1,0:T(8,128)}, u32[]{:S(2)}) copy-start(f32[1,16,128]{2,1,0:T(8,128)} %param.14) | copy-start | bytes 24580
  22.1 5.8 %copy-start.6 = (s32[1,32]{1,0:T(1,128)S(1)}, s32[1,32]{1,0:T(1,128)}, u32[]{:S(2)}) copy-start(s32[1,32]{1,0:T(1,128)} %param.15) | copy-start | bytes 388
  23.2 12.1 %collective-permute-start.4 = (bf16[144,1024]{1,0:T(8,128)(2,1)S(1)}, bf16[144,1024]{1,0:T(8,128)(2,1)S(1)}, u32[]{:S(2)}, u32[]{:S(2)}) collective-permute-start(bf16[144,1024]{1,0:T(8,128)(2,1)S(1)} %combine.2.refs_4_), channel_id=1, source_target_pairs={{0,7},{1,0},{2,1},{3,2},{4,3},{5,4},{6,5},{7,6},{8,15},{9,8},{10,9... | collective-permute-start | bytes 884744 | tf_op jit(solution)/shard_map/ppermute | solution.py:308
  29.5 5.8 %copy-start.1 = (bf16[1,128,2048]{2,1,0:T(8,128)(2,1)S(1)}, bf16[1,128,2048]{2,1,0:T(8,128)(2,1)}, u32[]{:S(2)}) copy-start(bf16[1,128,2048]{2,1,0:T(8,128)(2,1)} %param.9) | copy-start | bytes 1572868
  29.5 5.8 %copy-start.2 = (bf16[1,128,2048]{2,1,0:T(8,128)(2,1)S(1)}, bf16[1,128,2048]{2,1,0:T(8,128)(2,1)}, u32[]{:S(2)}) copy-start(bf16[1,128,2048]{2,1,0:T(8,128)(2,1)} %param.10) | copy-start | bytes 1572868
  29.9 7.2 %copy-start.4 = (bf16[1,128,2048]{2,1,0:T(8,128)(2,1)S(1)}, bf16[1,128,2048]{2,1,0:T(8,128)(2,1)}, u32[]{:S(2)}) copy-start(bf16[1,128,2048]{2,1,0:T(8,128)(2,1)} %param.8) | copy-start | bytes 1572868
  29.9 9.1 %collective-permute-start.7 = (bf16[144,640]{1,0:T(8,128)(2,1)S(1)}, bf16[144,640]{1,0:T(8,128)(2,1)S(1)}, u32[]{:S(2)}, u32[]{:S(2)}) collective-permute-start(bf16[144,640]{1,0:T(8,128)(2,1)S(1)} %get-tuple-element.30.refs_4_), channel_id=1, source_target_pairs={{0,7},{1,0},{2,1},{3,2},{4,3},{5,4},{6,5},{7,6},{8,15},{9,8},{10,9... | collective-permute-start | bytes 552968 | tf_op jit(solution)/shard_map/ppermute | solution.py:308
  31.5 11.2 %collective-permute-start.10 = (bf16[144,384]{1,0:T(8,128)(2,1)S(1)}, bf16[144,384]{1,0:T(8,128)(2,1)S(1)}, u32[]{:S(2)}, u32[]{:S(2)}) collective-permute-start(bf16[144,384]{1,0:T(8,128)(2,1)S(1)} %get-tuple-element.31.refs_5_), channel_id=1, source_target_pairs={{0,7},{1,0},{2,1},{3,2},{4,3},{5,4},{6,5},{7,6},{8,15},{9,8},{10,9... | collective-permute-start | bytes 331784 | tf_op jit(solution)/shard_map/ppermute | solution.py:308
  37.1 12.2 %collective-permute-start.8 = (bf16[128,1024]{1,0:T(8,128)(2,1)S(1)}, bf16[128,1024]{1,0:T(8,128)(2,1)S(1)}, u32[]{:S(2)}, u32[]{:S(2)}) collective-permute-start(bf16[128,1024]{1,0:T(8,128)(2,1)S(1)} %get-tuple-element.28.refs_5_), channel_id=1, source_target_pairs={{0,1},{1,2},{2,3},{3,4},{4,5},{5,6},{6,7},{7,0},{8,9},{9,10},{10,1... | collective-permute-start | bytes 786440 | tf_op jit(solution)/shard_map/ppermute | solution.py:308
  40.3 9.1 %collective-permute-start.9 = (bf16[128,640]{1,0:T(8,128)(2,1)S(1)}, bf16[128,640]{1,0:T(8,128)(2,1)S(1)}, u32[]{:S(2)}, u32[]{:S(2)}) collective-permute-start(bf16[128,640]{1,0:T(8,128)(2,1)S(1)} %get-tuple-element.33.refs_8_), channel_id=1, source_target_pairs={{0,1},{1,2},{2,3},{3,4},{4,5},{5,6},{6,7},{7,0},{8,9},{9,10},{10,1... | collective-permute-start | bytes 491528 | tf_op jit(solution)/shard_map/ppermute | solution.py:308
